TPU v7x, 32 devices: a whole 2x2x4 slice. The times are simulated.
32 devices in a mesh: op: 4 (over y, core), sec: 8 (over z, x).
Axes of the slice: x: 2, y: 2, z: 4, core: 2. Of those that a mesh axis runs over, the one named last changes fastest.
Arguments:
- psi_first: bfloat16 [32, 256, 256], P('sec'), may hold values from -6 to 6
- psi_second: bfloat16 [32, 256, 256], P('sec'), may hold values from -6 to 6
- left_ops: bfloat16 [1024, 256, 256], P(('op', 'sec')), may hold values from -0.375 to 0.375
- right_ops: bfloat16 [1024, 256, 256], P(('op', 'sec')), may hold values from -0.0625 to 0.0625
- source_local: int32 [1024], P(('op', 'sec')), may hold values from 0 to 3
- target_sector: int32 [1024], P(('op', 'sec')), may hold values from 0 to 31, as said below
Outputs:
- sigma_first: bfloat16 [32, 256, 256], P('sec')
- sigma_second: bfloat16 [32, 256, 256], P('sec')
Inputs may be any that keep to these rules, and one draw needn't show every extreme that they name: The 32 terms of one block of the terms name exactly 4 distinct target sectors, no two of them owned by the same index of sec (the same target_sector // 4).
All inputs are finite; a program needn't handle non-finite values.
Results may differ from a plain program's by a relative error of at most 0.0065.
Values may be sent and summed in bfloat16 or wider, within the bound.
No kernel may reach another device: no remote copies, remote signals or barrier semaphores. Data moves between devices by JAX's collectives and lax.ppermute only.
A program may use at most 128 MiB of HBM per device.

v0:
```python
import jax
import jax.numpy as jnp
from jax import lax
from jax.sharding import PartitionSpec as P


def per_device(psi_first, psi_second, left_ops, right_ops, source_local, target_sector):
    sec_count = lax.axis_size("sec")
    sector_count = psi_first.shape[0]
    holder = target_sector // sector_count
    within = target_sector % sector_count
    placed = jnp.arange(sec_count, dtype=jnp.int32)[:, None] == holder[None, :]
    labels = jnp.max(jnp.where(placed, within[None, :], -1), axis=1)
    placer = placed.astype(jnp.bfloat16)

    def contract(wavefunction):
        source_blocks = jnp.take(wavefunction, source_local, axis=0)
        halfway = jnp.einsum(
            "tij,tjk->tik", left_ops, source_blocks, preferred_element_type=jnp.float32
        ).astype(jnp.bfloat16)
        contracted = jnp.einsum(
            "tik,tlk->til", halfway, right_ops, preferred_element_type=jnp.float32
        ).astype(jnp.bfloat16)
        return jnp.einsum(
            "st,tij->sij", placer, contracted, preferred_element_type=jnp.float32
        ).astype(jnp.bfloat16)

    def collect(arrived, labels_in):
        selector = (
            jnp.arange(sector_count, dtype=jnp.int32)[:, None] == labels_in[None, :]
        ).astype(jnp.bfloat16)
        return jnp.einsum("ks,sij->kij", selector, arrived, preferred_element_type=jnp.float32)

    arrived, arrived_second, labels_in = (
        lax.all_to_all(contract(psi_first), "sec", split_axis=0, concat_axis=0, tiled=True),
        lax.all_to_all(contract(psi_second), "sec", split_axis=0, concat_axis=0, tiled=True),
        lax.all_to_all(labels, "sec", split_axis=0, concat_axis=0, tiled=True),
    )
    summed = lax.psum((collect(arrived, labels_in), collect(arrived_second, labels_in)), "op")
    result_first, result_second = tuple((x.astype(jnp.bfloat16) for x in summed))
    return (result_first, result_second)


def solution(mesh):
    in_specs = (
        P("sec", None, None),
        P("sec", None, None),
        P(("op", "sec"), None, None),
        P(("op", "sec"), None, None),
        P(("op", "sec")),
        P(("op", "sec")),
    )
    out_specs = (P("sec", None, None), P("sec", None, None))
    return jax.shard_map(
        per_device, mesh=mesh, in_specs=in_specs, out_specs=out_specs, check_vma=False
    )
```

profile of v0, /device:TPU:0, one launch (start us, length us, event | category | flops | bytes accessed | tf_op | source)
XLA Modules:
  0.0 133.9 jit_solution(11115435207484736659)
XLA Ops:
  0.6 0.7 and_select_fusion
  1.4 0.1 select_reduce_fusion
  1.5 0.7 copy.15
  2.2 7.3 %all-to-all-start = ((s32[8,1,1]{2,1,0:T(1,128)}), s32[8,1,1]{2,1,0:T(1,128)S(1)}, u32[]{:S(2)}, u32[]{:S(2)}) async-start(s32[8,1,1]{2,1,0:T(1,128)} %copy.15), calls=%async_computation | async-start | bytes 8192 | tf_op jit(solution)/shard_map/all_to_all | solution.py:37
  9.4 0.7 compare_and_fusion
  10.1 0.7 compare_select_fusion
  10.7 2.7 %gather_fusion.1 = bf16[32,256,256]{2,1,0:T(8,128)(2,1)} fusion(bf16[4,256,256]{2,1,0:T(8,128)(2,1)S(1)} %copy-done, s32[1024]{0:T(1024)S(1)} %pad_clamp_fusion), kind=kCustom, calls=%fused_computation.1.clone | custom fusion | bytes 8388736 | tf_op jit(solution)/shard_map/jit(_take)/gather | solution.py:17
  13.5 10.5 %fusion.27 = bf16[32,256,256]{2,1,0:T(8,128)(2,1)} fusion(bf16[32,256,256]{2,1,0:T(8,128)(2,1)} %param.11, bf16[32,256,256]{2,1,0:T(8,128)(2,1)} %param.10, bf16[32,256,256]{2,1,0:T(8,128)(2,1)} %gather_fusion.1, pred[32]{0:T(512)(128)(4,1)S(1)} %compare_and_fusion), kind=kOutput, calls=%fused_computation.17 | convolution fusion | flops 2153775104 | bytes 16777248 | tf_op jit(solution)/shard_map/tik,tlk->til/dot_general | solution.py:21
  24.0 4.6 %fusion.39 = bf16[8,256,256]{2,0,1:T(8,128)(2,1)S(1)} fusion(bf16[32,256,256]{2,1,0:T(8,128)(2,1)} %fusion.27, s32[32]{0:T(128)S(1)} %get-tuple-element.12), kind=kOutput, calls=%fused_computation.21 | convolution fusion | flops 34078976 | bytes 5243008 | tf_op jit(solution)/shard_map/st,tij->sij/dot_general | solution.py:24
  28.6 1.3 copy.24
  29.9 6.0 %all-to-all-start.2 = ((bf16[8,256,256]{2,1,0:T(8,128)(2,1)}), bf16[8,256,256]{2,1,0:T(8,128)(2,1)S(1)}, u32[]{:S(2)}, u32[]{:S(2)}) async-start(bf16[8,256,256]{2,1,0:T(8,128)(2,1)} %copy.24), calls=%async_computation.2 | async-start | bytes 2097152 | tf_op jit(solution)/shard_map/all_to_all | solution.py:36
  35.9 2.7 %gather_fusion = bf16[32,256,256]{2,1,0:T(8,128)(2,1)} fusion(bf16[4,256,256]{2,1,0:T(8,128)(2,1)S(1)} %copy-done.1, s32[1024]{0:T(1024)S(1)} %pad_clamp_fusion), kind=kCustom, calls=%fused_computation.clone | custom fusion | bytes 8388736 | tf_op jit(solution)/shard_map/jit(_take)/gather | solution.py:17
  38.6 10.5 %fusion.22 = bf16[32,256,256]{2,1,0:T(8,128)(2,1)} fusion(bf16[32,256,256]{2,1,0:T(8,128)(2,1)} %param.11, bf16[32,256,256]{2,1,0:T(8,128)(2,1)} %param.10, bf16[32,256,256]{2,1,0:T(8,128)(2,1)} %gather_fusion, pred[32]{0:T(512)(128)(4,1)S(1)} %compare_and_fusion), kind=kOutput, calls=%fused_computation.16 | convolution fusion | flops 2153775104 | bytes 16777248 | tf_op jit(solution)/shard_map/tik,tlk->til/dot_general | solution.py:21
  49.1 4.5 %fusion.36 = bf16[8,256,256]{2,0,1:T(8,128)(2,1)S(1)} fusion(bf16[32,256,256]{2,1,0:T(8,128)(2,1)} %fusion.22, s32[32]{0:T(128)S(1)} %get-tuple-element.12), kind=kOutput, calls=%fused_computation.20 | convolution fusion | flops 34078976 | bytes 5243008 | tf_op jit(solution)/shard_map/st,tij->sij/dot_general | solution.py:24
  53.6 1.2 copy.19
  54.8 6.5 %all-to-all-done.2 = bf16[8,256,256]{2,1,0:T(8,128)(2,1)S(1)} async-done(((bf16[8,256,256]{2,1,0:T(8,128)(2,1)}), bf16[8,256,256]{2,1,0:T(8,128)(2,1)S(1)}, u32[]{:S(2)}, u32[]{:S(2)}) %all-to-all-start.2) | async-done | bytes 1048608 | tf_op jit(solution)/shard_map/all_to_all | solution.py:36
  61.3 3.6 %all-to-all-start.1 = ((bf16[8,256,256]{2,1,0:T(8,128)(2,1)}), bf16[8,256,256]{2,1,0:T(8,128)(2,1)S(1)}, u32[]{:S(2)}, u32[]{:S(2)}) async-start(bf16[8,256,256]{2,1,0:T(8,128)(2,1)} %copy.19), calls=%async_computation.1 | async-start | bytes 2097152 | tf_op jit(solution)/shard_map/all_to_all | solution.py:35
  64.8 0.2 reduce
  65.1 1.8 %fusion.42 = f32[4,256,256]{2,0,1:T(4,128)} fusion(bf16[8,256,256]{2,1,0:T(8,128)(2,1)S(1)} %all-to-all-done.2, s32[8]{0:T(128)S(1)} %reduce), kind=kOutput, calls=%fused_computation.22 | convolution fusion | flops 4194336 | bytes 2097184 | tf_op jit(solution)/shard_map/ks,sij->kij/dot_general | solution.py:32
  66.9 23.7 %all-to-all-done.1 = bf16[8,256,256]{2,1,0:T(8,128)(2,1)S(1)} async-done(((bf16[8,256,256]{2,1,0:T(8,128)(2,1)}), bf16[8,256,256]{2,1,0:T(8,128)(2,1)S(1)}, u32[]{:S(2)}, u32[]{:S(2)}) %all-to-all-start.1) | async-done | bytes 1048608 | tf_op jit(solution)/shard_map/all_to_all | solution.py:35
  90.6 0.7 fusion.44
  91.3 40.8 %all-reduce.2 = (bf16[4,256,256]{2,0,1:T(4,128)(2,1)S(1)}, bf16[4,256,256]{2,0,1:T(4,128)(2,1)S(1)}) all-reduce(f32[4,256,256]{2,0,1:T(4,128)S(1)} %fusion.44, f32[4,256,256]{2,0,1:T(4,128)} %fusion.42), channel_id=1, replica_groups=mesh['op'=4,'sec'=8] {'op'}, use_global_device_ids=true, to_apply=%region_1.3 | all-reduce | flops 524288 | bytes 3145728 | tf_op jit(solution)/shard_map/psum | solution.py:39
  132.1 0.9 copy.26
  133.0 0.9 copy.27
  (6 shorter events, 0.0 us)
Async XLA Ops:
  0.6 10.1 %copy-start = (bf16[4,256,256]{2,1,0:T(8,128)(2,1)S(1)}, bf16[4,256,256]{2,1,0:T(8,128)(2,1)}, u32[]{:S(2)}) copy-start(bf16[4,256,256]{2,1,0:T(8,128)(2,1)} %param.9) | copy-start | bytes 1572868
  2.2 27.7 %all-to-all-start = ((s32[8,1,1]{2,1,0:T(1,128)}), s32[8,1,1]{2,1,0:T(1,128)S(1)}, u32[]{:S(2)}, u32[]{:S(2)}) async-start(s32[8,1,1]{2,1,0:T(1,128)} %copy.15), calls=%async_computation | async-start | bytes 8192 | tf_op jit(solution)/shard_map/all_to_all | solution.py:37
  24.0 11.9 %copy-start.1 = (bf16[4,256,256]{2,1,0:T(8,128)(2,1)S(1)}, bf16[4,256,256]{2,1,0:T(8,128)(2,1)}, u32[]{:S(2)}) copy-start(bf16[4,256,256]{2,1,0:T(8,128)(2,1)} %param.8) | copy-start | bytes 1572868
  29.9 31.4 %all-to-all-start.2 = ((bf16[8,256,256]{2,1,0:T(8,128)(2,1)}), bf16[8,256,256]{2,1,0:T(8,128)(2,1)S(1)}, u32[]{:S(2)}, u32[]{:S(2)}) async-start(bf16[8,256,256]{2,1,0:T(8,128)(2,1)} %copy.24), calls=%async_computation.2 | async-start | bytes 2097152 | tf_op jit(solution)/shard_map/all_to_all | solution.py:36
  61.3 29.3 %all-to-all-start.1 = ((bf16[8,256,256]{2,1,0:T(8,128)(2,1)}), bf16[8,256,256]{2,1,0:T(8,128)(2,1)S(1)}, u32[]{:S(2)}, u32[]{:S(2)}) async-start(bf16[8,256,256]{2,1,0:T(8,128)(2,1)} %copy.19), calls=%async_computation.1 | async-start | bytes 2097152 | tf_op jit(solution)/shard_map/all_to_all | solution.py:35
where the time goes:
time: 134 us
  blocking collectives  40.8 us (30%)
  matrix products  32.6 us (24%)
  waiting for transfers between devices  30.2 us (23%)
  starting transfers between devices  16.8 us (13%)
  local copies, waits for them, and re-layouts  10.4 us (8%)
  other arithmetic  2.4 us (2%)
    psum x1, blocking collectives, per_device(): lax.psum((collect(arrived, labels_in), collect(arrived_second, labels_in)...  40.8 us
    all_to_all x1, waiting for transfers between devices, per_device(): lax.all_to_all(contract(psi_first), 'sec', split_axis=0, concat_axis=0, t...  23.7 us
    dot_general x2, matrix products, contract(): jnp.einsum('tik,tlk->til', halfway, right_ops, preferred_element_type=jnp...  21 us
    dot_general x2, matrix products, contract(): jnp.einsum('st,tij->sij', placer, contracted, preferred_element_type=jnp....  9.14 us
    all_to_all x1, starting transfers between devices, per_device(): lax.all_to_all(labels, 'sec', split_axis=0, concat_axis=0, tiled=True)  7.25 us
    all_to_all x1, waiting for transfers between devices, per_device(): lax.all_to_all(contract(psi_second), 'sec', split_axis=0, concat_axis=0,...  6.45 us
    all_to_all x1, starting transfers between devices, per_device(): lax.all_to_all(contract(psi_second), 'sec', split_axis=0, concat_axis=0,...  6 us
    gather x2, local copies, waits for them, and re-layouts, contract(): source_blocks = jnp.take(wavefunction, source_local, axis=0)  5.5 us
  transfers between devices with their start and end apart: 3, of which 2 were waited for; matrix products, arithmetic and copies ran while one was open for 31% of the time, Pallas kernels for 0%

commit v1 on v0

v1 whole, which is shorter than its diff:
```python
import functools

import jax
import jax.numpy as jnp
from jax import lax
from jax.experimental import pallas as pl
from jax.experimental.pallas import tpu as pltpu
from jax.sharding import PartitionSpec as P

VMEM_LIMIT = 48 * 1024 * 1024
LABEL_ROWS = 16
AXES = ("op", "sec")


class Plan:
    def __init__(self, mesh, psi, terms):
        self.op, self.sec = mesh.shape["op"], mesh.shape["sec"]
        self.held, self.blk = psi.shape[0], psi.shape[1]
        self.terms = terms
        self.slots = self.sec // 2
        self.extra = 0
        while self.slots * self.op * 2**self.extra < self.held * self.sec:
            self.extra += 1
        self.places = (self.op // 2) * 2**self.extra
        self.rows = self.blk // self.places
        self.bits = list(range(self.extra, self.sec.bit_length() - 1))

    def place(self, op, sec):
        return (op // 2) * 2**self.extra + sec % 2**self.extra

    def swap(self, op_mask, sec_mask):
        n = self.op * self.sec
        mask = op_mask * self.sec + sec_mask
        return [(i, i ^ mask) for i in range(n)]

    def across(self, m):
        return self.swap((m >> self.extra) << 1, m & (2**self.extra - 1))


def contract_kernel(plan, step, src, tgt, left, right, first, second, *rest):
    outs = rest[: plan.places]
    acc, slot_of, labels, seen = rest[plan.places :]
    at = pl.program_id(0)

    @pl.when(at == 0)
    def _():
        for h in range(plan.sec):
            seen[h] = -1

        def name(t, count):
            target = tgt[t]
            holder = target // plan.held
            fresh = seen[holder] < 0
            slot = jnp.where(fresh, count, seen[holder])
            seen[holder] = slot
            labels[slot] = target
            slot_of[t] = slot
            return count + fresh.astype(jnp.int32)

        lax.fori_loop(0, plan.terms, name, jnp.int32(0))
        acc[...] = jnp.zeros_like(acc)

    for i in range(step):
        t = at * step + i
        a = src[t]
        half = [
            jnp.dot(left[i], psi[a], preferred_element_type=jnp.float32).astype(jnp.bfloat16)
            for psi in (first, second)
        ]
        both = jnp.concatenate(half, axis=0)
        acc[slot_of[t]] += lax.dot_general(
            both, right[i], (((1,), (1,)), ((), ())), preferred_element_type=jnp.float32
        )

    @pl.when(at == pl.num_programs(0) - 1)
    def _():
        op, sec = lax.axis_index("op"), lax.axis_index("sec")
        core, place = op % 2, plan.place(op, sec)
        lane = lax.broadcasted_iota(jnp.int32, (LABEL_ROWS, plan.blk), 1)
        tile = jnp.zeros((LABEL_ROWS, plan.blk), jnp.float32)
        for j in range(plan.slots):
            tile = jnp.where(lane == j, labels[j].astype(jnp.float32), tile)
        tile = tile.astype(jnp.bfloat16)
        for m in range(plan.places):
            row = (place ^ m) * plan.rows
            for v in range(2):
                base = pl.multiple_of((core ^ v) * plan.blk + row, plan.rows)
                for j in range(plan.slots):
                    outs[m][pl.ds((v * plan.slots + j) * plan.rows, plan.rows), :] = acc[
                        j, pl.ds(base, plan.rows), :
                    ].astype(jnp.bfloat16)
            outs[m][pl.ds(2 * plan.slots * plan.rows, LABEL_ROWS), :] = tile


def contract(plan, source, target, left, right, first, second):
    step = 4
    blk = plan.blk
    height = 2 * plan.slots * plan.rows + LABEL_ROWS
    whole = pl.BlockSpec((plan.held, blk, blk), lambda t, *_: (0, 0, 0))
    part = pl.BlockSpec((step, blk, blk), lambda t, *_: (t, 0, 0))
    return pl.pallas_call(
        functools.partial(contract_kernel, plan, step),
        grid_spec=pltpu.PrefetchScalarGridSpec(
            num_scalar_prefetch=2,
            grid=(plan.terms // step,),
            in_specs=[part, part, whole, whole],
            out_specs=[pl.BlockSpec((height, blk), lambda t, *_: (0, 0))] * plan.places,
            scratch_shapes=[
                pltpu.VMEM((plan.slots, 2 * blk, blk), jnp.float32),
                pltpu.SMEM((plan.terms,), jnp.int32),
                pltpu.SMEM((plan.slots,), jnp.int32),
                pltpu.SMEM((plan.sec,), jnp.int32),
            ],
        ),
        out_shape=[jax.ShapeDtypeStruct((height, blk), jnp.bfloat16)] * plan.places,
        compiler_params=pltpu.CompilerParams(
            vmem_limit_bytes=VMEM_LIMIT, dimension_semantics=("arbitrary",)
        ),
        name="contract",
    )(source, target, left, right, first, second)


def spread_kernel(plan, want, *refs):
    n = 2 * plan.places
    blocks, tags, out = refs[:n], refs[n : 2 * n], refs[2 * n]
    acc, tags_vector, tags_scalar, sem = refs[2 * n + 1 :]
    for i in range(n):
        row = jnp.max(tags[i][...].astype(jnp.float32), axis=0, keepdims=True)
        tags_vector[pl.ds(i, 1), :] = row[:, :128].astype(jnp.int32)
    copy = pltpu.make_async_copy(tags_vector, tags_scalar, sem)
    copy.start()
    acc[...] = jnp.zeros_like(acc)
    copy.wait()
    sec = lax.axis_index("sec")
    for i in range(n):
        for j in range(plan.slots):
            label = tags_scalar[i, j]
            away = (label // plan.held) ^ sec
            index = jnp.int32(0)
            for b in plan.bits[1:]:
                index = index * 2 + ((away >> b) & 1)
            index = index * 2**plan.extra + (away & (2**plan.extra - 1))
            index = index * plan.held + label % plan.held

            @pl.when(((away >> plan.bits[0]) & 1) == want)
            def _():
                acc[index] += blocks[i][pl.ds(j * plan.rows, plan.rows), :].astype(jnp.float32)

    out[...] = acc[...].astype(jnp.bfloat16).reshape(out.shape)


def spread(plan, want, own, other):
    blk, rows, slots = plan.blk, plan.rows, plan.slots
    sectors = plan.held * 2 ** (plan.extra + len(plan.bits) - 1)
    n = 2 * plan.places

    def half(v):
        return pl.BlockSpec((slots * rows, blk), lambda t: (v, 0))

    tag = pl.BlockSpec((LABEL_ROWS, blk), lambda t: (2 * slots * rows // LABEL_ROWS, 0))
    return pl.pallas_call(
        functools.partial(spread_kernel, plan, want),
        grid=(1,),
        in_specs=[half(0)] * plan.places + [half(1)] * plan.places + [tag] * n,
        out_specs=pl.BlockSpec((sectors * rows, blk), lambda t: (0, 0)),
        out_shape=jax.ShapeDtypeStruct((sectors * rows, blk), jnp.bfloat16),
        scratch_shapes=[
            pltpu.VMEM((sectors, rows, blk), jnp.float32),
            pltpu.VMEM((n, 128), jnp.int32),
            pltpu.SMEM((n, 128), jnp.int32),
            pltpu.SemaphoreType.DMA,
        ],
        compiler_params=pltpu.CompilerParams(vmem_limit_bytes=VMEM_LIMIT),
        name="spread",
    )(*own, *other, *own, *other)


def place_kernel(plan, *refs):
    n = plan.places
    own, other = refs[:n], refs[n : 2 * n]
    outs = refs[2 * n : 2 * n + 2]
    sems = refs[2 * n + 2]
    op, sec = lax.axis_index("op"), lax.axis_index("sec")
    core, place = op % 2, plan.place(op, sec)

    def copies(mine, theirs):
        return [
            pltpu.make_async_copy(
                piece,
                out.at[:, pl.ds(pl.multiple_of((place ^ m) * plan.rows, plan.rows), plan.rows), :],
                sems.at[k, m],
            )
            for k, (pieces, out) in enumerate(((own, mine), (other, theirs)))
            for m, piece in enumerate(pieces)
        ]

    for c in range(2):

        @pl.when(core == c)
        def _():
            moving = copies(outs[c], outs[1 - c])
            for copy in moving:
                copy.start()
            for copy in moving:
                copy.wait()


def assemble(plan, own, other):
    anywhere = pl.BlockSpec(memory_space=pl.ANY)
    result = jax.ShapeDtypeStruct((plan.held, plan.blk, plan.blk), jnp.bfloat16)
    pieces = [x.reshape(plan.held, plan.rows, plan.blk) for x in (*own, *other)]
    return pl.pallas_call(
        functools.partial(place_kernel, plan),
        in_specs=[anywhere] * (2 * plan.places),
        out_specs=[anywhere] * 2,
        out_shape=[result, result],
        scratch_shapes=[pltpu.SemaphoreType.DMA((2, plan.places))],
        name="assemble",
    )(*pieces)


def per_device(mesh, first, second, left, right, source, target):
    plan = Plan(mesh, first, left.shape[0])
    core = plan.swap(1, 0)
    pieces = contract(plan, source, target, left, right, first, second)
    own = list(pieces)
    for m in reversed(range(1, plan.places)):
        own[m] = lax.ppermute(pieces[m], AXES, plan.across(m))
    other = [lax.ppermute(x, AXES, core) for x in own]

    away = spread(plan, 1, own, other)
    kept = spread(plan, 0, own, other)
    total = kept.astype(jnp.float32)
    for k, b in enumerate(plan.bits):
        arrived = lax.ppermute(away, AXES, plan.swap(0, 1 << b))
        total = total + arrived.astype(jnp.float32)
        if k + 1 < len(plan.bits):
            middle = total.shape[0] // 2
            away = total[middle:].astype(jnp.bfloat16)
            total = total[:middle]
    total = total.astype(jnp.bfloat16)

    size = plan.held * plan.rows
    sums = [total[e * size : (e + 1) * size] for e in range(2**plan.extra)]
    own = [sums[m % 2**plan.extra] for m in range(plan.places)]
    for m in reversed(range(1, plan.places)):
        own[m] = lax.ppermute(own[m], AXES, plan.across(m))
    other = [lax.ppermute(x, AXES, core) for x in own]
    return tuple(assemble(plan, own, other))


def solution(mesh):
    in_specs = (
        P("sec", None, None),
        P("sec", None, None),
        P(AXES, None, None),
        P(AXES, None, None),
        P(AXES),
        P(AXES),
    )
    out_specs = (P("sec", None, None), P("sec", None, None))
    return jax.shard_map(
        functools.partial(per_device, mesh),
        mesh=mesh,
        in_specs=in_specs,
        out_specs=out_specs,
        check_vma=False,
    )
```

time: 134 us -> 106 us (0.79)
  Pallas kernels: 0 us -> 45.9 us
  blocking collectives: 40.8 us -> 0 us
  matrix products: 32.6 us -> 0 us
  waiting for transfers between devices: 30.2 us -> 41.8 us
  local copies, waits for them, and re-layouts: 10.4 us -> 4.06 us
  starting transfers between devices: 16.8 us -> 13.4 us
  other arithmetic: 2.4 us -> 0.16 us
    pallas_call x0 -> x4, Pallas kernels: none -> 45.9 us  [the longest x1 32.9 us: assemble(): pl.pallas_call(functools.partial(place_kernel, plan), in_specs=[anywhere]...]
    ppermute x0 -> x16, waiting for transfers between devices: none -> 41.8 us  [the longest x2 22.5 us: per_device(): arrived = lax.ppermute(away, AXES, plan.swap(0, 1 << b))]
    psum x1 -> x0, blocking collectives: 40.8 us -> none  [per_device(): lax.psum((collect(arrived, labels_in), collect(arrived_second, labels_in)...]
    dot_general x6 -> x0, matrix products: 32.6 us -> none  [the longest x2 21 us: contract(): jnp.einsum('tik,tlk->til', halfway, right_ops, preferred_element_type=jnp...]
    all_to_all x3 -> x0, waiting for transfers between devices: 30.2 us -> none  [the longest x1 23.7 us: per_device(): lax.all_to_all(contract(psi_first), 'sec', split_axis=0, concat_axis=0, t...]
    all_to_all x3 -> x0, starting transfers between devices: 16.8 us -> none  [the longest x1 7.25 us: per_device(): lax.all_to_all(labels, 'sec', split_axis=0, concat_axis=0, tiled=True)]
    ppermute x0 -> x16, starting transfers between devices: none -> 13.4 us  [the longest x3 4.55 us: per_device(): own[m] = lax.ppermute(pieces[m], AXES, plan.across(m))]
    gather x2 -> x0, local copies, waits for them, and re-layouts: 5.5 us -> none  [contract(): source_blocks = jnp.take(wavefunction, source_local, axis=0)]
  transfers between devices with their start and end apart: 3 -> 16, of which waited for: 2 -> 11; matrix products, arithmetic and copies ran while one was open for 31% -> 0% of each run, Pallas kernels for 0% -> 1%
where the time goes in v1:
time: 106 us
  Pallas kernels  45.9 us (43%)
  waiting for transfers between devices  41.8 us (39%)
  starting transfers between devices  13.4 us (13%)
  local copies, waits for them, and re-layouts  4.06 us (4%)
    pallas_call x1, Pallas kernels, assemble(): pl.pallas_call(functools.partial(place_kernel, plan), in_specs=[anywhere]...  32.9 us
    ppermute x2, waiting for transfers between devices, per_device(): arrived = lax.ppermute(away, AXES, plan.swap(0, 1 << b))  22.5 us
    ppermute x3, waiting for transfers between devices, per_device(): own[m] = lax.ppermute(pieces[m], AXES, plan.across(m))  12.2 us
    pallas_call x1, Pallas kernels, contract(): pl.pallas_call(functools.partial(contract_kernel, plan, step), grid_spec=...  10.4 us
    ppermute x3, waiting for transfers between devices, per_device(): own[m] = lax.ppermute(own[m], AXES, plan.across(m))  4.66 us
    ppermute x3, starting transfers between devices, per_device(): own[m] = lax.ppermute(pieces[m], AXES, plan.across(m))  4.55 us
    ppermute x2, starting transfers between devices, per_device(): arrived = lax.ppermute(away, AXES, plan.swap(0, 1 << b))  4.31 us
    unnamed x24, local copies, waits for them, and re-layouts  4.01 us
  transfers between devices with their start and end apart: 16, of which 11 were waited for; matrix products, arithmetic and copies ran while one was open for 0% of the time, Pallas kernels for 1%

profile of v1, /device:TPU:0, one launch (start us, length us, event | category | flops | bytes accessed | tf_op | source)
XLA Modules:
  0.0 106.1 jit_solution(11595379517515385629)
XLA Ops:
  0.6 1.0 copy-done
  1.7 1.0 copy-done.1
  2.7 0.7 copy-done.2
  3.4 0.7 copy-done.3
  4.0 10.4 %contract.1 = (bf16[528,256]{1,0:T(8,128)(2,1)S(1)}, bf16[528,256]{1,0:T(8,128)(2,1)S(1)}, bf16[528,256]{1,0:T(8,128)(2,1)S(1)}, bf16[528,256]{1,0:T(8,128)(2,1)S(1)}) custom-call(s32[32]{0:T(128)S(1)} %copy-done.2, s32[32]{0:T(128)S(1)} %copy-done.3, bf16[32,256,256]{2,1,0:T(8,128)(2,1)} %left.1, bf16[32,256,256]{2,1,0:T(8,128)(2,1)} %right.1, ...), custom_call_target="tpu_custom_call" | custom-call | tf_op jit(solution)/shard_map/contract/pallas_call | solution.py:101
  14.4 3.0 %collective-permute-start = (bf16[528,256]{1,0:T(8,128)(2,1)S(1)}, bf16[528,256]{1,0:T(8,128)(2,1)S(1)}, u32[]{:S(2)}, u32[]{:S(2)}) collective-permute-start(bf16[528,256]{1,0:T(8,128)(2,1)S(1)} %get-tuple-element.7), channel_id=1, source_target_pairs={{0,1},{1,0},{2,3},{3,2},{4,5},{5,4},{6,7},{7,6},{8,9},{9,8},{10,11... | collective-permute-start | bytes 811016 | tf_op jit(solution)/shard_map/ppermute | solution.py:228
  17.4 1.5 %collective-permute-start.1 = (bf16[528,256]{1,0:T(8,128)(2,1)S(1)}, bf16[528,256]{1,0:T(8,128)(2,1)S(1)}, u32[]{:S(2)}, u32[]{:S(2)}) collective-permute-start(bf16[528,256]{1,0:T(8,128)(2,1)S(1)} %get-tuple-element.8), channel_id=1, source_target_pairs={{0,16},{1,17},{2,18},{3,19},{4,20},{5,21},{6,22},{7,23},{8,24},{9,... | collective-permute-start | bytes 811016 | tf_op jit(solution)/shard_map/ppermute | solution.py:228
  18.9 5.8 %collective-permute-done.refs_1_.refs_9_ = bf16[528,256]{1,0:T(8,128)(2,1)S(1)} collective-permute-done((bf16[528,256]{1,0:T(8,128)(2,1)S(1)}, bf16[528,256]{1,0:T(8,128)(2,1)S(1)}, u32[]{:S(2)}, u32[]{:S(2)}) %collective-permute-start) | collective-permute-done | bytes 270368 | tf_op jit(solution)/shard_map/ppermute | solution.py:228
  24.7 6.4 %collective-permute-done.1.refs_2_.refs_10_ = bf16[528,256]{1,0:T(8,128)(2,1)S(1)} collective-permute-done((bf16[528,256]{1,0:T(8,128)(2,1)S(1)}, bf16[528,256]{1,0:T(8,128)(2,1)S(1)}, u32[]{:S(2)}, u32[]{:S(2)}) %collective-permute-start.1) | collective-permute-done | bytes 270368 | tf_op jit(solution)/shard_map/ppermute | solution.py:228
  31.1 0.5 collective-permute-start.6
  31.7 1.0 collective-permute-done.5.refs_6_.refs_14_
  33.1 1.3 %spread.3 = bf16[1024,256]{1,0:T(8,128)(2,1)S(1)} custom-call(bf16[528,256]{1,0:T(8,128)(2,1)S(1)} %get-tuple-element.6.refs_0_.refs_8_, bf16[528,256]{1,0:T(8,128)(2,1)S(1)} %collective-permute-done.refs_1_.refs_9_, bf16[528,256]{1,0:T(8,128)(2,1)S(1)} %collective-permute-done.1.refs_2_.refs_10_, ...), custom_call_target="tpu_custom_call" | custom-call | tf_op jit(solution)/shard_map/spread/pallas_call | solution.py:161
  34.4 1.7 %collective-permute-start.7 = (bf16[1024,256]{1,0:T(8,128)(2,1)S(1)}, bf16[1024,256]{1,0:T(8,128)(2,1)S(1)}, u32[]{:S(2)}, u32[]{:S(2)}) collective-permute-start(bf16[1024,256]{1,0:T(8,128)(2,1)S(1)} %spread.3), channel_id=1, source_target_pairs={{0,2},{1,3},{2,0},{3,1},{4,6},{5,7},{6,4},{7,5},{8,10},{9,11},{10,... | collective-permute-start | bytes 1572872 | tf_op jit(solution)/shard_map/ppermute | solution.py:235
  36.0 1.3 %spread.2 = bf16[1024,256]{1,0:T(8,128)(2,1)S(1)} custom-call(bf16[528,256]{1,0:T(8,128)(2,1)S(1)} %get-tuple-element.6.refs_0_.refs_8_, bf16[528,256]{1,0:T(8,128)(2,1)S(1)} %collective-permute-done.refs_1_.refs_9_, bf16[528,256]{1,0:T(8,128)(2,1)S(1)} %collective-permute-done.1.refs_2_.refs_10_, ...), custom_call_target="tpu_custom_call" | custom-call | tf_op jit(solution)/shard_map/spread/pallas_call | solution.py:161
  37.4 11.0 %collective-permute-done.7 = bf16[1024,256]{1,0:T(8,128)(2,1)S(1)} collective-permute-done((bf16[1024,256]{1,0:T(8,128)(2,1)S(1)}, bf16[1024,256]{1,0:T(8,128)(2,1)S(1)}, u32[]{:S(2)}, u32[]{:S(2)}) %collective-permute-start.7) | collective-permute-done | bytes 524320 | tf_op jit(solution)/shard_map/ppermute | solution.py:235
  48.6 2.7 %collective-permute-start.8 = (bf16[512,256]{1,0:T(8,128)(2,1)S(1)}, bf16[512,256]{1,0:T(8,128)(2,1)S(1)}, u32[]{:S(2)}, u32[]{:S(2)}) collective-permute-start(bf16[512,256]{1,0:T(8,128)(2,1)S(1)} %slice.25), channel_id=1, source_target_pairs={{0,4},{1,5},{2,6},{3,7},{4,0},{5,1},{6,2},{7,3},{8,12},{9,13},{10,... | collective-permute-start | bytes 786440 | tf_op jit(solution)/shard_map/ppermute | solution.py:235
  51.2 11.4 %collective-permute-done.8 = bf16[512,256]{1,0:T(8,128)(2,1)S(1)} collective-permute-done((bf16[512,256]{1,0:T(8,128)(2,1)S(1)}, bf16[512,256]{1,0:T(8,128)(2,1)S(1)}, u32[]{:S(2)}, u32[]{:S(2)}) %collective-permute-start.8) | collective-permute-done | bytes 262176 | tf_op jit(solution)/shard_map/ppermute | solution.py:235
  62.8 1.6 %collective-permute-start.11 = (bf16[256,256]{1,0:T(8,128)(2,1)S(1)}, bf16[256,256]{1,0:T(8,128)(2,1)S(1)}, u32[]{:S(2)}, u32[]{:S(2)}) collective-permute-start(bf16[256,256]{1,0:T(8,128)(2,1)S(1)} %get-tuple-element.10), channel_id=1, source_target_pairs={{0,17},{1,16},{2,19},{3,18},{4,21},{5,20},{6,23},{7,22},{8,25},{9,... | collective-permute-start | bytes 393224 | tf_op jit(solution)/shard_map/ppermute | solution.py:247
  64.3 1.5 %collective-permute-start.9 = (bf16[256,256]{1,0:T(8,128)(2,1)S(1)}, bf16[256,256]{1,0:T(8,128)(2,1)S(1)}, u32[]{:S(2)}, u32[]{:S(2)}) collective-permute-start(bf16[256,256]{1,0:T(8,128)(2,1)S(1)} %get-tuple-element.10), channel_id=1, source_target_pairs={{0,1},{1,0},{2,3},{3,2},{4,5},{5,4},{6,7},{7,6},{8,9},{9,8},{10,11... | collective-permute-start | bytes 393224 | tf_op jit(solution)/shard_map/ppermute | solution.py:247
  65.8 0.5 collective-permute-start.10
  66.3 3.2 %collective-permute-done.11 = bf16[256,256]{1,0:T(8,128)(2,1)S(1)} collective-permute-done((bf16[256,256]{1,0:T(8,128)(2,1)S(1)}, bf16[256,256]{1,0:T(8,128)(2,1)S(1)}, u32[]{:S(2)}, u32[]{:S(2)}) %collective-permute-start.11) | collective-permute-done | bytes 131104 | tf_op jit(solution)/shard_map/ppermute | solution.py:247
  69.6 1.4 %collective-permute-done.9 = bf16[256,256]{1,0:T(8,128)(2,1)S(1)} collective-permute-done((bf16[256,256]{1,0:T(8,128)(2,1)S(1)}, bf16[256,256]{1,0:T(8,128)(2,1)S(1)}, u32[]{:S(2)}, u32[]{:S(2)}) %collective-permute-start.9) | collective-permute-done | bytes 131104 | tf_op jit(solution)/shard_map/ppermute | solution.py:247
  71.5 0.8 collective-permute-done.13
  73.1 32.9 %assemble.1 = (bf16[4,256,256]{2,1,0:T(8,128)(2,1)}, bf16[4,256,256]{2,1,0:T(8,128)(2,1)}) custom-call(bf16[4,64,256]{2,1,0:T(8,128)(2,1)} %bitcast.8, bf16[4,64,256]{2,1,0:T(8,128)(2,1)} %bitcast.10, bf16[4,64,256]{2,1,0:T(8,128)(2,1)} %bitcast.11, bf16[4,64,256]{2,1,0:T(8,128)(2,1)} %bitcast.9, bf16[4,64,256]{2,1,0:T(8,128)(2,1)} %bitcast.12, ...), custom_call_target="tpu_custom_call" | custom-call | tf_op jit(solution)/shard_map/assemble/pallas_call | solution.py:212
  (40 shorter events, 2.0 us)
Async XLA Ops:
  0.6 1.0 copy-start
  1.7 1.0 copy-start.1
  14.4 10.3 %collective-permute-start = (bf16[528,256]{1,0:T(8,128)(2,1)S(1)}, bf16[528,256]{1,0:T(8,128)(2,1)S(1)}, u32[]{:S(2)}, u32[]{:S(2)}) collective-permute-start(bf16[528,256]{1,0:T(8,128)(2,1)S(1)} %get-tuple-element.7), channel_id=1, source_target_pairs={{0,1},{1,0},{2,3},{3,2},{4,5},{5,4},{6,7},{7,6},{8,9},{9,8},{10,11... | collective-permute-start | bytes 811016 | tf_op jit(solution)/shard_map/ppermute | solution.py:228
  17.4 13.7 %collective-permute-start.1 = (bf16[528,256]{1,0:T(8,128)(2,1)S(1)}, bf16[528,256]{1,0:T(8,128)(2,1)S(1)}, u32[]{:S(2)}, u32[]{:S(2)}) collective-permute-start(bf16[528,256]{1,0:T(8,128)(2,1)S(1)} %get-tuple-element.8), channel_id=1, source_target_pairs={{0,16},{1,17},{2,18},{3,19},{4,20},{5,21},{6,22},{7,23},{8,24},{9,... | collective-permute-start | bytes 811016 | tf_op jit(solution)/shard_map/ppermute | solution.py:228
  18.9 12.2 %collective-permute-start.2 = (bf16[528,256]{1,0:T(8,128)(2,1)S(1)}, bf16[528,256]{1,0:T(8,128)(2,1)S(1)}, u32[]{:S(2)}, u32[]{:S(2)}) collective-permute-start(bf16[528,256]{1,0:T(8,128)(2,1)S(1)} %get-tuple-element.9), channel_id=1, source_target_pairs={{0,17},{1,16},{2,19},{3,18},{4,21},{5,20},{6,23},{7,22},{8,25},{9,... | collective-permute-start | bytes 811016 | tf_op jit(solution)/shard_map/ppermute | solution.py:228
  18.9 12.7 %collective-permute-start.3 = (bf16[528,256]{1,0:T(8,128)(2,1)S(1)}, bf16[528,256]{1,0:T(8,128)(2,1)S(1)}, u32[]{:S(2)}, u32[]{:S(2)}) collective-permute-start(bf16[528,256]{1,0:T(8,128)(2,1)S(1)} %get-tuple-element.6.refs_0_.refs_8_), channel_id=1, source_target_pairs={{0,8},{1,9},{2,10},{3,11},{4,12},{5,13},{6,14},{7,15},{8,0},{9,1},... | collective-permute-start | bytes 811016 | tf_op jit(solution)/shard_map/ppermute | solution.py:229
  24.7 6.9 %collective-permute-start.4 = (bf16[528,256]{1,0:T(8,128)(2,1)S(1)}, bf16[528,256]{1,0:T(8,128)(2,1)S(1)}, u32[]{:S(2)}, u32[]{:S(2)}) collective-permute-start(bf16[528,256]{1,0:T(8,128)(2,1)S(1)} %collective-permute-done.refs_1_.refs_9_), channel_id=1, source_target_pairs={{0,8},{1,9},{2,10},{3,11},{4,12},{5,13},{6,14},{7,15},{8,0},{9,1},... | collective-permute-start | bytes 811016 | tf_op jit(solution)/shard_map/ppermute | solution.py:229
  31.1 1.5 %collective-permute-start.5 = (bf16[528,256]{1,0:T(8,128)(2,1)S(1)}, bf16[528,256]{1,0:T(8,128)(2,1)S(1)}, u32[]{:S(2)}, u32[]{:S(2)}) collective-permute-start(bf16[528,256]{1,0:T(8,128)(2,1)S(1)} %collective-permute-done.1.refs_2_.refs_10_), channel_id=1, source_target_pairs={{0,8},{1,9},{2,10},{3,11},{4,12},{5,13},{6,14},{7,15},{8,0},{9,1},... | collective-permute-start | bytes 811016 | tf_op jit(solution)/shard_map/ppermute | solution.py:229
  31.1 1.9 %collective-permute-start.6 = (bf16[528,256]{1,0:T(8,128)(2,1)S(1)}, bf16[528,256]{1,0:T(8,128)(2,1)S(1)}, u32[]{:S(2)}, u32[]{:S(2)}) collective-permute-start(bf16[528,256]{1,0:T(8,128)(2,1)S(1)} %collective-permute-done.2.refs_3_.refs_11_), channel_id=1, source_target_pairs={{0,8},{1,9},{2,10},{3,11},{4,12},{5,13},{6,14},{7,15},{8,0},{9,1},... | collective-permute-start | bytes 811016 | tf_op jit(solution)/shard_map/ppermute | solution.py:229
  34.4 14.0 %collective-permute-start.7 = (bf16[1024,256]{1,0:T(8,128)(2,1)S(1)}, bf16[1024,256]{1,0:T(8,128)(2,1)S(1)}, u32[]{:S(2)}, u32[]{:S(2)}) collective-permute-start(bf16[1024,256]{1,0:T(8,128)(2,1)S(1)} %spread.3), channel_id=1, source_target_pairs={{0,2},{1,3},{2,0},{3,1},{4,6},{5,7},{6,4},{7,5},{8,10},{9,11},{10,... | collective-permute-start | bytes 1572872 | tf_op jit(solution)/shard_map/ppermute | solution.py:235
  48.6 14.1 %collective-permute-start.8 = (bf16[512,256]{1,0:T(8,128)(2,1)S(1)}, bf16[512,256]{1,0:T(8,128)(2,1)S(1)}, u32[]{:S(2)}, u32[]{:S(2)}) collective-permute-start(bf16[512,256]{1,0:T(8,128)(2,1)S(1)} %slice.25), channel_id=1, source_target_pairs={{0,4},{1,5},{2,6},{3,7},{4,0},{5,1},{6,2},{7,3},{8,12},{9,13},{10,... | collective-permute-start | bytes 786440 | tf_op jit(solution)/shard_map/ppermute | solution.py:235
  62.8 9.7 %copy-start.4 = (bf16[256,256]{1,0:T(8,128)(2,1)}, bf16[256,256]{1,0:T(8,128)(2,1)S(1)}, u32[]{:S(2)}) copy-start(bf16[256,256]{1,0:T(8,128)(2,1)S(1)} %get-tuple-element.11) | copy-start | bytes 393220
  62.8 6.8 %collective-permute-start.11 = (bf16[256,256]{1,0:T(8,128)(2,1)S(1)}, bf16[256,256]{1,0:T(8,128)(2,1)S(1)}, u32[]{:S(2)}, u32[]{:S(2)}) collective-permute-start(bf16[256,256]{1,0:T(8,128)(2,1)S(1)} %get-tuple-element.10), channel_id=1, source_target_pairs={{0,17},{1,16},{2,19},{3,18},{4,21},{5,20},{6,23},{7,22},{8,25},{9,... | collective-permute-start | bytes 393224 | tf_op jit(solution)/shard_map/ppermute | solution.py:247
  64.3 6.6 %collective-permute-start.9 = (bf16[256,256]{1,0:T(8,128)(2,1)S(1)}, bf16[256,256]{1,0:T(8,128)(2,1)S(1)}, u32[]{:S(2)}, u32[]{:S(2)}) collective-permute-start(bf16[256,256]{1,0:T(8,128)(2,1)S(1)} %get-tuple-element.10), channel_id=1, source_target_pairs={{0,1},{1,0},{2,3},{3,2},{4,5},{5,4},{6,7},{7,6},{8,9},{9,8},{10,11... | collective-permute-start | bytes 393224 | tf_op jit(solution)/shard_map/ppermute | solution.py:247
  65.8 5.2 %collective-permute-start.10 = (bf16[256,256]{1,0:T(8,128)(2,1)S(1)}, bf16[256,256]{1,0:T(8,128)(2,1)S(1)}, u32[]{:S(2)}, u32[]{:S(2)}) collective-permute-start(bf16[256,256]{1,0:T(8,128)(2,1)S(1)} %get-tuple-element.11), channel_id=1, source_target_pairs={{0,16},{1,17},{2,18},{3,19},{4,20},{5,21},{6,22},{7,23},{8,24},{9,... | collective-permute-start | bytes 393224 | tf_op jit(solution)/shard_map/ppermute | solution.py:247
  66.3 5.1 %collective-permute-start.12 = (bf16[256,256]{1,0:T(8,128)(2,1)S(1)}, bf16[256,256]{1,0:T(8,128)(2,1)S(1)}, u32[]{:S(2)}, u32[]{:S(2)}) collective-permute-start(bf16[256,256]{1,0:T(8,128)(2,1)S(1)} %get-tuple-element.11), channel_id=1, source_target_pairs={{0,8},{1,9},{2,10},{3,11},{4,12},{5,13},{6,14},{7,15},{8,0},{9,1},... | collective-permute-start | bytes 393224 | tf_op jit(solution)/shard_map/ppermute | solution.py:248
  69.6 2.9 %copy-start.5 = (bf16[256,256]{1,0:T(8,128)(2,1)}, bf16[256,256]{1,0:T(8,128)(2,1)S(1)}, u32[]{:S(2)}) copy-start(bf16[256,256]{1,0:T(8,128)(2,1)S(1)} %collective-permute-done.11) | copy-start | bytes 393220
  69.6 1.9 %collective-permute-start.15 = (bf16[256,256]{1,0:T(8,128)(2,1)S(1)}, bf16[256,256]{1,0:T(8,128)(2,1)S(1)}, u32[]{:S(2)}, u32[]{:S(2)}) collective-permute-start(bf16[256,256]{1,0:T(8,128)(2,1)S(1)} %collective-permute-done.11), channel_id=1, source_target_pairs={{0,8},{1,9},{2,10},{3,11},{4,12},{5,13},{6,14},{7,15},{8,0},{9,1},... | collective-permute-start | bytes 393224 | tf_op jit(solution)/shard_map/ppermute | solution.py:248
  70.9 1.5 %copy-start.6 = (bf16[256,256]{1,0:T(8,128)(2,1)}, bf16[256,256]{1,0:T(8,128)(2,1)S(1)}, u32[]{:S(2)}) copy-start(bf16[256,256]{1,0:T(8,128)(2,1)S(1)} %collective-permute-done.9) | copy-start | bytes 393220
  70.9 1.3 %collective-permute-start.13 = (bf16[256,256]{1,0:T(8,128)(2,1)S(1)}, bf16[256,256]{1,0:T(8,128)(2,1)S(1)}, u32[]{:S(2)}, u32[]{:S(2)}) collective-permute-start(bf16[256,256]{1,0:T(8,128)(2,1)S(1)} %collective-permute-done.9), channel_id=1, source_target_pairs={{0,8},{1,9},{2,10},{3,11},{4,12},{5,13},{6,14},{7,15},{8,0},{9,1},... | collective-permute-start | bytes 393224 | tf_op jit(solution)/shard_map/ppermute | solution.py:248
  71.0 1.5 %copy-start.7 = (bf16[256,256]{1,0:T(8,128)(2,1)}, bf16[256,256]{1,0:T(8,128)(2,1)S(1)}, u32[]{:S(2)}) copy-start(bf16[256,256]{1,0:T(8,128)(2,1)S(1)} %collective-permute-done.10) | copy-start | bytes 393220
  71.0 1.5 %collective-permute-start.14 = (bf16[256,256]{1,0:T(8,128)(2,1)S(1)}, bf16[256,256]{1,0:T(8,128)(2,1)S(1)}, u32[]{:S(2)}, u32[]{:S(2)}) collective-permute-start(bf16[256,256]{1,0:T(8,128)(2,1)S(1)} %collective-permute-done.10), channel_id=1, source_target_pairs={{0,8},{1,9},{2,10},{3,11},{4,12},{5,13},{6,14},{7,15},{8,0},{9,1},... | collective-permute-start | bytes 393224 | tf_op jit(solution)/shard_map/ppermute | solution.py:248
  71.5 1.0 copy-start.8
  71.5 1.0 copy-start.9
  (4 other events, 2.6 us)

commit v2 on v1

v2 whole, which is shorter than its diff:
```python
import functools

import jax
import jax.numpy as jnp
from jax import lax
from jax.experimental import pallas as pl
from jax.experimental.pallas import tpu as pltpu
from jax.sharding import PartitionSpec as P

VMEM_LIMIT = 24 * 1024 * 1024
LABEL_ROWS = 16
AXES = ("op", "sec")


class Plan:
    def __init__(self, mesh, psi, terms):
        self.op, self.sec = mesh.shape["op"], mesh.shape["sec"]
        self.held, self.blk = psi.shape[0], psi.shape[1]
        self.terms = terms
        self.slots = self.sec // 2
        self.extra = 0
        while self.slots * self.op * 2**self.extra < self.held * self.sec:
            self.extra += 1
        self.places = (self.op // 2) * 2**self.extra
        self.rows = self.blk // (2 * self.places)
        self.step = 4
        self.bits = list(range(self.extra, self.sec.bit_length() - 1))

    def place(self, op, sec):
        return (op // 2) * 2**self.extra + sec % 2**self.extra

    def swap(self, op_mask, sec_mask):
        n = self.op * self.sec
        mask = op_mask * self.sec + sec_mask
        return [(i, i ^ mask) for i in range(n)]

    def across(self, m):
        return self.swap((m >> self.extra) << 1, m & (2**self.extra - 1))


def contract_kernel(plan, nv, *refs):
    source, target, left, right = refs[:4]
    vectors = refs[4 : 4 + nv]
    outs = refs[4 + nv : 4 + nv + plan.places]
    src, tgt, lhs, rhs, psi, acc, slot_of, labels, seen, sems, first_sems = refs[4 + nv + plan.places :]
    blk, terms = plan.blk, plan.terms

    heads = [pltpu.make_async_copy(x, y, first_sems.at[i]) for i, (x, y) in enumerate(((target, tgt), (source, src)))]
    heads += [pltpu.make_async_copy(x, psi.at[v], first_sems.at[2 + v]) for v, x in enumerate(vectors)]
    for copy in heads:
        copy.start()

    def loads(c):
        part = pl.ds(c * plan.step, plan.step)
        return [
            pltpu.make_async_copy(left.at[part], lhs.at[part], sems.at[0, c]),
            pltpu.make_async_copy(right.at[part], rhs.at[part], sems.at[1, c]),
        ]

    for c in range(terms // plan.step):
        for copy in loads(c):
            copy.start()
    for h in range(plan.sec):
        seen[h] = -1
    acc[...] = jnp.zeros_like(acc)
    heads[0].wait()

    def name(t, count):
        goal = tgt[t]
        holder = goal // plan.held
        fresh = seen[holder] < 0
        slot = jnp.where(fresh, count, seen[holder])
        seen[holder] = slot
        labels[slot] = goal
        slot_of[t] = slot
        return count + fresh.astype(jnp.int32)

    lax.fori_loop(0, terms, name, jnp.int32(0))
    for copy in heads[1:]:
        copy.wait()

    for t in range(terms):
        if t % plan.step == 0:
            for copy in loads(t // plan.step):
                copy.wait()
        half = [
            jnp.dot(lhs[t], psi[v, src[t]], preferred_element_type=jnp.float32).astype(jnp.bfloat16)
            for v in range(nv)
        ]
        both = jnp.concatenate(half, axis=0) if nv > 1 else half[0]
        acc[slot_of[t]] += lax.dot_general(
            both, rhs[t], (((1,), (1,)), ((), ())), preferred_element_type=jnp.float32
        )

    op, sec = lax.axis_index("op"), lax.axis_index("sec")
    core, place = op % 2, plan.place(op, sec)
    lane = lax.broadcasted_iota(jnp.int32, (LABEL_ROWS, blk), 1)
    tile = jnp.zeros((LABEL_ROWS, blk), jnp.float32)
    for j in range(plan.slots):
        tile = jnp.where(lane == j, labels[j].astype(jnp.float32), tile)
    tile = tile.astype(jnp.bfloat16)
    for m in range(plan.places):
        for rc in range(2):
            row = ((place ^ m) * 2 + (core ^ rc)) * plan.rows
            for v in range(nv):
                base = pl.multiple_of(v * blk + row, plan.rows)
                for j in range(plan.slots):
                    to = ((rc * nv + v) * plan.slots + j) * plan.rows
                    outs[m][pl.ds(to, plan.rows), :] = acc[j, pl.ds(base, plan.rows), :].astype(jnp.bfloat16)
        outs[m][pl.ds(2 * nv * plan.slots * plan.rows, LABEL_ROWS), :] = tile


def contract(plan, source, target, left, right, vectors):
    nv, blk, terms = len(vectors), plan.blk, plan.terms
    height = 2 * nv * plan.slots * plan.rows + LABEL_ROWS
    bf16 = jnp.bfloat16
    arrays = [pltpu.with_memory_space_constraint(x, pltpu.HBM) for x in (source, target, left, right, *vectors)]
    flops = 4 * nv * terms * blk**3
    return pl.pallas_call(
        functools.partial(contract_kernel, plan, nv),
        in_specs=[pl.BlockSpec(memory_space=pltpu.HBM)] * len(arrays),
        out_specs=[pl.BlockSpec(memory_space=pltpu.VMEM)] * plan.places,
        out_shape=[pltpu.VMEM((height, blk), bf16)] * plan.places,
        scratch_shapes=[
            pltpu.SMEM((terms,), jnp.int32),
            pltpu.SMEM((terms,), jnp.int32),
            pltpu.VMEM((terms, blk, blk), bf16),
            pltpu.VMEM((terms, blk, blk), bf16),
            pltpu.VMEM((nv, plan.held, blk, blk), bf16),
            pltpu.VMEM((plan.slots, nv * blk, blk), jnp.float32),
            pltpu.SMEM((terms,), jnp.int32),
            pltpu.SMEM((plan.slots,), jnp.int32),
            pltpu.SMEM((plan.sec,), jnp.int32),
            pltpu.SemaphoreType.DMA((2, terms // plan.step)),
            pltpu.SemaphoreType.DMA((2 + nv,)),
        ],
        cost_estimate=pl.CostEstimate(flops=flops, bytes_accessed=4 * terms * blk * blk, transcendentals=0),
        compiler_params=pltpu.CompilerParams(vmem_limit_bytes=VMEM_LIMIT),
        name="contract",
    )(*arrays)


def spread_kernel(plan, nv, want, *refs):
    n = 2 * plan.places
    blocks, tags, out = refs[:n], refs[n : 2 * n], refs[2 * n]
    acc, tags_vector, tags_scalar, sem = refs[2 * n + 1 :]
    for i in range(n):
        row = jnp.max(tags[i][...].astype(jnp.float32), axis=0, keepdims=True)
        tags_vector[pl.ds(i, 1), :] = row[:, :128].astype(jnp.int32)
    copy = pltpu.make_async_copy(tags_vector, tags_scalar, sem)
    copy.start()
    acc[...] = jnp.zeros_like(acc)
    copy.wait()
    sec = lax.axis_index("sec")
    for i in range(n):
        for j in range(plan.slots):
            label = tags_scalar[i, j]
            away = (label // plan.held) ^ sec
            index = jnp.int32(0)
            for b in plan.bits[1:]:
                index = index * 2 + ((away >> b) & 1)
            index = index * 2**plan.extra + (away & (2**plan.extra - 1))

            @pl.when(((away >> plan.bits[0]) & 1) == want)
            def _():
                for v in range(nv):
                    block = blocks[i][pl.ds((v * plan.slots + j) * plan.rows, plan.rows), :]
                    acc[(index * nv + v) * plan.held + label % plan.held] += block.astype(jnp.float32)

    out[...] = acc[...].astype(jnp.bfloat16).reshape(out.shape)


def spread(plan, nv, want, own, other):
    blk, rows, slots = plan.blk, plan.rows, plan.slots
    sectors = nv * plan.held * 2 ** (plan.extra + len(plan.bits) - 1)
    n = 2 * plan.places

    def half(rc):
        return pl.BlockSpec((nv * slots * rows, blk), lambda t: (rc, 0))

    tag = pl.BlockSpec((LABEL_ROWS, blk), lambda t: (2 * nv * slots * rows // LABEL_ROWS, 0))
    return pl.pallas_call(
        functools.partial(spread_kernel, plan, nv, want),
        grid=(1,),
        in_specs=[half(0)] * plan.places + [half(1)] * plan.places + [tag] * n,
        out_specs=pl.BlockSpec((sectors * rows, blk), lambda t: (0, 0)),
        out_shape=jax.ShapeDtypeStruct((sectors * rows, blk), jnp.bfloat16),
        scratch_shapes=[
            pltpu.VMEM((sectors, rows, blk), jnp.float32),
            pltpu.VMEM((n, 128), jnp.int32),
            pltpu.SMEM((n, 128), jnp.int32),
            pltpu.SemaphoreType.DMA,
        ],
        compiler_params=pltpu.CompilerParams(vmem_limit_bytes=VMEM_LIMIT),
        name="spread",
    )(*own, *other, *own, *other)


def place_kernel(plan, nv, *refs):
    n = 2 * plan.places
    pieces, outs, sems = refs[:n], refs[n : n + nv], refs[n + nv]
    op, sec = lax.axis_index("op"), lax.axis_index("sec")
    core, place = op % 2, plan.place(op, sec)
    moving = []
    for i, piece in enumerate(pieces):
        rc, m = divmod(i, plan.places)
        row = pl.multiple_of(((place ^ m) * 2 + (core ^ rc)) * plan.rows, plan.rows)
        for v in range(nv):
            moving.append(pltpu.make_async_copy(piece.at[v], outs[v].at[:, pl.ds(row, plan.rows), :], sems.at[i, v]))
    for copy in moving:
        copy.start()
    for copy in moving:
        copy.wait()


def assemble(plan, nv, own, other):
    result = jax.ShapeDtypeStruct((plan.held, plan.blk, plan.blk), jnp.bfloat16)
    pieces = [
        pltpu.with_memory_space_constraint(x.reshape(nv, plan.held, plan.rows, plan.blk), pltpu.VMEM)
        for x in (*own, *other)
    ]
    return pl.pallas_call(
        functools.partial(place_kernel, plan, nv),
        in_specs=[pl.BlockSpec(memory_space=pltpu.VMEM)] * len(pieces),
        out_specs=[pl.BlockSpec(memory_space=pl.ANY)] * nv,
        out_shape=[result] * nv,
        scratch_shapes=[pltpu.SemaphoreType.DMA((len(pieces), nv))],
        compiler_params=pltpu.CompilerParams(vmem_limit_bytes=VMEM_LIMIT),
        name="assemble",
    )(*pieces)


def exchange(plan, pieces):
    own = list(pieces)
    for m in reversed(range(1, plan.places)):
        own[m] = lax.ppermute(pieces[m], AXES, plan.across(m))
    other = [lax.ppermute(x, AXES, plan.swap(1, 0)) for x in own]
    return own, other


def combine(plan, nv, pieces):
    own, other = exchange(plan, pieces)
    away = spread(plan, nv, 1, own, other)
    kept = spread(plan, nv, 0, own, other)
    total = kept.astype(jnp.float32)
    for k, b in enumerate(plan.bits):
        arrived = lax.ppermute(away, AXES, plan.swap(0, 1 << b))
        total = total + arrived.astype(jnp.float32)
        if k + 1 < len(plan.bits):
            middle = total.shape[0] // 2
            away = total[middle:].astype(jnp.bfloat16)
            total = total[:middle]
    total = total.astype(jnp.bfloat16)
    size = nv * plan.held * plan.rows
    sums = [total[e * size : (e + 1) * size] for e in range(2**plan.extra)]
    own, other = exchange(plan, [sums[m % 2**plan.extra] for m in range(plan.places)])
    return assemble(plan, nv, own, other)


def per_device(mesh, groups, first, second, left, right, source, target):
    plan = Plan(mesh, first, left.shape[0])
    vectors = (first, second)
    results = []
    for group in groups:
        pieces = contract(plan, source, target, left, right, [vectors[v] for v in group])
        results += combine(plan, len(group), pieces)
    return tuple(results)


def solution(mesh):
    in_specs = (
        P("sec", None, None),
        P("sec", None, None),
        P(AXES, None, None),
        P(AXES, None, None),
        P(AXES),
        P(AXES),
    )
    out_specs = (P("sec", None, None), P("sec", None, None))
    return jax.shard_map(
        functools.partial(per_device, mesh, ((0,), (1,))),
        mesh=mesh,
        in_specs=in_specs,
        out_specs=out_specs,
        check_vma=False,
    )
```

time: 106 us -> 69.7 us (0.66)
  Pallas kernels: 45.9 us -> 22.7 us
  waiting for transfers between devices: 41.8 us -> 21.6 us
  starting transfers between devices: 13.4 us -> 24.1 us
  local copies, waits for them, and re-layouts: 4.06 us -> 0.05 us
    pallas_call x4 -> x8, Pallas kernels: 45.9 us -> 22.7 us  [the longest x2 16 us: contract(): pl.pallas_call(functools.partial(contract_kernel, plan, nv), in_specs=[pl...]
    ppermute x16 -> x32, waiting for transfers between devices: 41.8 us -> 21.6 us  [the longest x12 12.5 us: exchange(): own[m] = lax.ppermute(pieces[m], AXES, plan.across(m))]
    ppermute x16 -> x32, starting transfers between devices: 13.4 us -> 24.1 us  [the longest x12 15.2 us: exchange(): own[m] = lax.ppermute(pieces[m], AXES, plan.across(m))]
    unnamed x24 -> x0, local copies, waits for them, and re-layouts: 4.01 us -> none
  transfers between devices with their start and end apart: 16 -> 32, of which waited for: 11 -> 11; matrix products, arithmetic and copies ran while one was open for 0% -> 0% of each run, Pallas kernels for 1% -> 20%
where the time goes in v2:
time: 69.7 us; the launch traced here: 69.5 us
  starting transfers between devices  24.1 us (35%)
  Pallas kernels  22.7 us (33%)
  waiting for transfers between devices  21.6 us (31%)
  between operations  0.81 us (1%)
    pallas_call x2, Pallas kernels, contract(): pl.pallas_call(functools.partial(contract_kernel, plan, nv), in_specs=[pl...  16 us
    ppermute x12, starting transfers between devices, exchange(): own[m] = lax.ppermute(pieces[m], AXES, plan.across(m))  15.2 us
    ppermute x12, waiting for transfers between devices, exchange(): own[m] = lax.ppermute(pieces[m], AXES, plan.across(m))  12.5 us
    ppermute x4, waiting for transfers between devices, combine(): arrived = lax.ppermute(away, AXES, plan.swap(0, 1 << b))  7.49 us
    ppermute x4, starting transfers between devices, combine(): arrived = lax.ppermute(away, AXES, plan.swap(0, 1 << b))  6.79 us
    pallas_call x4, Pallas kernels, spread(): pl.pallas_call(functools.partial(spread_kernel, plan, nv, want), grid=(1,...  5.05 us
    ppermute x16, starting transfers between devices, exchange(): other = [lax.ppermute(x, AXES, plan.swap(1, 0)) for x in own]  2.13 us
    pallas_call x2, Pallas kernels, assemble(): pl.pallas_call(functools.partial(place_kernel, plan, nv), in_specs=[pl.Bl...  1.69 us
  transfers between devices with their start and end apart: 32, of which 11 were waited for; matrix products, arithmetic and copies ran while one was open for 0% of the time, Pallas kernels for 20%

profile of v2, /device:TPU:0, one launch (start us, length us, event | category | flops | bytes accessed | tf_op | source)
XLA Modules:
  0.0 69.5 jit_solution(10680447353575052078)
XLA Ops:
  0.6 8.0 %contract.2 = (bf16[272,256]{1,0:T(8,128)(2,1)S(1)}, bf16[272,256]{1,0:T(8,128)(2,1)S(1)}, bf16[272,256]{1,0:T(8,128)(2,1)S(1)}, bf16[272,256]{1,0:T(8,128)(2,1)S(1)}) custom-call(s32[32]{0:T(128)} %refs_0_.3, s32[32]{0:T(128)} %refs_1_.3, bf16[32,256,256]{2,1,0:T(8,128)(2,1)} %refs_2_.3, bf16[32,256,256]{2,1,0:T(8,128)(2,1)} %refs_3_.3, ...), custom_call_target="tpu_custom_call" | custom-call | flops 2147483648 | bytes 8388608 | tf_op jit(solution)/shard_map/contract/pallas_call | solution.py:119
  8.6 3.0 %collective-permute-start = (bf16[272,256]{1,0:T(8,128)(2,1)S(1)}, bf16[272,256]{1,0:T(8,128)(2,1)S(1)}, u32[]{:S(2)}, u32[]{:S(2)}) collective-permute-start(bf16[272,256]{1,0:T(8,128)(2,1)S(1)} %get-tuple-element.11), channel_id=1, source_target_pairs={{0,1},{1,0},{2,3},{3,2},{4,5},{5,4},{6,7},{7,6},{8,9},{9,8},{10,11... | collective-permute-start | bytes 417800 | tf_op jit(solution)/shard_map/ppermute | solution.py:236
  11.6 1.5 %collective-permute-start.1 = (bf16[272,256]{1,0:T(8,128)(2,1)S(1)}, bf16[272,256]{1,0:T(8,128)(2,1)S(1)}, u32[]{:S(2)}, u32[]{:S(2)}) collective-permute-start(bf16[272,256]{1,0:T(8,128)(2,1)S(1)} %get-tuple-element.12), channel_id=1, source_target_pairs={{0,16},{1,17},{2,18},{3,19},{4,20},{5,21},{6,22},{7,23},{8,24},{9,... | collective-permute-start | bytes 417800 | tf_op jit(solution)/shard_map/ppermute | solution.py:236
  13.2 2.5 %collective-permute-done.refs_1_.refs_9_ = bf16[272,256]{1,0:T(8,128)(2,1)S(1)} collective-permute-done((bf16[272,256]{1,0:T(8,128)(2,1)S(1)}, bf16[272,256]{1,0:T(8,128)(2,1)S(1)}, u32[]{:S(2)}, u32[]{:S(2)}) %collective-permute-start) | collective-permute-done | bytes 139296 | tf_op jit(solution)/shard_map/ppermute | solution.py:236
  15.7 4.0 %collective-permute-done.1.refs_2_.refs_10_ = bf16[272,256]{1,0:T(8,128)(2,1)S(1)} collective-permute-done((bf16[272,256]{1,0:T(8,128)(2,1)S(1)}, bf16[272,256]{1,0:T(8,128)(2,1)S(1)}, u32[]{:S(2)}, u32[]{:S(2)}) %collective-permute-start.1) | collective-permute-done | bytes 139296 | tf_op jit(solution)/shard_map/ppermute | solution.py:236
  20.3 8.0 %contract.3 = (bf16[272,256]{1,0:T(8,128)(2,1)S(1)}, bf16[272,256]{1,0:T(8,128)(2,1)S(1)}, bf16[272,256]{1,0:T(8,128)(2,1)S(1)}, bf16[272,256]{1,0:T(8,128)(2,1)S(1)}) custom-call(s32[32]{0:T(128)} %refs_0_.3, s32[32]{0:T(128)} %refs_1_.3, bf16[32,256,256]{2,1,0:T(8,128)(2,1)} %refs_2_.3, bf16[32,256,256]{2,1,0:T(8,128)(2,1)} %refs_3_.3, ...), custom_call_target="tpu_custom_call" | custom-call | flops 2147483648 | bytes 8388608 | tf_op jit(solution)/shard_map/contract/pallas_call | solution.py:119
  29.1 1.3 %collective-permute-start.17 = (bf16[272,256]{1,0:T(8,128)(2,1)S(1)}, bf16[272,256]{1,0:T(8,128)(2,1)S(1)}, u32[]{:S(2)}, u32[]{:S(2)}) collective-permute-start(bf16[272,256]{1,0:T(8,128)(2,1)S(1)} %get-tuple-element.16), channel_id=1, source_target_pairs={{0,16},{1,17},{2,18},{3,19},{4,20},{5,21},{6,22},{7,23},{8,24},{9,... | collective-permute-start | bytes 417800 | tf_op jit(solution)/shard_map/ppermute | solution.py:236
  30.4 1.4 %collective-permute-start.18 = (bf16[272,256]{1,0:T(8,128)(2,1)S(1)}, bf16[272,256]{1,0:T(8,128)(2,1)S(1)}, u32[]{:S(2)}, u32[]{:S(2)}) collective-permute-start(bf16[272,256]{1,0:T(8,128)(2,1)S(1)} %get-tuple-element.17), channel_id=1, source_target_pairs={{0,17},{1,16},{2,19},{3,18},{4,21},{5,20},{6,23},{7,22},{8,25},{9,... | collective-permute-start | bytes 417800 | tf_op jit(solution)/shard_map/ppermute | solution.py:236
  31.9 1.3 %spread.5 = bf16[512,256]{1,0:T(8,128)(2,1)S(1)} custom-call(bf16[272,256]{1,0:T(8,128)(2,1)S(1)} %get-tuple-element.10.refs_0_.refs_8_, bf16[272,256]{1,0:T(8,128)(2,1)S(1)} %collective-permute-done.refs_1_.refs_9_, bf16[272,256]{1,0:T(8,128)(2,1)S(1)} %collective-permute-done.1.refs_2_.refs_10_, ...), custom_call_target="tpu_custom_call" | custom-call | tf_op jit(solution)/shard_map/spread/pallas_call | solution.py:182
  33.1 1.6 %collective-permute-start.7 = (bf16[512,256]{1,0:T(8,128)(2,1)S(1)}, bf16[512,256]{1,0:T(8,128)(2,1)S(1)}, u32[]{:S(2)}, u32[]{:S(2)}) collective-permute-start(bf16[512,256]{1,0:T(8,128)(2,1)S(1)} %spread.5), channel_id=1, source_target_pairs={{0,2},{1,3},{2,0},{3,1},{4,6},{5,7},{6,4},{7,5},{8,10},{9,11},{10,... | collective-permute-start | bytes 786440 | tf_op jit(solution)/shard_map/ppermute | solution.py:247
  35.3 1.0 %collective-permute-done.17.refs_2_.refs_10_ = bf16[272,256]{1,0:T(8,128)(2,1)S(1)} collective-permute-done((bf16[272,256]{1,0:T(8,128)(2,1)S(1)}, bf16[272,256]{1,0:T(8,128)(2,1)S(1)}, u32[]{:S(2)}, u32[]{:S(2)}) %collective-permute-start.17) | collective-permute-done | bytes 139296 | tf_op jit(solution)/shard_map/ppermute | solution.py:236
  36.3 1.6 %collective-permute-done.18.refs_3_.refs_11_ = bf16[272,256]{1,0:T(8,128)(2,1)S(1)} collective-permute-done((bf16[272,256]{1,0:T(8,128)(2,1)S(1)}, bf16[272,256]{1,0:T(8,128)(2,1)S(1)}, u32[]{:S(2)}, u32[]{:S(2)}) %collective-permute-start.18) | collective-permute-done | bytes 139296 | tf_op jit(solution)/shard_map/ppermute | solution.py:236
  37.9 1.3 %collective-permute-done.22.refs_7_.refs_15_ = bf16[272,256]{1,0:T(8,128)(2,1)S(1)} collective-permute-done((bf16[272,256]{1,0:T(8,128)(2,1)S(1)}, bf16[272,256]{1,0:T(8,128)(2,1)S(1)}, u32[]{:S(2)}, u32[]{:S(2)}) %collective-permute-start.22) | collective-permute-done | bytes 139296 | tf_op jit(solution)/shard_map/ppermute | solution.py:237
  39.2 1.3 %spread.7 = bf16[512,256]{1,0:T(8,128)(2,1)S(1)} custom-call(bf16[272,256]{1,0:T(8,128)(2,1)S(1)} %get-tuple-element.14.refs_0_.refs_8_, bf16[272,256]{1,0:T(8,128)(2,1)S(1)} %collective-permute-done.16.refs_1_.refs_9_, bf16[272,256]{1,0:T(8,128)(2,1)S(1)} %collective-permute-done.17.refs_2_.refs_10_, ...), custom_call_target="tpu_custom_call" | custom-call | tf_op jit(solution)/shard_map/spread/pallas_call | solution.py:182
  40.5 1.6 %collective-permute-start.23 = (bf16[512,256]{1,0:T(8,128)(2,1)S(1)}, bf16[512,256]{1,0:T(8,128)(2,1)S(1)}, u32[]{:S(2)}, u32[]{:S(2)}) collective-permute-start(bf16[512,256]{1,0:T(8,128)(2,1)S(1)} %spread.7), channel_id=1, source_target_pairs={{0,2},{1,3},{2,0},{3,1},{4,6},{5,7},{6,4},{7,5},{8,10},{9,11},{10,... | collective-permute-start | bytes 786440 | tf_op jit(solution)/shard_map/ppermute | solution.py:247
  42.1 1.3 %spread.4 = bf16[512,256]{1,0:T(8,128)(2,1)S(1)} custom-call(bf16[272,256]{1,0:T(8,128)(2,1)S(1)} %get-tuple-element.10.refs_0_.refs_8_, bf16[272,256]{1,0:T(8,128)(2,1)S(1)} %collective-permute-done.refs_1_.refs_9_, bf16[272,256]{1,0:T(8,128)(2,1)S(1)} %collective-permute-done.1.refs_2_.refs_10_, ...), custom_call_target="tpu_custom_call" | custom-call | tf_op jit(solution)/shard_map/spread/pallas_call | solution.py:182
  43.4 1.3 %spread.6 = bf16[512,256]{1,0:T(8,128)(2,1)S(1)} custom-call(bf16[272,256]{1,0:T(8,128)(2,1)S(1)} %get-tuple-element.14.refs_0_.refs_8_, bf16[272,256]{1,0:T(8,128)(2,1)S(1)} %collective-permute-done.16.refs_1_.refs_9_, bf16[272,256]{1,0:T(8,128)(2,1)S(1)} %collective-permute-done.17.refs_2_.refs_10_, ...), custom_call_target="tpu_custom_call" | custom-call | tf_op jit(solution)/shard_map/spread/pallas_call | solution.py:182
  44.8 2.7 %collective-permute-start.8 = (bf16[256,256]{1,0:T(8,128)(2,1)S(1)}, bf16[256,256]{1,0:T(8,128)(2,1)S(1)}, u32[]{:S(2)}, u32[]{:S(2)}) collective-permute-start(bf16[256,256]{1,0:T(8,128)(2,1)S(1)} %slice.51), channel_id=1, source_target_pairs={{0,4},{1,5},{2,6},{3,7},{4,0},{5,1},{6,2},{7,3},{8,12},{9,13},{10,... | collective-permute-start | bytes 393224 | tf_op jit(solution)/shard_map/ppermute | solution.py:247
  47.4 4.1 %collective-permute-done.23 = bf16[512,256]{1,0:T(8,128)(2,1)S(1)} collective-permute-done((bf16[512,256]{1,0:T(8,128)(2,1)S(1)}, bf16[512,256]{1,0:T(8,128)(2,1)S(1)}, u32[]{:S(2)}, u32[]{:S(2)}) %collective-permute-start.23) | collective-permute-done | bytes 262176 | tf_op jit(solution)/shard_map/ppermute | solution.py:247
  52.5 2.2 %collective-permute-start.11 = (bf16[128,256]{1,0:T(8,128)(2,1)S(1)}, bf16[128,256]{1,0:T(8,128)(2,1)S(1)}, u32[]{:S(2)}, u32[]{:S(2)}) collective-permute-start(bf16[128,256]{1,0:T(8,128)(2,1)S(1)} %get-tuple-element.20), channel_id=1, source_target_pairs={{0,17},{1,16},{2,19},{3,18},{4,21},{5,20},{6,23},{7,22},{8,25},{9,... | collective-permute-start | bytes 196616 | tf_op jit(solution)/shard_map/ppermute | solution.py:236
  56.1 3.4 %collective-permute-done.24 = bf16[256,256]{1,0:T(8,128)(2,1)S(1)} collective-permute-done((bf16[256,256]{1,0:T(8,128)(2,1)S(1)}, bf16[256,256]{1,0:T(8,128)(2,1)S(1)}, u32[]{:S(2)}, u32[]{:S(2)}) %collective-permute-start.24) | collective-permute-done | bytes 131104 | tf_op jit(solution)/shard_map/ppermute | solution.py:247
  59.5 2.6 %collective-permute-start.27 = (bf16[128,256]{1,0:T(8,128)(2,1)S(1)}, bf16[128,256]{1,0:T(8,128)(2,1)S(1)}, u32[]{:S(2)}, u32[]{:S(2)}) collective-permute-start(bf16[128,256]{1,0:T(8,128)(2,1)S(1)} %get-tuple-element.18), channel_id=1, source_target_pairs={{0,17},{1,16},{2,19},{3,18},{4,21},{5,20},{6,23},{7,22},{8,25},{9,... | collective-permute-start | bytes 196616 | tf_op jit(solution)/shard_map/ppermute | solution.py:236
  63.6 1.8 %collective-permute-done.27 = bf16[128,256]{1,0:T(8,128)(2,1)S(1)} collective-permute-done((bf16[128,256]{1,0:T(8,128)(2,1)S(1)}, bf16[128,256]{1,0:T(8,128)(2,1)S(1)}, u32[]{:S(2)}, u32[]{:S(2)}) %collective-permute-start.27) | collective-permute-done | bytes 65568 | tf_op jit(solution)/shard_map/ppermute | solution.py:236
  65.4 0.9 %collective-permute-done.25 = bf16[128,256]{1,0:T(8,128)(2,1)S(1)} collective-permute-done((bf16[128,256]{1,0:T(8,128)(2,1)S(1)}, bf16[128,256]{1,0:T(8,128)(2,1)S(1)}, u32[]{:S(2)}, u32[]{:S(2)}) %collective-permute-start.25) | collective-permute-done | bytes 65568 | tf_op jit(solution)/shard_map/ppermute | solution.py:236
  (56 shorter events, 8.9 us)
Async XLA Ops:
  8.6 7.1 %collective-permute-start = (bf16[272,256]{1,0:T(8,128)(2,1)S(1)}, bf16[272,256]{1,0:T(8,128)(2,1)S(1)}, u32[]{:S(2)}, u32[]{:S(2)}) collective-permute-start(bf16[272,256]{1,0:T(8,128)(2,1)S(1)} %get-tuple-element.11), channel_id=1, source_target_pairs={{0,1},{1,0},{2,3},{3,2},{4,5},{5,4},{6,7},{7,6},{8,9},{9,8},{10,11... | collective-permute-start | bytes 417800 | tf_op jit(solution)/shard_map/ppermute | solution.py:236
  11.6 8.1 %collective-permute-start.1 = (bf16[272,256]{1,0:T(8,128)(2,1)S(1)}, bf16[272,256]{1,0:T(8,128)(2,1)S(1)}, u32[]{:S(2)}, u32[]{:S(2)}) collective-permute-start(bf16[272,256]{1,0:T(8,128)(2,1)S(1)} %get-tuple-element.12), channel_id=1, source_target_pairs={{0,16},{1,17},{2,18},{3,19},{4,20},{5,21},{6,22},{7,23},{8,24},{9,... | collective-permute-start | bytes 417800 | tf_op jit(solution)/shard_map/ppermute | solution.py:236
  13.2 6.6 %collective-permute-start.2 = (bf16[272,256]{1,0:T(8,128)(2,1)S(1)}, bf16[272,256]{1,0:T(8,128)(2,1)S(1)}, u32[]{:S(2)}, u32[]{:S(2)}) collective-permute-start(bf16[272,256]{1,0:T(8,128)(2,1)S(1)} %get-tuple-element.13), channel_id=1, source_target_pairs={{0,17},{1,16},{2,19},{3,18},{4,21},{5,20},{6,23},{7,22},{8,25},{9,... | collective-permute-start | bytes 417800 | tf_op jit(solution)/shard_map/ppermute | solution.py:236
  13.2 15.9 %collective-permute-start.3 = (bf16[272,256]{1,0:T(8,128)(2,1)S(1)}, bf16[272,256]{1,0:T(8,128)(2,1)S(1)}, u32[]{:S(2)}, u32[]{:S(2)}) collective-permute-start(bf16[272,256]{1,0:T(8,128)(2,1)S(1)} %get-tuple-element.10.refs_0_.refs_8_), channel_id=1, source_target_pairs={{0,8},{1,9},{2,10},{3,11},{4,12},{5,13},{6,14},{7,15},{8,0},{9,1},... | collective-permute-start | bytes 417800 | tf_op jit(solution)/shard_map/ppermute | solution.py:237
  15.7 14.7 %collective-permute-start.4 = (bf16[272,256]{1,0:T(8,128)(2,1)S(1)}, bf16[272,256]{1,0:T(8,128)(2,1)S(1)}, u32[]{:S(2)}, u32[]{:S(2)}) collective-permute-start(bf16[272,256]{1,0:T(8,128)(2,1)S(1)} %collective-permute-done.refs_1_.refs_9_), channel_id=1, source_target_pairs={{0,8},{1,9},{2,10},{3,11},{4,12},{5,13},{6,14},{7,15},{8,0},{9,1},... | collective-permute-start | bytes 417800 | tf_op jit(solution)/shard_map/ppermute | solution.py:237
  19.8 12.1 %collective-permute-start.5 = (bf16[272,256]{1,0:T(8,128)(2,1)S(1)}, bf16[272,256]{1,0:T(8,128)(2,1)S(1)}, u32[]{:S(2)}, u32[]{:S(2)}) collective-permute-start(bf16[272,256]{1,0:T(8,128)(2,1)S(1)} %collective-permute-done.1.refs_2_.refs_10_), channel_id=1, source_target_pairs={{0,8},{1,9},{2,10},{3,11},{4,12},{5,13},{6,14},{7,15},{8,0},{9,1},... | collective-permute-start | bytes 417800 | tf_op jit(solution)/shard_map/ppermute | solution.py:237
  19.8 12.1 %collective-permute-start.6 = (bf16[272,256]{1,0:T(8,128)(2,1)S(1)}, bf16[272,256]{1,0:T(8,128)(2,1)S(1)}, u32[]{:S(2)}, u32[]{:S(2)}) collective-permute-start(bf16[272,256]{1,0:T(8,128)(2,1)S(1)} %collective-permute-done.2.refs_3_.refs_11_), channel_id=1, source_target_pairs={{0,8},{1,9},{2,10},{3,11},{4,12},{5,13},{6,14},{7,15},{8,0},{9,1},... | collective-permute-start | bytes 417800 | tf_op jit(solution)/shard_map/ppermute | solution.py:237
  28.3 6.5 %collective-permute-start.16 = (bf16[272,256]{1,0:T(8,128)(2,1)S(1)}, bf16[272,256]{1,0:T(8,128)(2,1)S(1)}, u32[]{:S(2)}, u32[]{:S(2)}) collective-permute-start(bf16[272,256]{1,0:T(8,128)(2,1)S(1)} %get-tuple-element.15), channel_id=1, source_target_pairs={{0,1},{1,0},{2,3},{3,2},{4,5},{5,4},{6,7},{7,6},{8,9},{9,8},{10,11... | collective-permute-start | bytes 417800 | tf_op jit(solution)/shard_map/ppermute | solution.py:236
  29.1 7.2 %collective-permute-start.17 = (bf16[272,256]{1,0:T(8,128)(2,1)S(1)}, bf16[272,256]{1,0:T(8,128)(2,1)S(1)}, u32[]{:S(2)}, u32[]{:S(2)}) collective-permute-start(bf16[272,256]{1,0:T(8,128)(2,1)S(1)} %get-tuple-element.16), channel_id=1, source_target_pairs={{0,16},{1,17},{2,18},{3,19},{4,20},{5,21},{6,22},{7,23},{8,24},{9,... | collective-permute-start | bytes 417800 | tf_op jit(solution)/shard_map/ppermute | solution.py:236
  30.4 7.5 %collective-permute-start.18 = (bf16[272,256]{1,0:T(8,128)(2,1)S(1)}, bf16[272,256]{1,0:T(8,128)(2,1)S(1)}, u32[]{:S(2)}, u32[]{:S(2)}) collective-permute-start(bf16[272,256]{1,0:T(8,128)(2,1)S(1)} %get-tuple-element.17), channel_id=1, source_target_pairs={{0,17},{1,16},{2,19},{3,18},{4,21},{5,20},{6,23},{7,22},{8,25},{9,... | collective-permute-start | bytes 417800 | tf_op jit(solution)/shard_map/ppermute | solution.py:236
  33.1 11.5 %collective-permute-start.7 = (bf16[512,256]{1,0:T(8,128)(2,1)S(1)}, bf16[512,256]{1,0:T(8,128)(2,1)S(1)}, u32[]{:S(2)}, u32[]{:S(2)}) collective-permute-start(bf16[512,256]{1,0:T(8,128)(2,1)S(1)} %spread.5), channel_id=1, source_target_pairs={{0,2},{1,3},{2,0},{3,1},{4,6},{5,7},{6,4},{7,5},{8,10},{9,11},{10,... | collective-permute-start | bytes 786440 | tf_op jit(solution)/shard_map/ppermute | solution.py:247
  34.8 3.1 %collective-permute-start.19 = (bf16[272,256]{1,0:T(8,128)(2,1)S(1)}, bf16[272,256]{1,0:T(8,128)(2,1)S(1)}, u32[]{:S(2)}, u32[]{:S(2)}) collective-permute-start(bf16[272,256]{1,0:T(8,128)(2,1)S(1)} %get-tuple-element.14.refs_0_.refs_8_), channel_id=1, source_target_pairs={{0,8},{1,9},{2,10},{3,11},{4,12},{5,13},{6,14},{7,15},{8,0},{9,1},... | collective-permute-start | bytes 417800 | tf_op jit(solution)/shard_map/ppermute | solution.py:237
  40.5 11.0 %collective-permute-start.23 = (bf16[512,256]{1,0:T(8,128)(2,1)S(1)}, bf16[512,256]{1,0:T(8,128)(2,1)S(1)}, u32[]{:S(2)}, u32[]{:S(2)}) collective-permute-start(bf16[512,256]{1,0:T(8,128)(2,1)S(1)} %spread.7), channel_id=1, source_target_pairs={{0,2},{1,3},{2,0},{3,1},{4,6},{5,7},{6,4},{7,5},{8,10},{9,11},{10,... | collective-permute-start | bytes 786440 | tf_op jit(solution)/shard_map/ppermute | solution.py:247
  44.8 7.7 %collective-permute-start.8 = (bf16[256,256]{1,0:T(8,128)(2,1)S(1)}, bf16[256,256]{1,0:T(8,128)(2,1)S(1)}, u32[]{:S(2)}, u32[]{:S(2)}) collective-permute-start(bf16[256,256]{1,0:T(8,128)(2,1)S(1)} %slice.51), channel_id=1, source_target_pairs={{0,4},{1,5},{2,6},{3,7},{4,0},{5,1},{6,2},{7,3},{8,12},{9,13},{10,... | collective-permute-start | bytes 393224 | tf_op jit(solution)/shard_map/ppermute | solution.py:247
  51.6 7.8 %collective-permute-start.24 = (bf16[256,256]{1,0:T(8,128)(2,1)S(1)}, bf16[256,256]{1,0:T(8,128)(2,1)S(1)}, u32[]{:S(2)}, u32[]{:S(2)}) collective-permute-start(bf16[256,256]{1,0:T(8,128)(2,1)S(1)} %slice.50), channel_id=1, source_target_pairs={{0,4},{1,5},{2,6},{3,7},{4,0},{5,1},{6,2},{7,3},{8,12},{9,13},{10,... | collective-permute-start | bytes 393224 | tf_op jit(solution)/shard_map/ppermute | solution.py:247
  52.5 9.6 %collective-permute-start.11 = (bf16[128,256]{1,0:T(8,128)(2,1)S(1)}, bf16[128,256]{1,0:T(8,128)(2,1)S(1)}, u32[]{:S(2)}, u32[]{:S(2)}) collective-permute-start(bf16[128,256]{1,0:T(8,128)(2,1)S(1)} %get-tuple-element.20), channel_id=1, source_target_pairs={{0,17},{1,16},{2,19},{3,18},{4,21},{5,20},{6,23},{7,22},{8,25},{9,... | collective-permute-start | bytes 196616 | tf_op jit(solution)/shard_map/ppermute | solution.py:236
  54.7 7.9 %collective-permute-start.9 = (bf16[128,256]{1,0:T(8,128)(2,1)S(1)}, bf16[128,256]{1,0:T(8,128)(2,1)S(1)}, u32[]{:S(2)}, u32[]{:S(2)}) collective-permute-start(bf16[128,256]{1,0:T(8,128)(2,1)S(1)} %get-tuple-element.20), channel_id=1, source_target_pairs={{0,1},{1,0},{2,3},{3,2},{4,5},{5,4},{6,7},{7,6},{8,9},{9,8},{10,11... | collective-permute-start | bytes 196616 | tf_op jit(solution)/shard_map/ppermute | solution.py:236
  55.3 7.8 %collective-permute-start.12 = (bf16[128,256]{1,0:T(8,128)(2,1)S(1)}, bf16[128,256]{1,0:T(8,128)(2,1)S(1)}, u32[]{:S(2)}, u32[]{:S(2)}) collective-permute-start(bf16[128,256]{1,0:T(8,128)(2,1)S(1)} %get-tuple-element.21), channel_id=1, source_target_pairs={{0,8},{1,9},{2,10},{3,11},{4,12},{5,13},{6,14},{7,15},{8,0},{9,1},... | collective-permute-start | bytes 196616 | tf_op jit(solution)/shard_map/ppermute | solution.py:237
  55.3 7.8 %collective-permute-start.10 = (bf16[128,256]{1,0:T(8,128)(2,1)S(1)}, bf16[128,256]{1,0:T(8,128)(2,1)S(1)}, u32[]{:S(2)}, u32[]{:S(2)}) collective-permute-start(bf16[128,256]{1,0:T(8,128)(2,1)S(1)} %get-tuple-element.21), channel_id=1, source_target_pairs={{0,16},{1,17},{2,18},{3,19},{4,20},{5,21},{6,22},{7,23},{8,24},{9,... | collective-permute-start | bytes 196616 | tf_op jit(solution)/shard_map/ppermute | solution.py:236
  59.5 5.9 %collective-permute-start.27 = (bf16[128,256]{1,0:T(8,128)(2,1)S(1)}, bf16[128,256]{1,0:T(8,128)(2,1)S(1)}, u32[]{:S(2)}, u32[]{:S(2)}) collective-permute-start(bf16[128,256]{1,0:T(8,128)(2,1)S(1)} %get-tuple-element.18), channel_id=1, source_target_pairs={{0,17},{1,16},{2,19},{3,18},{4,21},{5,20},{6,23},{7,22},{8,25},{9,... | collective-permute-start | bytes 196616 | tf_op jit(solution)/shard_map/ppermute | solution.py:236
  62.1 4.3 %collective-permute-start.25 = (bf16[128,256]{1,0:T(8,128)(2,1)S(1)}, bf16[128,256]{1,0:T(8,128)(2,1)S(1)}, u32[]{:S(2)}, u32[]{:S(2)}) collective-permute-start(bf16[128,256]{1,0:T(8,128)(2,1)S(1)} %get-tuple-element.18), channel_id=1, source_target_pairs={{0,1},{1,0},{2,3},{3,2},{4,5},{5,4},{6,7},{7,6},{8,9},{9,8},{10,11... | collective-permute-start | bytes 196616 | tf_op jit(solution)/shard_map/ppermute | solution.py:236
  62.7 4.3 %collective-permute-start.26 = (bf16[128,256]{1,0:T(8,128)(2,1)S(1)}, bf16[128,256]{1,0:T(8,128)(2,1)S(1)}, u32[]{:S(2)}, u32[]{:S(2)}) collective-permute-start(bf16[128,256]{1,0:T(8,128)(2,1)S(1)} %get-tuple-element.19), channel_id=1, source_target_pairs={{0,16},{1,17},{2,18},{3,19},{4,20},{5,21},{6,22},{7,23},{8,24},{9,... | collective-permute-start | bytes 196616 | tf_op jit(solution)/shard_map/ppermute | solution.py:236
  63.1 3.8 %collective-permute-start.15 = (bf16[128,256]{1,0:T(8,128)(2,1)S(1)}, bf16[128,256]{1,0:T(8,128)(2,1)S(1)}, u32[]{:S(2)}, u32[]{:S(2)}) collective-permute-start(bf16[128,256]{1,0:T(8,128)(2,1)S(1)} %collective-permute-done.11), channel_id=1, source_target_pairs={{0,8},{1,9},{2,10},{3,11},{4,12},{5,13},{6,14},{7,15},{8,0},{9,1},... | collective-permute-start | bytes 196616 | tf_op jit(solution)/shard_map/ppermute | solution.py:237
  63.1 4.3 %collective-permute-start.13 = (bf16[128,256]{1,0:T(8,128)(2,1)S(1)}, bf16[128,256]{1,0:T(8,128)(2,1)S(1)}, u32[]{:S(2)}, u32[]{:S(2)}) collective-permute-start(bf16[128,256]{1,0:T(8,128)(2,1)S(1)} %collective-permute-done.9), channel_id=1, source_target_pairs={{0,8},{1,9},{2,10},{3,11},{4,12},{5,13},{6,14},{7,15},{8,0},{9,1},... | collective-permute-start | bytes 196616 | tf_op jit(solution)/shard_map/ppermute | solution.py:237
  (8 other events, 14.3 us)

commit v3 on v2

v3 whole, which is shorter than its diff:
```python
import functools

import jax
import jax.numpy as jnp
from jax import lax
from jax.experimental import pallas as pl
from jax.experimental.pallas import tpu as pltpu
from jax.sharding import PartitionSpec as P

VMEM_LIMIT = 16 * 1024 * 1024
LABEL_ROWS = 16
AXES = ("op", "sec")


class Plan:
    def __init__(self, mesh, psi, terms):
        self.op, self.sec = mesh.shape["op"], mesh.shape["sec"]
        self.held, self.blk = psi.shape[0], psi.shape[1]
        self.terms = terms
        self.slots = self.sec // 2
        self.extra = 0
        while self.slots * self.op * 2**self.extra < self.held * self.sec:
            self.extra += 1
        self.places = (self.op // 2) * 2**self.extra
        self.rows = self.blk // (2 * self.places)
        self.step, self.window = 2, 6
        self.bits = list(range(self.extra, self.sec.bit_length() - 1))

    def place(self, op, sec):
        return (op // 2) * 2**self.extra + sec % 2**self.extra

    def swap(self, op_mask, sec_mask):
        n = self.op * self.sec
        mask = op_mask * self.sec + sec_mask
        return [(i, i ^ mask) for i in range(n)]

    def across(self, m):
        return self.swap((m >> self.extra) << 1, m & (2**self.extra - 1))


def contract_kernel(plan, fetch, *refs):
    source, target, left, right, vector = refs[:5]
    outs, refs = refs[5 : 5 + plan.places], refs[5 + plan.places :]
    if fetch:
        lhs, rhs, refs = refs[0], refs[1], refs[2:]
    else:
        lhs, rhs = left, right
    src, tgt, psi, acc, slot_of, labels, seen, sems, first_sems = refs
    blk, terms, step = plan.blk, plan.terms, plan.step
    chunks = terms // step if fetch else 0

    heads = [
        pltpu.make_async_copy(x, y, first_sems.at[i])
        for i, (x, y) in enumerate(((target, tgt), (source, src), (vector, psi)))
    ]
    for copy in heads:
        copy.start()

    def loads(c):
        part = pl.ds(c * step, step)
        return [
            pltpu.make_async_copy(left.at[part], lhs.at[part], sems.at[0, c]),
            pltpu.make_async_copy(right.at[part], rhs.at[part], sems.at[1, c]),
        ]

    def begin(c):
        if c < chunks:
            for copy in loads(c):
                copy.start()

    for c in range(plan.window):
        begin(c)
    for h in range(plan.sec):
        seen[h] = -1
    acc[...] = jnp.zeros_like(acc)
    heads[0].wait()

    def name(t, count):
        goal = tgt[t]
        holder = goal // plan.held
        fresh = seen[holder] < 0
        slot = jnp.where(fresh, count, seen[holder])
        seen[holder] = slot
        labels[slot] = goal
        slot_of[t] = slot
        return count + fresh.astype(jnp.int32)

    lax.fori_loop(0, terms, name, jnp.int32(0))
    for copy in heads[1:]:
        copy.wait()

    for t in range(terms):
        if fetch and t % step == 0:
            for copy in loads(t // step):
                copy.wait()
            begin(t // step + plan.window)
        half = jnp.dot(lhs[t], psi[src[t]], preferred_element_type=jnp.float32).astype(jnp.bfloat16)
        acc[slot_of[t]] += lax.dot_general(
            half, rhs[t], (((1,), (1,)), ((), ())), preferred_element_type=jnp.float32
        )

    op, sec = lax.axis_index("op"), lax.axis_index("sec")
    core, place = op % 2, plan.place(op, sec)
    lane = lax.broadcasted_iota(jnp.int32, (LABEL_ROWS, blk), 1)
    tile = jnp.zeros((LABEL_ROWS, blk), jnp.float32)
    for j in range(plan.slots):
        tile = jnp.where(lane == j, labels[j].astype(jnp.float32), tile)
    tile = tile.astype(jnp.bfloat16)
    for m in range(plan.places):
        for rc in range(2):
            row = pl.multiple_of(((place ^ m) * 2 + (core ^ rc)) * plan.rows, plan.rows)
            for j in range(plan.slots):
                to = (rc * plan.slots + j) * plan.rows
                outs[m][pl.ds(to, plan.rows), :] = acc[j, pl.ds(row, plan.rows), :].astype(jnp.bfloat16)
        outs[m][pl.ds(2 * plan.slots * plan.rows, LABEL_ROWS), :] = tile


def contract(plan, fetch, source, target, left, right, vector):
    blk, terms = plan.blk, plan.terms
    height = 2 * plan.slots * plan.rows + LABEL_ROWS
    bf16 = jnp.bfloat16
    spaces = [pltpu.HBM, pltpu.HBM, *[pltpu.HBM if fetch else pltpu.VMEM] * 2, pltpu.HBM]
    arrays = [
        pltpu.with_memory_space_constraint(x, space)
        for x, space in zip((source, target, left, right, vector), spaces)
    ]
    out_shape = [pltpu.VMEM((height, blk), bf16)] * plan.places
    if fetch:
        out_shape += [pltpu.VMEM((terms, blk, blk), bf16)] * 2
    return pl.pallas_call(
        functools.partial(contract_kernel, plan, fetch),
        in_specs=[pl.BlockSpec(memory_space=space) for space in spaces],
        out_specs=[pl.BlockSpec(memory_space=pltpu.VMEM)] * len(out_shape),
        out_shape=out_shape,
        scratch_shapes=[
            pltpu.SMEM((terms,), jnp.int32),
            pltpu.SMEM((terms,), jnp.int32),
            pltpu.VMEM((plan.held, blk, blk), bf16),
            pltpu.VMEM((plan.slots, blk, blk), jnp.float32),
            pltpu.SMEM((terms,), jnp.int32),
            pltpu.SMEM((plan.slots,), jnp.int32),
            pltpu.SMEM((plan.sec,), jnp.int32),
            pltpu.SemaphoreType.DMA((2, terms // plan.step)),
            pltpu.SemaphoreType.DMA((3,)),
        ],
        cost_estimate=pl.CostEstimate(
            flops=4 * terms * blk**3,
            bytes_accessed=4 * terms * blk * blk if fetch else terms * blk,
            transcendentals=0,
        ),
        compiler_params=pltpu.CompilerParams(vmem_limit_bytes=VMEM_LIMIT),
        name="contract",
    )(*arrays)


def spread_kernel(plan, *refs):
    n = 2 * plan.places
    blocks, tags, outs = refs[:n], refs[n : 2 * n], refs[2 * n : 2 * n + 2]
    acc, tags_vector, tags_scalar, sem = refs[2 * n + 2 :]
    for i in range(n):
        row = jnp.max(tags[i][...].astype(jnp.float32), axis=0, keepdims=True)
        tags_vector[pl.ds(i, 1), :] = row[:, :128].astype(jnp.int32)
    copy = pltpu.make_async_copy(tags_vector, tags_scalar, sem)
    copy.start()
    acc[...] = jnp.zeros_like(acc)
    copy.wait()
    sec = lax.axis_index("sec")
    for i in range(n):
        for j in range(plan.slots):
            label = tags_scalar[i, j]
            away = (label // plan.held) ^ sec
            index = jnp.int32(0)
            for b in plan.bits:
                index = index * 2 + ((away >> b) & 1)
            index = index * 2**plan.extra + (away & (2**plan.extra - 1))
            acc[index * plan.held + label % plan.held] += blocks[i][pl.ds(j * plan.rows, plan.rows), :].astype(jnp.float32)
    half = acc.shape[0] // 2
    for k, out in enumerate(outs):
        out[...] = acc[pl.ds((1 - k) * half, half)].astype(jnp.bfloat16).reshape(out.shape)


def spread(plan, own, other):
    blk, rows, slots = plan.blk, plan.rows, plan.slots
    sectors = plan.held * 2 ** (plan.extra + len(plan.bits))
    n = 2 * plan.places

    def half(rc):
        return pl.BlockSpec((slots * rows, blk), lambda t: (rc, 0))

    tag = pl.BlockSpec((LABEL_ROWS, blk), lambda t: (2 * slots * rows // LABEL_ROWS, 0))
    height = sectors // 2 * rows
    return pl.pallas_call(
        functools.partial(spread_kernel, plan),
        grid=(1,),
        in_specs=[half(0)] * plan.places + [half(1)] * plan.places + [tag] * n,
        out_specs=[pl.BlockSpec((height, blk), lambda t: (0, 0))] * 2,
        out_shape=[jax.ShapeDtypeStruct((height, blk), jnp.bfloat16)] * 2,
        scratch_shapes=[
            pltpu.VMEM((sectors, rows, blk), jnp.float32),
            pltpu.VMEM((n, 128), jnp.int32),
            pltpu.SMEM((n, 128), jnp.int32),
            pltpu.SemaphoreType.DMA,
        ],
        compiler_params=pltpu.CompilerParams(vmem_limit_bytes=VMEM_LIMIT),
        name="spread",
    )(*own, *other, *own, *other)


def place_kernel(plan, *refs):
    n = 2 * plan.places
    pieces, out, sems = refs[:n], refs[n], refs[n + 1]
    op, sec = lax.axis_index("op"), lax.axis_index("sec")
    core, place = op % 2, plan.place(op, sec)
    moving = []
    for i, piece in enumerate(pieces):
        rc, m = divmod(i, plan.places)
        row = pl.multiple_of(((place ^ m) * 2 + (core ^ rc)) * plan.rows, plan.rows)
        moving.append(pltpu.make_async_copy(piece, out.at[:, pl.ds(row, plan.rows), :], sems.at[i]))
    for copy in moving:
        copy.start()
    for copy in moving:
        copy.wait()


def assemble(plan, own, other):
    pieces = [
        pltpu.with_memory_space_constraint(x.reshape(plan.held, plan.rows, plan.blk), pltpu.VMEM)
        for x in (*own, *other)
    ]
    return pl.pallas_call(
        functools.partial(place_kernel, plan),
        in_specs=[pl.BlockSpec(memory_space=pltpu.VMEM)] * len(pieces),
        out_specs=pl.BlockSpec(memory_space=pl.ANY),
        out_shape=jax.ShapeDtypeStruct((plan.held, plan.blk, plan.blk), jnp.bfloat16),
        scratch_shapes=[pltpu.SemaphoreType.DMA((len(pieces),))],
        compiler_params=pltpu.CompilerParams(vmem_limit_bytes=VMEM_LIMIT),
        name="assemble",
    )(*pieces)


def across(plan, pieces):
    own = list(pieces)
    for m in reversed(range(1, plan.places)):
        own[m] = lax.ppermute(pieces[m], AXES, plan.across(m))
    return own


def to_core(plan, own):
    return [lax.ppermute(x, AXES, plan.swap(1, 0)) for x in own]


def combine(plan, own):
    away, kept = spread(plan, own, to_core(plan, own))
    total = kept.astype(jnp.float32)
    for k, b in enumerate(plan.bits):
        arrived = lax.ppermute(away, AXES, plan.swap(0, 1 << b))
        total = total + arrived.astype(jnp.float32)
        if k + 1 < len(plan.bits):
            middle = total.shape[0] // 2
            away = total[middle:].astype(jnp.bfloat16)
            total = total[:middle]
    total = total.astype(jnp.bfloat16)
    size = plan.held * plan.rows
    sums = [total[e * size : (e + 1) * size] for e in range(2**plan.extra)]
    own = across(plan, [sums[m % 2**plan.extra] for m in range(plan.places)])
    return assemble(plan, own, to_core(plan, own))


def per_device(mesh, first, second, left, right, source, target):
    plan = Plan(mesh, first, left.shape[0])
    *pieces, lhs, rhs = contract(plan, True, source, target, left, right, first)
    early = across(plan, pieces)
    pieces = contract(plan, False, source, target, lhs, rhs, second)
    early, pieces = lax.optimization_barrier((early, pieces))
    late = across(plan, pieces)
    return combine(plan, early), combine(plan, late)


def solution(mesh):
    in_specs = (
        P("sec", None, None),
        P("sec", None, None),
        P(AXES, None, None),
        P(AXES, None, None),
        P(AXES),
        P(AXES),
    )
    out_specs = (P("sec", None, None), P("sec", None, None))
    return jax.shard_map(
        functools.partial(per_device, mesh),
        mesh=mesh,
        in_specs=in_specs,
        out_specs=out_specs,
        check_vma=False,
    )
```

time: 69.7 us -> 66.9 us (0.960)
  Pallas kernels: 22.7 us -> 16.6 us
  waiting for transfers between devices: 21.6 us -> 27.3 us
  starting transfers between devices: 24.1 us -> 21.8 us
    pallas_call x8 -> x6, Pallas kernels: 22.7 us -> 16.6 us  [the longest x2 12.9 us: contract(): pl.pallas_call(functools.partial(contract_kernel, plan, fetch), in_specs=...]
    ppermute x4, waiting for transfers between devices: 7.49 us -> 12.4 us  [combine(): arrived = lax.ppermute(away, AXES, plan.swap(0, 1 << b))]
    ppermute x4, starting transfers between devices: 6.79 us -> 4.87 us  [combine(): arrived = lax.ppermute(away, AXES, plan.swap(0, 1 << b))]
    ppermute x28, waiting for transfers between devices: 14.1 us -> 14.9 us  [the longest x12 13.5 us: across(): own[m] = lax.ppermute(pieces[m], AXES, plan.across(m))]
  transfers between devices with their start and end apart: 32 -> 32, of which waited for: 11 -> 17; matrix products, arithmetic and copies ran while one was open for 0% -> 0% of each run, Pallas kernels for 20% -> 9%
where the time goes in v3:
time: 66.9 us; the launch traced here: 66.8 us
  waiting for transfers between devices  27.3 us (41%)
  starting transfers between devices  21.8 us (33%)
  Pallas kernels  16.6 us (25%)
  between operations  0.8 us (1%)
    ppermute x12, starting transfers between devices, across(): own[m] = lax.ppermute(pieces[m], AXES, plan.across(m))  15.1 us
    ppermute x12, waiting for transfers between devices, across(): own[m] = lax.ppermute(pieces[m], AXES, plan.across(m))  13.5 us
    pallas_call x2, Pallas kernels, contract(): pl.pallas_call(functools.partial(contract_kernel, plan, fetch), in_specs=...  12.9 us
    ppermute x4, waiting for transfers between devices, combine(): arrived = lax.ppermute(away, AXES, plan.swap(0, 1 << b))  12.4 us
    ppermute x4, starting transfers between devices, combine(): arrived = lax.ppermute(away, AXES, plan.swap(0, 1 << b))  4.87 us
    pallas_call x2, Pallas kernels, spread(): pl.pallas_call(functools.partial(spread_kernel, plan), grid=(1,), in_spec...  2.09 us
    ppermute x16, starting transfers between devices, to_core(): return [lax.ppermute(x, AXES, plan.swap(1, 0)) for x in own]  1.75 us
    pallas_call x2, Pallas kernels, assemble(): pl.pallas_call(functools.partial(place_kernel, plan), in_specs=[pl.BlockS...  1.7 us
  transfers between devices with their start and end apart: 32, of which 17 were waited for; matrix products, arithmetic and copies ran while one was open for 0% of the time, Pallas kernels for 9%

profile of v3, /device:TPU:0, one launch (start us, length us, event | category | flops | bytes accessed | tf_op | source)
XLA Modules:
  0.0 66.8 jit_solution(6493780211824021555)
XLA Ops:
  0.6 8.9 %contract.2 = (bf16[272,256]{1,0:T(8,128)(2,1)S(1)}, bf16[272,256]{1,0:T(8,128)(2,1)S(1)}, bf16[272,256]{1,0:T(8,128)(2,1)S(1)}, bf16[272,256]{1,0:T(8,128)(2,1)...) custom-call(s32[32]{0:T(128)} %refs_0_.3, s32[32]{0:T(128)} %refs_1_.3, ...), custom_call_target="tpu_custom_call" | custom-call | flops 2147483648 | bytes 8388608 | tf_op jit(solution)/shard_map/contract/pallas_call | solution.py:130
  9.5 3.0 %collective-permute-start = (bf16[272,256]{1,0:T(8,128)(2,1)S(1)}, bf16[272,256]{1,0:T(8,128)(2,1)S(1)}, u32[]{:S(2)}, u32[]{:S(2)}) collective-permute-start(bf16[272,256]{1,0:T(8,128)(2,1)S(1)} %get-tuple-element.25), channel_id=1, source_target_pairs={{0,1},{1,0},{2,3},{3,2},{4,5},{5,4},{6,7},{7,6},{8,9},{9,8},{10,11... | collective-permute-start | bytes 417800 | tf_op jit(solution)/shard_map/ppermute | solution.py:244
  12.5 1.5 %collective-permute-start.1 = (bf16[272,256]{1,0:T(8,128)(2,1)S(1)}, bf16[272,256]{1,0:T(8,128)(2,1)S(1)}, u32[]{:S(2)}, u32[]{:S(2)}) collective-permute-start(bf16[272,256]{1,0:T(8,128)(2,1)S(1)} %get-tuple-element.26), channel_id=1, source_target_pairs={{0,16},{1,17},{2,18},{3,19},{4,20},{5,21},{6,22},{7,23},{8,24},{9,... | collective-permute-start | bytes 417800 | tf_op jit(solution)/shard_map/ppermute | solution.py:244
  14.0 4.0 %contract.3 = (bf16[272,256]{1,0:T(8,128)(2,1)S(1)}, bf16[272,256]{1,0:T(8,128)(2,1)S(1)}, bf16[272,256]{1,0:T(8,128)(2,1)S(1)}, bf16[272,256]{1,0:T(8,128)(2,1)S(1)}) custom-call(s32[32]{0:T(128)} %refs_0_.3, s32[32]{0:T(128)} %refs_1_.3, bf16[32,256,256]{2,1,0:T(8,128)(2,1)S(1)} %get-tuple-element.28.refs_2_, ...), custom_call_target="tpu_custom_call" | custom-call | flops 2147483648 | bytes 8192 | tf_op jit(solution)/shard_map/contract/pallas_call | solution.py:130
  18.1 2.6 %collective-permute-done.1.refs_2_.refs_10_ = bf16[272,256]{1,0:T(8,128)(2,1)S(1)} collective-permute-done((bf16[272,256]{1,0:T(8,128)(2,1)S(1)}, bf16[272,256]{1,0:T(8,128)(2,1)S(1)}, u32[]{:S(2)}, u32[]{:S(2)}) %collective-permute-start.1) | collective-permute-done | bytes 139296 | tf_op jit(solution)/shard_map/ppermute | solution.py:244
  22.7 1.0 %spread.2 = (bf16[512,256]{1,0:T(8,128)(2,1)S(1)}, bf16[512,256]{1,0:T(8,128)(2,1)S(1)}) custom-call(bf16[272,256]{1,0:T(8,128)(2,1)S(1)} %get-tuple-element.34.refs_0_.refs_8_, bf16[272,256]{1,0:T(8,128)(2,1)S(1)} %collective-permute-done.refs_1_.refs_9_, bf16[272,256]{1,0:T(8,128)(2,1)S(1)} %collective-permute-done.1.refs_2_.refs_10_, ...), custom_call_target="tpu_custom_call" | custom-call | tf_op jit(solution)/shard_map/spread/pallas_call | solution.py:192
  23.7 1.6 %collective-permute-start.7 = (bf16[512,256]{1,0:T(8,128)(2,1)S(1)}, bf16[512,256]{1,0:T(8,128)(2,1)S(1)}, u32[]{:S(2)}, u32[]{:S(2)}) collective-permute-start(bf16[512,256]{1,0:T(8,128)(2,1)S(1)} %get-tuple-element.39), channel_id=1, source_target_pairs={{0,2},{1,3},{2,0},{3,1},{4,6},{5,7},{6,4},{7,5},{8,10},{9,11},{10,... | collective-permute-start | bytes 786440 | tf_op jit(solution)/shard_map/ppermute | solution.py:256
  25.4 1.2 %collective-permute-start.16 = (bf16[272,256]{1,0:T(8,128)(2,1)S(1)}, bf16[272,256]{1,0:T(8,128)(2,1)S(1)}, u32[]{:S(2)}, u32[]{:S(2)}) collective-permute-start(bf16[272,256]{1,0:T(8,128)(2,1)S(1)} %get-tuple-element.41), channel_id=1, source_target_pairs={{0,1},{1,0},{2,3},{3,2},{4,5},{5,4},{6,7},{7,6},{8,9},{9,8},{10,11... | collective-permute-start | bytes 417800 | tf_op jit(solution)/shard_map/ppermute | solution.py:244
  27.4 1.4 %collective-permute-start.18 = (bf16[272,256]{1,0:T(8,128)(2,1)S(1)}, bf16[272,256]{1,0:T(8,128)(2,1)S(1)}, u32[]{:S(2)}, u32[]{:S(2)}) collective-permute-start(bf16[272,256]{1,0:T(8,128)(2,1)S(1)} %get-tuple-element.43), channel_id=1, source_target_pairs={{0,17},{1,16},{2,19},{3,18},{4,21},{5,20},{6,23},{7,22},{8,25},{9,... | collective-permute-start | bytes 417800 | tf_op jit(solution)/shard_map/ppermute | solution.py:244
  28.9 2.9 %collective-permute-done.16.refs_1_.refs_9_ = bf16[272,256]{1,0:T(8,128)(2,1)S(1)} collective-permute-done((bf16[272,256]{1,0:T(8,128)(2,1)S(1)}, bf16[272,256]{1,0:T(8,128)(2,1)S(1)}, u32[]{:S(2)}, u32[]{:S(2)}) %collective-permute-start.16) | collective-permute-done | bytes 139296 | tf_op jit(solution)/shard_map/ppermute | solution.py:244
  31.8 1.5 %collective-permute-done.17.refs_2_.refs_10_ = bf16[272,256]{1,0:T(8,128)(2,1)S(1)} collective-permute-done((bf16[272,256]{1,0:T(8,128)(2,1)S(1)}, bf16[272,256]{1,0:T(8,128)(2,1)S(1)}, u32[]{:S(2)}, u32[]{:S(2)}) %collective-permute-start.17) | collective-permute-done | bytes 139296 | tf_op jit(solution)/shard_map/ppermute | solution.py:244
  33.3 1.6 %collective-permute-done.18.refs_3_.refs_11_ = bf16[272,256]{1,0:T(8,128)(2,1)S(1)} collective-permute-done((bf16[272,256]{1,0:T(8,128)(2,1)S(1)}, bf16[272,256]{1,0:T(8,128)(2,1)S(1)}, u32[]{:S(2)}, u32[]{:S(2)}) %collective-permute-start.18) | collective-permute-done | bytes 139296 | tf_op jit(solution)/shard_map/ppermute | solution.py:244
  35.0 2.7 %collective-permute-start.8 = (bf16[256,256]{1,0:T(8,128)(2,1)S(1)}, bf16[256,256]{1,0:T(8,128)(2,1)S(1)}, u32[]{:S(2)}, u32[]{:S(2)}) collective-permute-start(bf16[256,256]{1,0:T(8,128)(2,1)S(1)} %slice.51), channel_id=1, source_target_pairs={{0,4},{1,5},{2,6},{3,7},{4,0},{5,1},{6,2},{7,3},{8,12},{9,13},{10,... | collective-permute-start | bytes 393224 | tf_op jit(solution)/shard_map/ppermute | solution.py:256
  37.7 1.0 %spread.3 = (bf16[512,256]{1,0:T(8,128)(2,1)S(1)}, bf16[512,256]{1,0:T(8,128)(2,1)S(1)}) custom-call(bf16[272,256]{1,0:T(8,128)(2,1)S(1)} %get-tuple-element.40.refs_0_.refs_8_, bf16[272,256]{1,0:T(8,128)(2,1)S(1)} %collective-permute-done.16.refs_1_.refs_9_, bf16[272,256]{1,0:T(8,128)(2,1)S(1)} %collective-permute-done.17.refs_2_.refs_10_, ...), custom_call_target="tpu_custom_call" | custom-call | tf_op jit(solution)/shard_map/spread/pallas_call | solution.py:192
  39.3 5.4 %collective-permute-done.8 = bf16[256,256]{1,0:T(8,128)(2,1)S(1)} collective-permute-done((bf16[256,256]{1,0:T(8,128)(2,1)S(1)}, bf16[256,256]{1,0:T(8,128)(2,1)S(1)}, u32[]{:S(2)}, u32[]{:S(2)}) %collective-permute-start.8) | collective-permute-done | bytes 131104 | tf_op jit(solution)/shard_map/ppermute | solution.py:256
  44.7 5.2 %collective-permute-done.23 = bf16[512,256]{1,0:T(8,128)(2,1)S(1)} collective-permute-done((bf16[512,256]{1,0:T(8,128)(2,1)S(1)}, bf16[512,256]{1,0:T(8,128)(2,1)S(1)}, u32[]{:S(2)}, u32[]{:S(2)}) %collective-permute-start.23) | collective-permute-done | bytes 262176 | tf_op jit(solution)/shard_map/ppermute | solution.py:256
  50.1 1.8 %collective-permute-start.11 = (bf16[128,256]{1,0:T(8,128)(2,1)S(1)}, bf16[128,256]{1,0:T(8,128)(2,1)S(1)}, u32[]{:S(2)}, u32[]{:S(2)}) collective-permute-start(bf16[128,256]{1,0:T(8,128)(2,1)S(1)} %get-tuple-element.48), channel_id=1, source_target_pairs={{0,17},{1,16},{2,19},{3,18},{4,21},{5,20},{6,23},{7,22},{8,25},{9,... | collective-permute-start | bytes 196616 | tf_op jit(solution)/shard_map/ppermute | solution.py:244
  52.5 1.2 %collective-permute-start.10 = (bf16[128,256]{1,0:T(8,128)(2,1)S(1)}, bf16[128,256]{1,0:T(8,128)(2,1)S(1)}, u32[]{:S(2)}, u32[]{:S(2)}) collective-permute-start(bf16[128,256]{1,0:T(8,128)(2,1)S(1)} %get-tuple-element.49), channel_id=1, source_target_pairs={{0,16},{1,17},{2,18},{3,19},{4,20},{5,21},{6,22},{7,23},{8,24},{9,... | collective-permute-start | bytes 196616 | tf_op jit(solution)/shard_map/ppermute | solution.py:244
  53.7 1.9 %collective-permute-done.11 = bf16[128,256]{1,0:T(8,128)(2,1)S(1)} collective-permute-done((bf16[128,256]{1,0:T(8,128)(2,1)S(1)}, bf16[128,256]{1,0:T(8,128)(2,1)S(1)}, u32[]{:S(2)}, u32[]{:S(2)}) %collective-permute-start.11) | collective-permute-done | bytes 65568 | tf_op jit(solution)/shard_map/ppermute | solution.py:244
  56.2 1.8 %collective-permute-done.24 = bf16[256,256]{1,0:T(8,128)(2,1)S(1)} collective-permute-done((bf16[256,256]{1,0:T(8,128)(2,1)S(1)}, bf16[256,256]{1,0:T(8,128)(2,1)S(1)}, u32[]{:S(2)}, u32[]{:S(2)}) %collective-permute-start.24) | collective-permute-done | bytes 131104 | tf_op jit(solution)/shard_map/ppermute | solution.py:256
  58.1 1.8 %collective-permute-start.27 = (bf16[128,256]{1,0:T(8,128)(2,1)S(1)}, bf16[128,256]{1,0:T(8,128)(2,1)S(1)}, u32[]{:S(2)}, u32[]{:S(2)}) collective-permute-start(bf16[128,256]{1,0:T(8,128)(2,1)S(1)} %get-tuple-element.46), channel_id=1, source_target_pairs={{0,17},{1,16},{2,19},{3,18},{4,21},{5,20},{6,23},{7,22},{8,25},{9,... | collective-permute-start | bytes 196616 | tf_op jit(solution)/shard_map/ppermute | solution.py:244
  60.4 1.2 %collective-permute-start.26 = (bf16[128,256]{1,0:T(8,128)(2,1)S(1)}, bf16[128,256]{1,0:T(8,128)(2,1)S(1)}, u32[]{:S(2)}, u32[]{:S(2)}) collective-permute-start(bf16[128,256]{1,0:T(8,128)(2,1)S(1)} %get-tuple-element.47), channel_id=1, source_target_pairs={{0,16},{1,17},{2,18},{3,19},{4,20},{5,21},{6,22},{7,23},{8,24},{9,... | collective-permute-start | bytes 196616 | tf_op jit(solution)/shard_map/ppermute | solution.py:244
  62.1 1.6 %collective-permute-done.27 = bf16[128,256]{1,0:T(8,128)(2,1)S(1)} collective-permute-done((bf16[128,256]{1,0:T(8,128)(2,1)S(1)}, bf16[128,256]{1,0:T(8,128)(2,1)S(1)}, u32[]{:S(2)}, u32[]{:S(2)}) %collective-permute-start.27) | collective-permute-done | bytes 65568 | tf_op jit(solution)/shard_map/ppermute | solution.py:244
  64.7 0.8 %assemble.2 = bf16[4,256,256]{2,1,0:T(8,128)(2,1)} custom-call(bf16[4,32,256]{2,1,0:T(8,128)(2,1)S(1)} %bitcast.16, bf16[4,32,256]{2,1,0:T(8,128)(2,1)S(1)} %bitcast.19, bf16[4,32,256]{2,1,0:T(8,128)(2,1)S(1)} %bitcast.21, bf16[4,32,256]{2,1,0:T(8,128)(2,1)S(1)} %bitcast.18, bf16[4,32,256]{2,1,0:T(8,128)(2,1)S(1)} %bitcast.20, ...), custom_call_target="tpu_custom_call" | custom-call | tf_op jit(solution)/shard_map/assemble/pallas_call | solution.py:230
  (54 shorter events, 8.1 us)
Async XLA Ops:
  9.5 8.6 %collective-permute-start = (bf16[272,256]{1,0:T(8,128)(2,1)S(1)}, bf16[272,256]{1,0:T(8,128)(2,1)S(1)}, u32[]{:S(2)}, u32[]{:S(2)}) collective-permute-start(bf16[272,256]{1,0:T(8,128)(2,1)S(1)} %get-tuple-element.25), channel_id=1, source_target_pairs={{0,1},{1,0},{2,3},{3,2},{4,5},{5,4},{6,7},{7,6},{8,9},{9,8},{10,11... | collective-permute-start | bytes 417800 | tf_op jit(solution)/shard_map/ppermute | solution.py:244
  12.5 8.1 %collective-permute-start.1 = (bf16[272,256]{1,0:T(8,128)(2,1)S(1)}, bf16[272,256]{1,0:T(8,128)(2,1)S(1)}, u32[]{:S(2)}, u32[]{:S(2)}) collective-permute-start(bf16[272,256]{1,0:T(8,128)(2,1)S(1)} %get-tuple-element.26), channel_id=1, source_target_pairs={{0,16},{1,17},{2,18},{3,19},{4,20},{5,21},{6,22},{7,23},{8,24},{9,... | collective-permute-start | bytes 417800 | tf_op jit(solution)/shard_map/ppermute | solution.py:244
  14.0 6.6 %collective-permute-start.2 = (bf16[272,256]{1,0:T(8,128)(2,1)S(1)}, bf16[272,256]{1,0:T(8,128)(2,1)S(1)}, u32[]{:S(2)}, u32[]{:S(2)}) collective-permute-start(bf16[272,256]{1,0:T(8,128)(2,1)S(1)} %get-tuple-element.27), channel_id=1, source_target_pairs={{0,17},{1,16},{2,19},{3,18},{4,21},{5,20},{6,23},{7,22},{8,25},{9,... | collective-permute-start | bytes 417800 | tf_op jit(solution)/shard_map/ppermute | solution.py:244
  23.7 11.2 %collective-permute-start.7 = (bf16[512,256]{1,0:T(8,128)(2,1)S(1)}, bf16[512,256]{1,0:T(8,128)(2,1)S(1)}, u32[]{:S(2)}, u32[]{:S(2)}) collective-permute-start(bf16[512,256]{1,0:T(8,128)(2,1)S(1)} %get-tuple-element.39), channel_id=1, source_target_pairs={{0,2},{1,3},{2,0},{3,1},{4,6},{5,7},{6,4},{7,5},{8,10},{9,11},{10,... | collective-permute-start | bytes 786440 | tf_op jit(solution)/shard_map/ppermute | solution.py:256
  25.4 6.4 %collective-permute-start.16 = (bf16[272,256]{1,0:T(8,128)(2,1)S(1)}, bf16[272,256]{1,0:T(8,128)(2,1)S(1)}, u32[]{:S(2)}, u32[]{:S(2)}) collective-permute-start(bf16[272,256]{1,0:T(8,128)(2,1)S(1)} %get-tuple-element.41), channel_id=1, source_target_pairs={{0,1},{1,0},{2,3},{3,2},{4,5},{5,4},{6,7},{7,6},{8,9},{9,8},{10,11... | collective-permute-start | bytes 417800 | tf_op jit(solution)/shard_map/ppermute | solution.py:244
  26.6 6.7 %collective-permute-start.17 = (bf16[272,256]{1,0:T(8,128)(2,1)S(1)}, bf16[272,256]{1,0:T(8,128)(2,1)S(1)}, u32[]{:S(2)}, u32[]{:S(2)}) collective-permute-start(bf16[272,256]{1,0:T(8,128)(2,1)S(1)} %get-tuple-element.42), channel_id=1, source_target_pairs={{0,16},{1,17},{2,18},{3,19},{4,20},{5,21},{6,22},{7,23},{8,24},{9,... | collective-permute-start | bytes 417800 | tf_op jit(solution)/shard_map/ppermute | solution.py:244
  27.4 7.5 %collective-permute-start.18 = (bf16[272,256]{1,0:T(8,128)(2,1)S(1)}, bf16[272,256]{1,0:T(8,128)(2,1)S(1)}, u32[]{:S(2)}, u32[]{:S(2)}) collective-permute-start(bf16[272,256]{1,0:T(8,128)(2,1)S(1)} %get-tuple-element.43), channel_id=1, source_target_pairs={{0,17},{1,16},{2,19},{3,18},{4,21},{5,20},{6,23},{7,22},{8,25},{9,... | collective-permute-start | bytes 417800 | tf_op jit(solution)/shard_map/ppermute | solution.py:244
  28.9 8.8 %collective-permute-start.19 = (bf16[272,256]{1,0:T(8,128)(2,1)S(1)}, bf16[272,256]{1,0:T(8,128)(2,1)S(1)}, u32[]{:S(2)}, u32[]{:S(2)}) collective-permute-start(bf16[272,256]{1,0:T(8,128)(2,1)S(1)} %get-tuple-element.40.refs_0_.refs_8_), channel_id=1, source_target_pairs={{0,8},{1,9},{2,10},{3,11},{4,12},{5,13},{6,14},{7,15},{8,0},{9,1},... | collective-permute-start | bytes 417800 | tf_op jit(solution)/shard_map/ppermute | solution.py:249
  31.8 5.9 %collective-permute-start.20 = (bf16[272,256]{1,0:T(8,128)(2,1)S(1)}, bf16[272,256]{1,0:T(8,128)(2,1)S(1)}, u32[]{:S(2)}, u32[]{:S(2)}) collective-permute-start(bf16[272,256]{1,0:T(8,128)(2,1)S(1)} %collective-permute-done.16.refs_1_.refs_9_), channel_id=1, source_target_pairs={{0,8},{1,9},{2,10},{3,11},{4,12},{5,13},{6,14},{7,15},{8,0},{9,1},... | collective-permute-start | bytes 417800 | tf_op jit(solution)/shard_map/ppermute | solution.py:249
  33.3 4.4 %collective-permute-start.21 = (bf16[272,256]{1,0:T(8,128)(2,1)S(1)}, bf16[272,256]{1,0:T(8,128)(2,1)S(1)}, u32[]{:S(2)}, u32[]{:S(2)}) collective-permute-start(bf16[272,256]{1,0:T(8,128)(2,1)S(1)} %collective-permute-done.17.refs_2_.refs_10_), channel_id=1, source_target_pairs={{0,8},{1,9},{2,10},{3,11},{4,12},{5,13},{6,14},{7,15},{8,0},{9,1},... | collective-permute-start | bytes 417800 | tf_op jit(solution)/shard_map/ppermute | solution.py:249
  35.0 9.7 %collective-permute-start.8 = (bf16[256,256]{1,0:T(8,128)(2,1)S(1)}, bf16[256,256]{1,0:T(8,128)(2,1)S(1)}, u32[]{:S(2)}, u32[]{:S(2)}) collective-permute-start(bf16[256,256]{1,0:T(8,128)(2,1)S(1)} %slice.51), channel_id=1, source_target_pairs={{0,4},{1,5},{2,6},{3,7},{4,0},{5,1},{6,2},{7,3},{8,12},{9,13},{10,... | collective-permute-start | bytes 393224 | tf_op jit(solution)/shard_map/ppermute | solution.py:256
  38.8 11.2 %collective-permute-start.23 = (bf16[512,256]{1,0:T(8,128)(2,1)S(1)}, bf16[512,256]{1,0:T(8,128)(2,1)S(1)}, u32[]{:S(2)}, u32[]{:S(2)}) collective-permute-start(bf16[512,256]{1,0:T(8,128)(2,1)S(1)} %get-tuple-element.45), channel_id=1, source_target_pairs={{0,2},{1,3},{2,0},{3,1},{4,6},{5,7},{6,4},{7,5},{8,10},{9,11},{10,... | collective-permute-start | bytes 786440 | tf_op jit(solution)/shard_map/ppermute | solution.py:256
  50.1 8.0 %collective-permute-start.24 = (bf16[256,256]{1,0:T(8,128)(2,1)S(1)}, bf16[256,256]{1,0:T(8,128)(2,1)S(1)}, u32[]{:S(2)}, u32[]{:S(2)}) collective-permute-start(bf16[256,256]{1,0:T(8,128)(2,1)S(1)} %slice.50), channel_id=1, source_target_pairs={{0,4},{1,5},{2,6},{3,7},{4,0},{5,1},{6,2},{7,3},{8,12},{9,13},{10,... | collective-permute-start | bytes 393224 | tf_op jit(solution)/shard_map/ppermute | solution.py:256
  50.1 5.5 %collective-permute-start.11 = (bf16[128,256]{1,0:T(8,128)(2,1)S(1)}, bf16[128,256]{1,0:T(8,128)(2,1)S(1)}, u32[]{:S(2)}, u32[]{:S(2)}) collective-permute-start(bf16[128,256]{1,0:T(8,128)(2,1)S(1)} %get-tuple-element.48), channel_id=1, source_target_pairs={{0,17},{1,16},{2,19},{3,18},{4,21},{5,20},{6,23},{7,22},{8,25},{9,... | collective-permute-start | bytes 196616 | tf_op jit(solution)/shard_map/ppermute | solution.py:244
  52.0 4.3 %collective-permute-start.9 = (bf16[128,256]{1,0:T(8,128)(2,1)S(1)}, bf16[128,256]{1,0:T(8,128)(2,1)S(1)}, u32[]{:S(2)}, u32[]{:S(2)}) collective-permute-start(bf16[128,256]{1,0:T(8,128)(2,1)S(1)} %get-tuple-element.48), channel_id=1, source_target_pairs={{0,1},{1,0},{2,3},{3,2},{4,5},{5,4},{6,7},{7,6},{8,9},{9,8},{10,11... | collective-permute-start | bytes 196616 | tf_op jit(solution)/shard_map/ppermute | solution.py:244
  52.5 7.3 %collective-permute-start.12 = (bf16[128,256]{1,0:T(8,128)(2,1)S(1)}, bf16[128,256]{1,0:T(8,128)(2,1)S(1)}, u32[]{:S(2)}, u32[]{:S(2)}) collective-permute-start(bf16[128,256]{1,0:T(8,128)(2,1)S(1)} %get-tuple-element.49), channel_id=1, source_target_pairs={{0,8},{1,9},{2,10},{3,11},{4,12},{5,13},{6,14},{7,15},{8,0},{9,1},... | collective-permute-start | bytes 196616 | tf_op jit(solution)/shard_map/ppermute | solution.py:249
  52.5 7.9 %collective-permute-start.10 = (bf16[128,256]{1,0:T(8,128)(2,1)S(1)}, bf16[128,256]{1,0:T(8,128)(2,1)S(1)}, u32[]{:S(2)}, u32[]{:S(2)}) collective-permute-start(bf16[128,256]{1,0:T(8,128)(2,1)S(1)} %get-tuple-element.49), channel_id=1, source_target_pairs={{0,16},{1,17},{2,18},{3,19},{4,20},{5,21},{6,22},{7,23},{8,24},{9,... | collective-permute-start | bytes 196616 | tf_op jit(solution)/shard_map/ppermute | solution.py:244
  55.6 6.0 %collective-permute-start.15 = (bf16[128,256]{1,0:T(8,128)(2,1)S(1)}, bf16[128,256]{1,0:T(8,128)(2,1)S(1)}, u32[]{:S(2)}, u32[]{:S(2)}) collective-permute-start(bf16[128,256]{1,0:T(8,128)(2,1)S(1)} %collective-permute-done.11), channel_id=1, source_target_pairs={{0,8},{1,9},{2,10},{3,11},{4,12},{5,13},{6,14},{7,15},{8,0},{9,1},... | collective-permute-start | bytes 196616 | tf_op jit(solution)/shard_map/ppermute | solution.py:249
  56.2 5.4 %collective-permute-start.13 = (bf16[128,256]{1,0:T(8,128)(2,1)S(1)}, bf16[128,256]{1,0:T(8,128)(2,1)S(1)}, u32[]{:S(2)}, u32[]{:S(2)}) collective-permute-start(bf16[128,256]{1,0:T(8,128)(2,1)S(1)} %collective-permute-done.9), channel_id=1, source_target_pairs={{0,8},{1,9},{2,10},{3,11},{4,12},{5,13},{6,14},{7,15},{8,0},{9,1},... | collective-permute-start | bytes 196616 | tf_op jit(solution)/shard_map/ppermute | solution.py:249
  58.1 5.7 %collective-permute-start.27 = (bf16[128,256]{1,0:T(8,128)(2,1)S(1)}, bf16[128,256]{1,0:T(8,128)(2,1)S(1)}, u32[]{:S(2)}, u32[]{:S(2)}) collective-permute-start(bf16[128,256]{1,0:T(8,128)(2,1)S(1)} %get-tuple-element.46), channel_id=1, source_target_pairs={{0,17},{1,16},{2,19},{3,18},{4,21},{5,20},{6,23},{7,22},{8,25},{9,... | collective-permute-start | bytes 196616 | tf_op jit(solution)/shard_map/ppermute | solution.py:244
  59.8 4.3 %collective-permute-start.25 = (bf16[128,256]{1,0:T(8,128)(2,1)S(1)}, bf16[128,256]{1,0:T(8,128)(2,1)S(1)}, u32[]{:S(2)}, u32[]{:S(2)}) collective-permute-start(bf16[128,256]{1,0:T(8,128)(2,1)S(1)} %get-tuple-element.46), channel_id=1, source_target_pairs={{0,1},{1,0},{2,3},{3,2},{4,5},{5,4},{6,7},{7,6},{8,9},{9,8},{10,11... | collective-permute-start | bytes 196616 | tf_op jit(solution)/shard_map/ppermute | solution.py:244
  60.4 4.3 %collective-permute-start.26 = (bf16[128,256]{1,0:T(8,128)(2,1)S(1)}, bf16[128,256]{1,0:T(8,128)(2,1)S(1)}, u32[]{:S(2)}, u32[]{:S(2)}) collective-permute-start(bf16[128,256]{1,0:T(8,128)(2,1)S(1)} %get-tuple-element.47), channel_id=1, source_target_pairs={{0,16},{1,17},{2,18},{3,19},{4,20},{5,21},{6,22},{7,23},{8,24},{9,... | collective-permute-start | bytes 196616 | tf_op jit(solution)/shard_map/ppermute | solution.py:244
  61.6 3.0 %collective-permute-start.14 = (bf16[128,256]{1,0:T(8,128)(2,1)S(1)}, bf16[128,256]{1,0:T(8,128)(2,1)S(1)}, u32[]{:S(2)}, u32[]{:S(2)}) collective-permute-start(bf16[128,256]{1,0:T(8,128)(2,1)S(1)} %collective-permute-done.10), channel_id=1, source_target_pairs={{0,8},{1,9},{2,10},{3,11},{4,12},{5,13},{6,14},{7,15},{8,0},{9,1},... | collective-permute-start | bytes 196616 | tf_op jit(solution)/shard_map/ppermute | solution.py:249
  61.6 3.9 %collective-permute-start.28 = (bf16[128,256]{1,0:T(8,128)(2,1)S(1)}, bf16[128,256]{1,0:T(8,128)(2,1)S(1)}, u32[]{:S(2)}, u32[]{:S(2)}) collective-permute-start(bf16[128,256]{1,0:T(8,128)(2,1)S(1)} %get-tuple-element.47), channel_id=1, source_target_pairs={{0,8},{1,9},{2,10},{3,11},{4,12},{5,13},{6,14},{7,15},{8,0},{9,1},... | collective-permute-start | bytes 196616 | tf_op jit(solution)/shard_map/ppermute | solution.py:249
  (8 other events, 13.1 us)

commit v4 on v3

--- a/solution.py
+++ b/solution.py
@@ -13,21 +13,27 @@
 
 
 class Plan:
-    def __init__(self, mesh, psi, terms):
+    def __init__(self, mesh, psi, terms, order):
         self.op, self.sec = mesh.shape["op"], mesh.shape["sec"]
         self.held, self.blk = psi.shape[0], psi.shape[1]
         self.terms = terms
         self.slots = self.sec // 2
-        self.extra = 0
-        while self.slots * self.op * 2**self.extra < self.held * self.sec:
-            self.extra += 1
-        self.places = (self.op // 2) * 2**self.extra
+        extra = 0
+        while self.slots * self.op * 2**extra < self.held * self.sec:
+            extra += 1
+        self.inside, self.bits = order[:extra], order[extra:]
+        self.places = (self.op // 2) * 2**extra
         self.rows = self.blk // (2 * self.places)
-        self.step, self.window = 2, 6
-        self.bits = list(range(self.extra, self.sec.bit_length() - 1))
+        self.step, self.window = 8, 2
+
+    def extra(self, sec):
+        total = sec * 0
+        for i, b in enumerate(self.inside):
+            total = total + (((sec >> b) & 1) << i)
+        return total
 
     def place(self, op, sec):
-        return (op // 2) * 2**self.extra + sec % 2**self.extra
+        return (op // 2) * 2 ** len(self.inside) + self.extra(sec)
 
     def swap(self, op_mask, sec_mask):
         n = self.op * self.sec
@@ -35,7 +41,8 @@
         return [(i, i ^ mask) for i in range(n)]
 
     def across(self, m):
-        return self.swap((m >> self.extra) << 1, m & (2**self.extra - 1))
+        sec_mask = sum(((m >> i) & 1) << b for i, b in enumerate(self.inside))
+        return self.swap((m >> len(self.inside)) << 1, sec_mask)
 
 
 def contract_kernel(plan, fetch, *refs):
@@ -172,7 +179,7 @@
             index = jnp.int32(0)
             for b in plan.bits:
                 index = index * 2 + ((away >> b) & 1)
-            index = index * 2**plan.extra + (away & (2**plan.extra - 1))
+            index = index * 2 ** len(plan.inside) + plan.extra(away)
             acc[index * plan.held + label % plan.held] += blocks[i][pl.ds(j * plan.rows, plan.rows), :].astype(jnp.float32)
     half = acc.shape[0] // 2
     for k, out in enumerate(outs):
@@ -181,7 +188,7 @@
 
 def spread(plan, own, other):
     blk, rows, slots = plan.blk, plan.rows, plan.slots
-    sectors = plan.held * 2 ** (plan.extra + len(plan.bits))
+    sectors = plan.held * plan.sec
     n = 2 * plan.places
 
     def half(rc):
@@ -249,8 +256,7 @@
     return [lax.ppermute(x, AXES, plan.swap(1, 0)) for x in own]
 
 
-def combine(plan, own):
-    away, kept = spread(plan, own, to_core(plan, own))
+def finish(plan, away, kept):
     total = kept.astype(jnp.float32)
     for k, b in enumerate(plan.bits):
         arrived = lax.ppermute(away, AXES, plan.swap(0, 1 << b))
@@ -261,19 +267,27 @@
             total = total[:middle]
     total = total.astype(jnp.bfloat16)
     size = plan.held * plan.rows
-    sums = [total[e * size : (e + 1) * size] for e in range(2**plan.extra)]
-    own = across(plan, [sums[m % 2**plan.extra] for m in range(plan.places)])
+    extras = 2 ** len(plan.inside)
+    sums = [total[e * size : (e + 1) * size] for e in range(extras)]
+    own = across(plan, [sums[m % extras] for m in range(plan.places)])
     return assemble(plan, own, to_core(plan, own))
 
 
 def per_device(mesh, first, second, left, right, source, target):
-    plan = Plan(mesh, first, left.shape[0])
+    terms = left.shape[0]
+    order = list(range(mesh.shape["sec"].bit_length() - 1))
+    plan = Plan(mesh, first, terms, order)
+    other_plan = Plan(mesh, first, terms, [order[1], order[0], *order[2:]])
+
     *pieces, lhs, rhs = contract(plan, True, source, target, left, right, first)
     early = across(plan, pieces)
-    pieces = contract(plan, False, source, target, lhs, rhs, second)
+    pieces = contract(other_plan, False, source, target, lhs, rhs, second)
     early, pieces = lax.optimization_barrier((early, pieces))
-    late = across(plan, pieces)
-    return combine(plan, early), combine(plan, late)
+    late = across(other_plan, pieces)
+    away, kept = spread(plan, early, to_core(plan, early))
+    away, late = lax.optimization_barrier((away, late))
+    result = finish(plan, away, kept)
+    return result, finish(other_plan, *spread(other_plan, late, to_core(other_plan, late)))
 
 
 def solution(mesh):

time: 66.9 us -> 63 us (0.942)
  Pallas kernels: 16.6 us -> 13 us
  waiting for transfers between devices: 27.3 us -> 24.5 us
  starting transfers between devices: 21.8 us -> 24.3 us
    pallas_call x2, Pallas kernels: 12.9 us -> 9.27 us  [contract(): pl.pallas_call(functools.partial(contract_kernel, plan, fetch), in_specs=...]
    ppermute x4, waiting for transfers between devices: 12.4 us -> 9.48 us  [finish(): arrived = lax.ppermute(away, AXES, plan.swap(0, 1 << b))]
    ppermute x4, starting transfers between devices: 4.87 us -> 6.09 us  [finish(): arrived = lax.ppermute(away, AXES, plan.swap(0, 1 << b))]
    ppermute x12, waiting for transfers between devices: 13.5 us -> 14.6 us  [across(): own[m] = lax.ppermute(pieces[m], AXES, plan.across(m))]
    ppermute x16, waiting for transfers between devices: 1.44 us -> 0.4 us  [to_core(): return [lax.ppermute(x, AXES, plan.swap(1, 0)) for x in own]]
    ppermute x16, starting transfers between devices: 1.75 us -> 2.67 us  [to_core(): return [lax.ppermute(x, AXES, plan.swap(1, 0)) for x in own]]
  transfers between devices with their start and end apart: 32 -> 32, of which waited for: 17 -> 13; matrix products, arithmetic and copies ran while one was open for 0% -> 0% of each run, Pallas kernels for 9% -> 11%
where the time goes in v4:
time: 63 us; the launch traced here: 62.9 us
  waiting for transfers between devices  24.5 us (39%)
  starting transfers between devices  24.3 us (39%)
  Pallas kernels  13 us (21%)
  between operations  0.79 us (1%)
    ppermute x12, starting transfers between devices, across(): own[m] = lax.ppermute(pieces[m], AXES, plan.across(m))  15.6 us
    ppermute x12, waiting for transfers between devices, across(): own[m] = lax.ppermute(pieces[m], AXES, plan.across(m))  14.6 us
    ppermute x4, waiting for transfers between devices, finish(): arrived = lax.ppermute(away, AXES, plan.swap(0, 1 << b))  9.48 us
    pallas_call x2, Pallas kernels, contract(): pl.pallas_call(functools.partial(contract_kernel, plan, fetch), in_specs=...  9.27 us
    ppermute x4, starting transfers between devices, finish(): arrived = lax.ppermute(away, AXES, plan.swap(0, 1 << b))  6.09 us
    ppermute x16, starting transfers between devices, to_core(): return [lax.ppermute(x, AXES, plan.swap(1, 0)) for x in own]  2.67 us
    pallas_call x2, Pallas kernels, spread(): pl.pallas_call(functools.partial(spread_kernel, plan), grid=(1,), in_spec...  2.08 us
    pallas_call x2, Pallas kernels, assemble(): pl.pallas_call(functools.partial(place_kernel, plan), in_specs=[pl.BlockS...  1.7 us
  transfers between devices with their start and end apart: 32, of which 13 were waited for; matrix products, arithmetic and copies ran while one was open for 0% of the time, Pallas kernels for 11%

profile of v4, /device:TPU:0, one launch (start us, length us, event | category | flops | bytes accessed | tf_op | source)
XLA Modules:
  0.0 62.9 jit_solution(3760646315070726354)
XLA Ops:
  0.6 5.5 %contract.2 = (bf16[272,256]{1,0:T(8,128)(2,1)S(1)}, bf16[272,256]{1,0:T(8,128)(2,1)S(1)}, bf16[272,256]{1,0:T(8,128)(2,1)S(1)}, bf16[272,256]{1,0:T(8,128)(2,1)...) custom-call(s32[32]{0:T(128)} %refs_0_.3, s32[32]{0:T(128)} %refs_1_.3, ...), custom_call_target="tpu_custom_call" | custom-call | flops 2147483648 | bytes 8388608 | tf_op jit(solution)/shard_map/contract/pallas_call | solution.py:137
  6.1 3.0 %collective-permute-start = (bf16[272,256]{1,0:T(8,128)(2,1)S(1)}, bf16[272,256]{1,0:T(8,128)(2,1)S(1)}, u32[]{:S(2)}, u32[]{:S(2)}) collective-permute-start(bf16[272,256]{1,0:T(8,128)(2,1)S(1)} %get-tuple-element.30), channel_id=1, source_target_pairs={{0,1},{1,0},{2,3},{3,2},{4,5},{5,4},{6,7},{7,6},{8,9},{9,8},{10,11... | collective-permute-start | bytes 417800 | tf_op jit(solution)/shard_map/ppermute | solution.py:251
  9.1 1.5 %collective-permute-start.1 = (bf16[272,256]{1,0:T(8,128)(2,1)S(1)}, bf16[272,256]{1,0:T(8,128)(2,1)S(1)}, u32[]{:S(2)}, u32[]{:S(2)}) collective-permute-start(bf16[272,256]{1,0:T(8,128)(2,1)S(1)} %get-tuple-element.31), channel_id=1, source_target_pairs={{0,16},{1,17},{2,18},{3,19},{4,20},{5,21},{6,22},{7,23},{8,24},{9,... | collective-permute-start | bytes 417800 | tf_op jit(solution)/shard_map/ppermute | solution.py:251
  10.7 3.8 %contract.3 = (bf16[272,256]{1,0:T(8,128)(2,1)S(1)}, bf16[272,256]{1,0:T(8,128)(2,1)S(1)}, bf16[272,256]{1,0:T(8,128)(2,1)S(1)}, bf16[272,256]{1,0:T(8,128)(2,1)S(1)}) custom-call(s32[32]{0:T(128)} %refs_0_.3, s32[32]{0:T(128)} %refs_1_.3, bf16[32,256,256]{2,1,0:T(8,128)(2,1)S(1)} %get-tuple-element.33.refs_2_, ...), custom_call_target="tpu_custom_call" | custom-call | flops 2147483648 | bytes 8192 | tf_op jit(solution)/shard_map/contract/pallas_call | solution.py:137
  14.5 2.8 %collective-permute-done.1.refs_2_.refs_10_ = bf16[272,256]{1,0:T(8,128)(2,1)S(1)} collective-permute-done((bf16[272,256]{1,0:T(8,128)(2,1)S(1)}, bf16[272,256]{1,0:T(8,128)(2,1)S(1)}, u32[]{:S(2)}, u32[]{:S(2)}) %collective-permute-start.1) | collective-permute-done | bytes 139296 | tf_op jit(solution)/shard_map/ppermute | solution.py:251
  17.8 1.6 %collective-permute-start.7 = (bf16[272,256]{1,0:T(8,128)(2,1)S(1)}, bf16[272,256]{1,0:T(8,128)(2,1)S(1)}, u32[]{:S(2)}, u32[]{:S(2)}) collective-permute-start(bf16[272,256]{1,0:T(8,128)(2,1)S(1)} %get-tuple-element.46), channel_id=1, source_target_pairs={{0,2},{1,3},{2,0},{3,1},{4,6},{5,7},{6,4},{7,5},{8,10},{9,11},{10,... | collective-permute-start | bytes 417800 | tf_op jit(solution)/shard_map/ppermute | solution.py:251
  19.8 1.5 %collective-permute-start.8 = (bf16[272,256]{1,0:T(8,128)(2,1)S(1)}, bf16[272,256]{1,0:T(8,128)(2,1)S(1)}, u32[]{:S(2)}, u32[]{:S(2)}) collective-permute-start(bf16[272,256]{1,0:T(8,128)(2,1)S(1)} %get-tuple-element.47), channel_id=1, source_target_pairs={{0,16},{1,17},{2,18},{3,19},{4,20},{5,21},{6,22},{7,23},{8,24},{9,... | collective-permute-start | bytes 417800 | tf_op jit(solution)/shard_map/ppermute | solution.py:251
  21.8 1.0 %spread.2 = (bf16[512,256]{1,0:T(8,128)(2,1)S(1)}, bf16[512,256]{1,0:T(8,128)(2,1)S(1)}) custom-call(bf16[272,256]{1,0:T(8,128)(2,1)S(1)} %get-tuple-element.39.refs_0_.refs_8_, bf16[272,256]{1,0:T(8,128)(2,1)S(1)} %collective-permute-done.refs_1_.refs_9_, bf16[272,256]{1,0:T(8,128)(2,1)S(1)} %collective-permute-done.1.refs_2_.refs_10_, ...), custom_call_target="tpu_custom_call" | custom-call | tf_op jit(solution)/shard_map/spread/pallas_call | solution.py:199
  23.3 5.1 %collective-permute-done.8.refs_2_.refs_10_ = bf16[272,256]{1,0:T(8,128)(2,1)S(1)} collective-permute-done((bf16[272,256]{1,0:T(8,128)(2,1)S(1)}, bf16[272,256]{1,0:T(8,128)(2,1)S(1)}, u32[]{:S(2)}, u32[]{:S(2)}) %collective-permute-start.8) | collective-permute-done | bytes 139296 | tf_op jit(solution)/shard_map/ppermute | solution.py:251
  29.9 4.9 %collective-permute-done.10 = bf16[512,256]{1,0:T(8,128)(2,1)S(1)} collective-permute-done((bf16[512,256]{1,0:T(8,128)(2,1)S(1)}, bf16[512,256]{1,0:T(8,128)(2,1)S(1)}, u32[]{:S(2)}, u32[]{:S(2)}) %collective-permute-start.10) | collective-permute-done | bytes 262176 | tf_op jit(solution)/shard_map/ppermute | solution.py:262
  34.9 2.7 %collective-permute-start.11 = (bf16[256,256]{1,0:T(8,128)(2,1)S(1)}, bf16[256,256]{1,0:T(8,128)(2,1)S(1)}, u32[]{:S(2)}, u32[]{:S(2)}) collective-permute-start(bf16[256,256]{1,0:T(8,128)(2,1)S(1)} %slice.51), channel_id=1, source_target_pairs={{0,4},{1,5},{2,6},{3,7},{4,0},{5,1},{6,2},{7,3},{8,12},{9,13},{10,... | collective-permute-start | bytes 393224 | tf_op jit(solution)/shard_map/ppermute | solution.py:262
  37.5 1.0 %spread.3 = (bf16[512,256]{1,0:T(8,128)(2,1)S(1)}, bf16[512,256]{1,0:T(8,128)(2,1)S(1)}) custom-call(bf16[272,256]{1,0:T(8,128)(2,1)S(1)} %get-tuple-element.50.refs_0_.refs_8_, bf16[272,256]{1,0:T(8,128)(2,1)S(1)} %collective-permute-done.7.refs_1_.refs_9_, bf16[272,256]{1,0:T(8,128)(2,1)S(1)} %collective-permute-done.8.refs_2_.refs_10_, ...), custom_call_target="tpu_custom_call" | custom-call | tf_op jit(solution)/shard_map/spread/pallas_call | solution.py:199
  38.6 2.9 %collective-permute-start.23 = (bf16[512,256]{1,0:T(8,128)(2,1)S(1)}, bf16[512,256]{1,0:T(8,128)(2,1)S(1)}, u32[]{:S(2)}, u32[]{:S(2)}) collective-permute-start(bf16[512,256]{1,0:T(8,128)(2,1)S(1)} %get-tuple-element.55), channel_id=1, source_target_pairs={{0,1},{1,0},{2,3},{3,2},{4,5},{5,4},{6,7},{7,6},{8,9},{9,8},{10,11... | collective-permute-start | bytes 786440 | tf_op jit(solution)/shard_map/ppermute | solution.py:262
  41.5 0.7 %collective-permute-done.11 = bf16[256,256]{1,0:T(8,128)(2,1)S(1)} collective-permute-done((bf16[256,256]{1,0:T(8,128)(2,1)S(1)}, bf16[256,256]{1,0:T(8,128)(2,1)S(1)}, u32[]{:S(2)}, u32[]{:S(2)}) %collective-permute-start.11) | collective-permute-done | bytes 131104 | tf_op jit(solution)/shard_map/ppermute | solution.py:262
  42.2 3.6 %collective-permute-done.23 = bf16[512,256]{1,0:T(8,128)(2,1)S(1)} collective-permute-done((bf16[512,256]{1,0:T(8,128)(2,1)S(1)}, bf16[512,256]{1,0:T(8,128)(2,1)S(1)}, u32[]{:S(2)}, u32[]{:S(2)}) %collective-permute-start.23) | collective-permute-done | bytes 262176 | tf_op jit(solution)/shard_map/ppermute | solution.py:262
  46.0 2.2 %collective-permute-start.14 = (bf16[128,256]{1,0:T(8,128)(2,1)S(1)}, bf16[128,256]{1,0:T(8,128)(2,1)S(1)}, u32[]{:S(2)}, u32[]{:S(2)}) collective-permute-start(bf16[128,256]{1,0:T(8,128)(2,1)S(1)} %get-tuple-element.58), channel_id=1, source_target_pairs={{0,17},{1,16},{2,19},{3,18},{4,21},{5,20},{6,23},{7,22},{8,25},{9,... | collective-permute-start | bytes 196616 | tf_op jit(solution)/shard_map/ppermute | solution.py:251
  48.2 1.8 %collective-permute-start.12 = (bf16[128,256]{1,0:T(8,128)(2,1)S(1)}, bf16[128,256]{1,0:T(8,128)(2,1)S(1)}, u32[]{:S(2)}, u32[]{:S(2)}) collective-permute-start(bf16[128,256]{1,0:T(8,128)(2,1)S(1)} %get-tuple-element.58), channel_id=1, source_target_pairs={{0,1},{1,0},{2,3},{3,2},{4,5},{5,4},{6,7},{7,6},{8,9},{9,8},{10,11... | collective-permute-start | bytes 196616 | tf_op jit(solution)/shard_map/ppermute | solution.py:251
  50.0 1.2 %collective-permute-done.14 = bf16[128,256]{1,0:T(8,128)(2,1)S(1)} collective-permute-done((bf16[128,256]{1,0:T(8,128)(2,1)S(1)}, bf16[128,256]{1,0:T(8,128)(2,1)S(1)}, u32[]{:S(2)}, u32[]{:S(2)}) %collective-permute-start.14) | collective-permute-done | bytes 65568 | tf_op jit(solution)/shard_map/ppermute | solution.py:251
  51.3 1.7 %collective-permute-done.12 = bf16[128,256]{1,0:T(8,128)(2,1)S(1)} collective-permute-done((bf16[128,256]{1,0:T(8,128)(2,1)S(1)}, bf16[128,256]{1,0:T(8,128)(2,1)S(1)}, u32[]{:S(2)}, u32[]{:S(2)}) %collective-permute-start.12) | collective-permute-done | bytes 65568 | tf_op jit(solution)/shard_map/ppermute | solution.py:251
  53.9 2.6 %collective-permute-start.25 = (bf16[128,256]{1,0:T(8,128)(2,1)S(1)}, bf16[128,256]{1,0:T(8,128)(2,1)S(1)}, u32[]{:S(2)}, u32[]{:S(2)}) collective-permute-start(bf16[128,256]{1,0:T(8,128)(2,1)S(1)} %get-tuple-element.56), channel_id=1, source_target_pairs={{0,2},{1,3},{2,0},{3,1},{4,6},{5,7},{6,4},{7,5},{8,10},{9,11},{10,... | collective-permute-start | bytes 196616 | tf_op jit(solution)/shard_map/ppermute | solution.py:251
  57.4 1.8 %collective-permute-done.27 = bf16[128,256]{1,0:T(8,128)(2,1)S(1)} collective-permute-done((bf16[128,256]{1,0:T(8,128)(2,1)S(1)}, bf16[128,256]{1,0:T(8,128)(2,1)S(1)}, u32[]{:S(2)}, u32[]{:S(2)}) %collective-permute-start.27) | collective-permute-done | bytes 65568 | tf_op jit(solution)/shard_map/ppermute | solution.py:251
  59.7 1.1 %collective-permute-done.26 = bf16[128,256]{1,0:T(8,128)(2,1)S(1)} collective-permute-done((bf16[128,256]{1,0:T(8,128)(2,1)S(1)}, bf16[128,256]{1,0:T(8,128)(2,1)S(1)}, u32[]{:S(2)}, u32[]{:S(2)}) %collective-permute-start.26) | collective-permute-done | bytes 65568 | tf_op jit(solution)/shard_map/ppermute | solution.py:251
  60.8 0.8 %assemble.2 = bf16[4,256,256]{2,1,0:T(8,128)(2,1)} custom-call(bf16[4,32,256]{2,1,0:T(8,128)(2,1)S(1)} %bitcast.16, bf16[4,32,256]{2,1,0:T(8,128)(2,1)S(1)} %bitcast.19, bf16[4,32,256]{2,1,0:T(8,128)(2,1)S(1)} %bitcast.21, bf16[4,32,256]{2,1,0:T(8,128)(2,1)S(1)} %bitcast.18, bf16[4,32,256]{2,1,0:T(8,128)(2,1)S(1)} %bitcast.20, ...), custom_call_target="tpu_custom_call" | custom-call | tf_op jit(solution)/shard_map/assemble/pallas_call | solution.py:237
  62.0 0.8 %assemble.3 = bf16[4,256,256]{2,1,0:T(8,128)(2,1)} custom-call(bf16[4,32,256]{2,1,0:T(8,128)(2,1)S(1)} %bitcast.17, bf16[4,32,256]{2,1,0:T(8,128)(2,1)S(1)} %bitcast.25, bf16[4,32,256]{2,1,0:T(8,128)(2,1)S(1)} %bitcast.26, bf16[4,32,256]{2,1,0:T(8,128)(2,1)S(1)} %bitcast.23, bf16[4,32,256]{2,1,0:T(8,128)(2,1)S(1)} %bitcast.27, ...), custom_call_target="tpu_custom_call" | custom-call | tf_op jit(solution)/shard_map/assemble/pallas_call | solution.py:237
  (54 shorter events, 6.4 us)
Async XLA Ops:
  6.1 8.3 %collective-permute-start = (bf16[272,256]{1,0:T(8,128)(2,1)S(1)}, bf16[272,256]{1,0:T(8,128)(2,1)S(1)}, u32[]{:S(2)}, u32[]{:S(2)}) collective-permute-start(bf16[272,256]{1,0:T(8,128)(2,1)S(1)} %get-tuple-element.30), channel_id=1, source_target_pairs={{0,1},{1,0},{2,3},{3,2},{4,5},{5,4},{6,7},{7,6},{8,9},{9,8},{10,11... | collective-permute-start | bytes 417800 | tf_op jit(solution)/shard_map/ppermute | solution.py:251
  9.1 8.1 %collective-permute-start.1 = (bf16[272,256]{1,0:T(8,128)(2,1)S(1)}, bf16[272,256]{1,0:T(8,128)(2,1)S(1)}, u32[]{:S(2)}, u32[]{:S(2)}) collective-permute-start(bf16[272,256]{1,0:T(8,128)(2,1)S(1)} %get-tuple-element.31), channel_id=1, source_target_pairs={{0,16},{1,17},{2,18},{3,19},{4,20},{5,21},{6,22},{7,23},{8,24},{9,... | collective-permute-start | bytes 417800 | tf_op jit(solution)/shard_map/ppermute | solution.py:251
  10.6 6.6 %collective-permute-start.2 = (bf16[272,256]{1,0:T(8,128)(2,1)S(1)}, bf16[272,256]{1,0:T(8,128)(2,1)S(1)}, u32[]{:S(2)}, u32[]{:S(2)}) collective-permute-start(bf16[272,256]{1,0:T(8,128)(2,1)S(1)} %get-tuple-element.32), channel_id=1, source_target_pairs={{0,17},{1,16},{2,19},{3,18},{4,21},{5,20},{6,23},{7,22},{8,25},{9,... | collective-permute-start | bytes 417800 | tf_op jit(solution)/shard_map/ppermute | solution.py:251
  17.2 4.1 %collective-permute-start.4 = (bf16[272,256]{1,0:T(8,128)(2,1)S(1)}, bf16[272,256]{1,0:T(8,128)(2,1)S(1)}, u32[]{:S(2)}, u32[]{:S(2)}) collective-permute-start(bf16[272,256]{1,0:T(8,128)(2,1)S(1)} %collective-permute-done.refs_1_.refs_9_), channel_id=1, source_target_pairs={{0,8},{1,9},{2,10},{3,11},{4,12},{5,13},{6,14},{7,15},{8,0},{9,1},... | collective-permute-start | bytes 417800 | tf_op jit(solution)/shard_map/ppermute | solution.py:256
  17.8 5.6 %collective-permute-start.7 = (bf16[272,256]{1,0:T(8,128)(2,1)S(1)}, bf16[272,256]{1,0:T(8,128)(2,1)S(1)}, u32[]{:S(2)}, u32[]{:S(2)}) collective-permute-start(bf16[272,256]{1,0:T(8,128)(2,1)S(1)} %get-tuple-element.46), channel_id=1, source_target_pairs={{0,2},{1,3},{2,0},{3,1},{4,6},{5,7},{6,4},{7,5},{8,10},{9,11},{10,... | collective-permute-start | bytes 417800 | tf_op jit(solution)/shard_map/ppermute | solution.py:251
  19.8 8.6 %collective-permute-start.8 = (bf16[272,256]{1,0:T(8,128)(2,1)S(1)}, bf16[272,256]{1,0:T(8,128)(2,1)S(1)}, u32[]{:S(2)}, u32[]{:S(2)}) collective-permute-start(bf16[272,256]{1,0:T(8,128)(2,1)S(1)} %get-tuple-element.47), channel_id=1, source_target_pairs={{0,16},{1,17},{2,18},{3,19},{4,20},{5,21},{6,22},{7,23},{8,24},{9,... | collective-permute-start | bytes 417800 | tf_op jit(solution)/shard_map/ppermute | solution.py:251
  21.4 7.0 %collective-permute-start.9 = (bf16[272,256]{1,0:T(8,128)(2,1)S(1)}, bf16[272,256]{1,0:T(8,128)(2,1)S(1)}, u32[]{:S(2)}, u32[]{:S(2)}) collective-permute-start(bf16[272,256]{1,0:T(8,128)(2,1)S(1)} %get-tuple-element.48), channel_id=1, source_target_pairs={{0,18},{1,19},{2,16},{3,17},{4,22},{5,23},{6,20},{7,21},{8,26},{9,... | collective-permute-start | bytes 417800 | tf_op jit(solution)/shard_map/ppermute | solution.py:251
  28.4 6.4 %collective-permute-start.10 = (bf16[512,256]{1,0:T(8,128)(2,1)S(1)}, bf16[512,256]{1,0:T(8,128)(2,1)S(1)}, u32[]{:S(2)}, u32[]{:S(2)}) collective-permute-start(bf16[512,256]{1,0:T(8,128)(2,1)S(1)} %get-tuple-element.49), channel_id=1, source_target_pairs={{0,2},{1,3},{2,0},{3,1},{4,6},{5,7},{6,4},{7,5},{8,10},{9,11},{10,... | collective-permute-start | bytes 786440 | tf_op jit(solution)/shard_map/ppermute | solution.py:262
  28.9 8.6 %collective-permute-start.19 = (bf16[272,256]{1,0:T(8,128)(2,1)S(1)}, bf16[272,256]{1,0:T(8,128)(2,1)S(1)}, u32[]{:S(2)}, u32[]{:S(2)}) collective-permute-start(bf16[272,256]{1,0:T(8,128)(2,1)S(1)} %get-tuple-element.50.refs_0_.refs_8_), channel_id=1, source_target_pairs={{0,8},{1,9},{2,10},{3,11},{4,12},{5,13},{6,14},{7,15},{8,0},{9,1},... | collective-permute-start | bytes 417800 | tf_op jit(solution)/shard_map/ppermute | solution.py:256
  28.9 8.6 %collective-permute-start.20 = (bf16[272,256]{1,0:T(8,128)(2,1)S(1)}, bf16[272,256]{1,0:T(8,128)(2,1)S(1)}, u32[]{:S(2)}, u32[]{:S(2)}) collective-permute-start(bf16[272,256]{1,0:T(8,128)(2,1)S(1)} %collective-permute-done.7.refs_1_.refs_9_), channel_id=1, source_target_pairs={{0,8},{1,9},{2,10},{3,11},{4,12},{5,13},{6,14},{7,15},{8,0},{9,1},... | collective-permute-start | bytes 417800 | tf_op jit(solution)/shard_map/ppermute | solution.py:256
  29.4 8.1 %collective-permute-start.21 = (bf16[272,256]{1,0:T(8,128)(2,1)S(1)}, bf16[272,256]{1,0:T(8,128)(2,1)S(1)}, u32[]{:S(2)}, u32[]{:S(2)}) collective-permute-start(bf16[272,256]{1,0:T(8,128)(2,1)S(1)} %collective-permute-done.8.refs_2_.refs_10_), channel_id=1, source_target_pairs={{0,8},{1,9},{2,10},{3,11},{4,12},{5,13},{6,14},{7,15},{8,0},{9,1},... | collective-permute-start | bytes 417800 | tf_op jit(solution)/shard_map/ppermute | solution.py:256
  29.4 8.1 %collective-permute-start.22 = (bf16[272,256]{1,0:T(8,128)(2,1)S(1)}, bf16[272,256]{1,0:T(8,128)(2,1)S(1)}, u32[]{:S(2)}, u32[]{:S(2)}) collective-permute-start(bf16[272,256]{1,0:T(8,128)(2,1)S(1)} %collective-permute-done.9.refs_3_.refs_11_), channel_id=1, source_target_pairs={{0,8},{1,9},{2,10},{3,11},{4,12},{5,13},{6,14},{7,15},{8,0},{9,1},... | collective-permute-start | bytes 417800 | tf_op jit(solution)/shard_map/ppermute | solution.py:256
  34.9 7.3 %collective-permute-start.11 = (bf16[256,256]{1,0:T(8,128)(2,1)S(1)}, bf16[256,256]{1,0:T(8,128)(2,1)S(1)}, u32[]{:S(2)}, u32[]{:S(2)}) collective-permute-start(bf16[256,256]{1,0:T(8,128)(2,1)S(1)} %slice.51), channel_id=1, source_target_pairs={{0,4},{1,5},{2,6},{3,7},{4,0},{5,1},{6,2},{7,3},{8,12},{9,13},{10,... | collective-permute-start | bytes 393224 | tf_op jit(solution)/shard_map/ppermute | solution.py:262
  38.6 7.2 %collective-permute-start.23 = (bf16[512,256]{1,0:T(8,128)(2,1)S(1)}, bf16[512,256]{1,0:T(8,128)(2,1)S(1)}, u32[]{:S(2)}, u32[]{:S(2)}) collective-permute-start(bf16[512,256]{1,0:T(8,128)(2,1)S(1)} %get-tuple-element.55), channel_id=1, source_target_pairs={{0,1},{1,0},{2,3},{3,2},{4,5},{5,4},{6,7},{7,6},{8,9},{9,8},{10,11... | collective-permute-start | bytes 786440 | tf_op jit(solution)/shard_map/ppermute | solution.py:262
  45.9 7.3 %collective-permute-start.24 = (bf16[256,256]{1,0:T(8,128)(2,1)S(1)}, bf16[256,256]{1,0:T(8,128)(2,1)S(1)}, u32[]{:S(2)}, u32[]{:S(2)}) collective-permute-start(bf16[256,256]{1,0:T(8,128)(2,1)S(1)} %slice.50), channel_id=1, source_target_pairs={{0,4},{1,5},{2,6},{3,7},{4,0},{5,1},{6,2},{7,3},{8,12},{9,13},{10,... | collective-permute-start | bytes 393224 | tf_op jit(solution)/shard_map/ppermute | solution.py:262
  46.0 5.2 %collective-permute-start.14 = (bf16[128,256]{1,0:T(8,128)(2,1)S(1)}, bf16[128,256]{1,0:T(8,128)(2,1)S(1)}, u32[]{:S(2)}, u32[]{:S(2)}) collective-permute-start(bf16[128,256]{1,0:T(8,128)(2,1)S(1)} %get-tuple-element.58), channel_id=1, source_target_pairs={{0,17},{1,16},{2,19},{3,18},{4,21},{5,20},{6,23},{7,22},{8,25},{9,... | collective-permute-start | bytes 196616 | tf_op jit(solution)/shard_map/ppermute | solution.py:251
  48.2 4.7 %collective-permute-start.12 = (bf16[128,256]{1,0:T(8,128)(2,1)S(1)}, bf16[128,256]{1,0:T(8,128)(2,1)S(1)}, u32[]{:S(2)}, u32[]{:S(2)}) collective-permute-start(bf16[128,256]{1,0:T(8,128)(2,1)S(1)} %get-tuple-element.58), channel_id=1, source_target_pairs={{0,1},{1,0},{2,3},{3,2},{4,5},{5,4},{6,7},{7,6},{8,9},{9,8},{10,11... | collective-permute-start | bytes 196616 | tf_op jit(solution)/shard_map/ppermute | solution.py:251
  50.0 6.5 %collective-permute-start.13 = (bf16[128,256]{1,0:T(8,128)(2,1)S(1)}, bf16[128,256]{1,0:T(8,128)(2,1)S(1)}, u32[]{:S(2)}, u32[]{:S(2)}) collective-permute-start(bf16[128,256]{1,0:T(8,128)(2,1)S(1)} %get-tuple-element.59), channel_id=1, source_target_pairs={{0,16},{1,17},{2,18},{3,19},{4,20},{5,21},{6,22},{7,23},{8,24},{9,... | collective-permute-start | bytes 196616 | tf_op jit(solution)/shard_map/ppermute | solution.py:251
  51.2 5.6 %collective-permute-start.18 = (bf16[128,256]{1,0:T(8,128)(2,1)S(1)}, bf16[128,256]{1,0:T(8,128)(2,1)S(1)}, u32[]{:S(2)}, u32[]{:S(2)}) collective-permute-start(bf16[128,256]{1,0:T(8,128)(2,1)S(1)} %collective-permute-done.14), channel_id=1, source_target_pairs={{0,8},{1,9},{2,10},{3,11},{4,12},{5,13},{6,14},{7,15},{8,0},{9,1},... | collective-permute-start | bytes 196616 | tf_op jit(solution)/shard_map/ppermute | solution.py:256
  53.3 5.9 %collective-permute-start.27 = (bf16[128,256]{1,0:T(8,128)(2,1)S(1)}, bf16[128,256]{1,0:T(8,128)(2,1)S(1)}, u32[]{:S(2)}, u32[]{:S(2)}) collective-permute-start(bf16[128,256]{1,0:T(8,128)(2,1)S(1)} %get-tuple-element.56), channel_id=1, source_target_pairs={{0,18},{1,19},{2,16},{3,17},{4,22},{5,23},{6,20},{7,21},{8,26},{9,... | collective-permute-start | bytes 196616 | tf_op jit(solution)/shard_map/ppermute | solution.py:251
  53.9 5.7 %collective-permute-start.25 = (bf16[128,256]{1,0:T(8,128)(2,1)S(1)}, bf16[128,256]{1,0:T(8,128)(2,1)S(1)}, u32[]{:S(2)}, u32[]{:S(2)}) collective-permute-start(bf16[128,256]{1,0:T(8,128)(2,1)S(1)} %get-tuple-element.56), channel_id=1, source_target_pairs={{0,2},{1,3},{2,0},{3,1},{4,6},{5,7},{6,4},{7,5},{8,10},{9,11},{10,... | collective-permute-start | bytes 196616 | tf_op jit(solution)/shard_map/ppermute | solution.py:251
  56.5 4.3 %collective-permute-start.26 = (bf16[128,256]{1,0:T(8,128)(2,1)S(1)}, bf16[128,256]{1,0:T(8,128)(2,1)S(1)}, u32[]{:S(2)}, u32[]{:S(2)}) collective-permute-start(bf16[128,256]{1,0:T(8,128)(2,1)S(1)} %get-tuple-element.57), channel_id=1, source_target_pairs={{0,16},{1,17},{2,18},{3,19},{4,20},{5,21},{6,22},{7,23},{8,24},{9,... | collective-permute-start | bytes 196616 | tf_op jit(solution)/shard_map/ppermute | solution.py:251
  56.9 3.9 %collective-permute-start.17 = (bf16[128,256]{1,0:T(8,128)(2,1)S(1)}, bf16[128,256]{1,0:T(8,128)(2,1)S(1)}, u32[]{:S(2)}, u32[]{:S(2)}) collective-permute-start(bf16[128,256]{1,0:T(8,128)(2,1)S(1)} %collective-permute-done.13), channel_id=1, source_target_pairs={{0,8},{1,9},{2,10},{3,11},{4,12},{5,13},{6,14},{7,15},{8,0},{9,1},... | collective-permute-start | bytes 196616 | tf_op jit(solution)/shard_map/ppermute | solution.py:256
  56.9 4.8 %collective-permute-start.28 = (bf16[128,256]{1,0:T(8,128)(2,1)S(1)}, bf16[128,256]{1,0:T(8,128)(2,1)S(1)}, u32[]{:S(2)}, u32[]{:S(2)}) collective-permute-start(bf16[128,256]{1,0:T(8,128)(2,1)S(1)} %get-tuple-element.57), channel_id=1, source_target_pairs={{0,8},{1,9},{2,10},{3,11},{4,12},{5,13},{6,14},{7,15},{8,0},{9,1},... | collective-permute-start | bytes 196616 | tf_op jit(solution)/shard_map/ppermute | solution.py:256
  (8 other events, 21.1 us)

commit v5 on v4

--- a/solution.py
+++ b/solution.py
@@ -208,38 +208,42 @@
             pltpu.SMEM((n, 128), jnp.int32),
             pltpu.SemaphoreType.DMA,
         ],
+        cost_estimate=pl.CostEstimate(flops=1, bytes_accessed=1, transcendentals=0),
         compiler_params=pltpu.CompilerParams(vmem_limit_bytes=VMEM_LIMIT),
         name="spread",
     )(*own, *other, *own, *other)
 
 
-def place_kernel(plan, *refs):
-    n = 2 * plan.places
-    pieces, out, sems = refs[:n], refs[n], refs[n + 1]
+def place_kernel(plans, *refs):
+    n = 2 * plans[0].places
+    inputs, outs, sems = refs[: n * len(plans)], refs[n * len(plans) : -1], refs[-1]
     op, sec = lax.axis_index("op"), lax.axis_index("sec")
-    core, place = op % 2, plan.place(op, sec)
     moving = []
-    for i, piece in enumerate(pieces):
-        rc, m = divmod(i, plan.places)
-        row = pl.multiple_of(((place ^ m) * 2 + (core ^ rc)) * plan.rows, plan.rows)
-        moving.append(pltpu.make_async_copy(piece, out.at[:, pl.ds(row, plan.rows), :], sems.at[i]))
+    for k, (plan, out) in enumerate(zip(plans, outs)):
+        core, place = op % 2, plan.place(op, sec)
+        for i, piece in enumerate(inputs[k * n : (k + 1) * n]):
+            rc, m = divmod(i, plan.places)
+            row = pl.multiple_of(((place ^ m) * 2 + (core ^ rc)) * plan.rows, plan.rows)
+            moving.append(pltpu.make_async_copy(piece, out.at[:, pl.ds(row, plan.rows), :], sems.at[k, i]))
     for copy in moving:
         copy.start()
     for copy in moving:
         copy.wait()
 
 
-def assemble(plan, own, other):
+def assemble(plans, gathered):
+    plan = plans[0]
     pieces = [
         pltpu.with_memory_space_constraint(x.reshape(plan.held, plan.rows, plan.blk), pltpu.VMEM)
+        for own, other in gathered
         for x in (*own, *other)
     ]
     return pl.pallas_call(
-        functools.partial(place_kernel, plan),
+        functools.partial(place_kernel, plans),
         in_specs=[pl.BlockSpec(memory_space=pltpu.VMEM)] * len(pieces),
-        out_specs=pl.BlockSpec(memory_space=pl.ANY),
-        out_shape=jax.ShapeDtypeStruct((plan.held, plan.blk, plan.blk), jnp.bfloat16),
-        scratch_shapes=[pltpu.SemaphoreType.DMA((len(pieces),))],
+        out_specs=[pl.BlockSpec(memory_space=pl.ANY)] * len(plans),
+        out_shape=[jax.ShapeDtypeStruct((plan.held, plan.blk, plan.blk), jnp.bfloat16)] * len(plans),
+        scratch_shapes=[pltpu.SemaphoreType.DMA((len(plans), 2 * plan.places))],
         compiler_params=pltpu.CompilerParams(vmem_limit_bytes=VMEM_LIMIT),
         name="assemble",
     )(*pieces)
@@ -256,38 +260,54 @@
     return [lax.ppermute(x, AXES, plan.swap(1, 0)) for x in own]
 
 
-def finish(plan, away, kept):
-    total = kept.astype(jnp.float32)
-    for k, b in enumerate(plan.bits):
-        arrived = lax.ppermute(away, AXES, plan.swap(0, 1 << b))
-        total = total + arrived.astype(jnp.float32)
-        if k + 1 < len(plan.bits):
-            middle = total.shape[0] // 2
-            away = total[middle:].astype(jnp.bfloat16)
-            total = total[:middle]
+def add(arrived, kept):
+    return kept.astype(jnp.float32) + arrived.astype(jnp.float32)
+
+
+def halves(total):
+    middle = total.shape[0] // 2
+    return total[middle:].astype(jnp.bfloat16), total[:middle]
+
+
+def gather(plan, total):
     total = total.astype(jnp.bfloat16)
     size = plan.held * plan.rows
     extras = 2 ** len(plan.inside)
     sums = [total[e * size : (e + 1) * size] for e in range(extras)]
     own = across(plan, [sums[m % extras] for m in range(plan.places)])
-    return assemble(plan, own, to_core(plan, own))
+    return own, to_core(plan, own)
 
 
 def per_device(mesh, first, second, left, right, source, target):
     terms = left.shape[0]
     order = list(range(mesh.shape["sec"].bit_length() - 1))
-    plan = Plan(mesh, first, terms, order)
-    other_plan = Plan(mesh, first, terms, [order[1], order[0], *order[2:]])
-
-    *pieces, lhs, rhs = contract(plan, True, source, target, left, right, first)
-    early = across(plan, pieces)
-    pieces = contract(other_plan, False, source, target, lhs, rhs, second)
+    plans = [
+        Plan(mesh, first, terms, order),
+        Plan(mesh, first, terms, [order[1], order[0], *order[2:]]),
+    ]
+
+    *pieces, lhs, rhs = contract(plans[0], True, source, target, left, right, first)
+    early = across(plans[0], pieces)
+    pieces = contract(plans[1], False, source, target, lhs, rhs, second)
     early, pieces = lax.optimization_barrier((early, pieces))
-    late = across(other_plan, pieces)
-    away, kept = spread(plan, early, to_core(plan, early))
-    away, late = lax.optimization_barrier((away, late))
-    result = finish(plan, away, kept)
-    return result, finish(other_plan, *spread(other_plan, late, to_core(other_plan, late)))
+    late = across(plans[1], pieces)
+
+    forwarded = to_core(plans[0], early)
+    forwarded, late[-1] = lax.optimization_barrier((forwarded, late[-1]))
+    away, kept = spread(plans[0], early, forwarded)
+    arrived = lax.ppermute(away, AXES, plans[0].swap(0, 1 << plans[0].bits[0]))
+    late_away, late_kept = spread(plans[1], late, to_core(plans[1], late))
+    arrived, late_away = lax.optimization_barrier((arrived, late_away))
+    late_arrived = lax.ppermute(late_away, AXES, plans[1].swap(0, 1 << plans[1].bits[0]))
+
+    for k in range(1, len(plans[0].bits)):
+        away, kept = halves(add(arrived, kept))
+        arrived = lax.ppermute(away, AXES, plans[0].swap(0, 1 << plans[0].bits[k]))
+        away, late_kept = halves(add(late_arrived, late_kept))
+        arrived, away = lax.optimization_barrier((arrived, away))
+        late_arrived = lax.ppermute(away, AXES, plans[1].swap(0, 1 << plans[1].bits[k]))
+    totals = add(arrived, kept), add(late_arrived, late_kept)
+    return tuple(assemble(plans, [gather(plan, total) for plan, total in zip(plans, totals)]))
 
 
 def solution(mesh):

time: 63 us -> 60.9 us (0.967)
  waiting for transfers between devices: 24.5 us -> 23.2 us
    ppermute x12, waiting for transfers between devices: 14.6 us -> 12.3 us  [across(): own[m] = lax.ppermute(pieces[m], AXES, plan.across(m))]
    ppermute x16, waiting for transfers between devices: 0.4 us -> 2.49 us  [to_core(): return [lax.ppermute(x, AXES, plan.swap(1, 0)) for x in own]]
    ppermute x12, starting transfers between devices: 15.6 us -> 17.3 us  [across(): own[m] = lax.ppermute(pieces[m], AXES, plan.across(m))]
    ppermute x4, starting transfers between devices: 6.09 us -> 4.76 us  [the longest x1 2.66 us: per_device(): arrived = lax.ppermute(away, AXES, plans[0].swap(0, 1 << plans[0].bits[k]))]
    ppermute x4, waiting for transfers between devices: 9.48 us -> 8.42 us  [the longest x1 3.78 us: per_device(): lax.ppermute(late_away, AXES, plans[1].swap(0, 1 << plans[1].bits[0]))]
    pallas_call x2 -> x1, Pallas kernels: 1.7 us -> 1.09 us  [assemble(): pl.pallas_call(functools.partial(place_kernel, plans), in_specs=[pl.Block...]
  transfers between devices with their start and end apart: 32 -> 32, of which waited for: 13 -> 18; matrix products, arithmetic and copies ran while one was open for 0% -> 0% of each run, Pallas kernels for 11% -> 10%
where the time goes in v5:
time: 60.9 us; the launch traced here: 60.7 us
  starting transfers between devices  24.1 us (40%)
  waiting for transfers between devices  23.2 us (38%)
  Pallas kernels  12.4 us (20%)
  between operations  0.76 us (1%)
    ppermute x12, starting transfers between devices, across(): own[m] = lax.ppermute(pieces[m], AXES, plan.across(m))  17.3 us
    ppermute x12, waiting for transfers between devices, across(): own[m] = lax.ppermute(pieces[m], AXES, plan.across(m))  12.3 us
    pallas_call x2, Pallas kernels, contract(): pl.pallas_call(functools.partial(contract_kernel, plan, fetch), in_specs=...  9.27 us
    ppermute x1, waiting for transfers between devices, per_device(): lax.ppermute(late_away, AXES, plans[1].swap(0, 1 << plans[1].bits[0]))  3.78 us
    ppermute x1, starting transfers between devices, per_device(): arrived = lax.ppermute(away, AXES, plans[0].swap(0, 1 << plans[0].bits[k]))  2.66 us
    ppermute x16, waiting for transfers between devices, to_core(): return [lax.ppermute(x, AXES, plan.swap(1, 0)) for x in own]  2.49 us
    pallas_call x2, Pallas kernels, spread(): pl.pallas_call(functools.partial(spread_kernel, plan), grid=(1,), in_spec...  2.08 us
    ppermute x16, starting transfers between devices, to_core(): return [lax.ppermute(x, AXES, plan.swap(1, 0)) for x in own]  2.06 us
  transfers between devices with their start and end apart: 32, of which 18 were waited for; matrix products, arithmetic and copies ran while one was open for 0% of the time, Pallas kernels for 10%

profile of v5, /device:TPU:0, one launch (start us, length us, event | category | flops | bytes accessed | tf_op | source)
XLA Modules:
  0.0 60.7 jit_solution(783138888568446912)
XLA Ops:
  0.6 5.5 %contract.2 = (bf16[272,256]{1,0:T(8,128)(2,1)S(1)}, bf16[272,256]{1,0:T(8,128)(2,1)S(1)}, bf16[272,256]{1,0:T(8,128)(2,1)S(1)}, bf16[272,256]{1,0:T(8,128)(2,1)...) custom-call(s32[32]{0:T(128)} %refs_0_.3, s32[32]{0:T(128)} %refs_1_.3, ...), custom_call_target="tpu_custom_call" | custom-call | flops 2147483648 | bytes 8388608 | tf_op jit(solution)/shard_map/contract/pallas_call | solution.py:137
  6.1 3.0 %collective-permute-start = (bf16[272,256]{1,0:T(8,128)(2,1)S(1)}, bf16[272,256]{1,0:T(8,128)(2,1)S(1)}, u32[]{:S(2)}, u32[]{:S(2)}) collective-permute-start(bf16[272,256]{1,0:T(8,128)(2,1)S(1)} %get-tuple-element.34), channel_id=1, source_target_pairs={{0,1},{1,0},{2,3},{3,2},{4,5},{5,4},{6,7},{7,6},{8,9},{9,8},{10,11... | collective-permute-start | bytes 417800 | tf_op jit(solution)/shard_map/ppermute | solution.py:255
  9.1 1.5 %collective-permute-start.1 = (bf16[272,256]{1,0:T(8,128)(2,1)S(1)}, bf16[272,256]{1,0:T(8,128)(2,1)S(1)}, u32[]{:S(2)}, u32[]{:S(2)}) collective-permute-start(bf16[272,256]{1,0:T(8,128)(2,1)S(1)} %get-tuple-element.35), channel_id=1, source_target_pairs={{0,16},{1,17},{2,18},{3,19},{4,20},{5,21},{6,22},{7,23},{8,24},{9,... | collective-permute-start | bytes 417800 | tf_op jit(solution)/shard_map/ppermute | solution.py:255
  10.7 3.8 %contract.3 = (bf16[272,256]{1,0:T(8,128)(2,1)S(1)}, bf16[272,256]{1,0:T(8,128)(2,1)S(1)}, bf16[272,256]{1,0:T(8,128)(2,1)S(1)}, bf16[272,256]{1,0:T(8,128)(2,1)S(1)}) custom-call(s32[32]{0:T(128)} %refs_0_.3, s32[32]{0:T(128)} %refs_1_.3, bf16[32,256,256]{2,1,0:T(8,128)(2,1)S(1)} %get-tuple-element.37.refs_2_, ...), custom_call_target="tpu_custom_call" | custom-call | flops 2147483648 | bytes 8192 | tf_op jit(solution)/shard_map/contract/pallas_call | solution.py:137
  14.5 2.8 %collective-permute-done.1.refs_2_.refs_10_ = bf16[272,256]{1,0:T(8,128)(2,1)S(1)} collective-permute-done((bf16[272,256]{1,0:T(8,128)(2,1)S(1)}, bf16[272,256]{1,0:T(8,128)(2,1)S(1)}, u32[]{:S(2)}, u32[]{:S(2)}) %collective-permute-start.1) | collective-permute-done | bytes 139296 | tf_op jit(solution)/shard_map/ppermute | solution.py:255
  17.2 2.5 %collective-permute-start.7 = (bf16[272,256]{1,0:T(8,128)(2,1)S(1)}, bf16[272,256]{1,0:T(8,128)(2,1)S(1)}, u32[]{:S(2)}, u32[]{:S(2)}) collective-permute-start(bf16[272,256]{1,0:T(8,128)(2,1)S(1)} %get-tuple-element.47), channel_id=1, source_target_pairs={{0,18},{1,19},{2,16},{3,17},{4,22},{5,23},{6,20},{7,21},{8,26},{9,... | collective-permute-start | bytes 417800 | tf_op jit(solution)/shard_map/ppermute | solution.py:255
  20.8 2.4 %collective-permute-done.7.refs_3_.refs_11_ = bf16[272,256]{1,0:T(8,128)(2,1)S(1)} collective-permute-done((bf16[272,256]{1,0:T(8,128)(2,1)S(1)}, bf16[272,256]{1,0:T(8,128)(2,1)S(1)}, u32[]{:S(2)}, u32[]{:S(2)}) %collective-permute-start.7) | collective-permute-done | bytes 139296 | tf_op jit(solution)/shard_map/ppermute | solution.py:255
  23.2 1.6 %collective-permute-start.9 = (bf16[272,256]{1,0:T(8,128)(2,1)S(1)}, bf16[272,256]{1,0:T(8,128)(2,1)S(1)}, u32[]{:S(2)}, u32[]{:S(2)}) collective-permute-start(bf16[272,256]{1,0:T(8,128)(2,1)S(1)} %get-tuple-element.55), channel_id=1, source_target_pairs={{0,2},{1,3},{2,0},{3,1},{4,6},{5,7},{6,4},{7,5},{8,10},{9,11},{10,... | collective-permute-start | bytes 417800 | tf_op jit(solution)/shard_map/ppermute | solution.py:255
  24.8 1.5 %collective-permute-start.10 = (bf16[272,256]{1,0:T(8,128)(2,1)S(1)}, bf16[272,256]{1,0:T(8,128)(2,1)S(1)}, u32[]{:S(2)}, u32[]{:S(2)}) collective-permute-start(bf16[272,256]{1,0:T(8,128)(2,1)S(1)} %get-tuple-element.56), channel_id=1, source_target_pairs={{0,16},{1,17},{2,18},{3,19},{4,20},{5,21},{6,22},{7,23},{8,24},{9,... | collective-permute-start | bytes 417800 | tf_op jit(solution)/shard_map/ppermute | solution.py:255
  26.3 1.0 %spread.2 = (bf16[512,256]{1,0:T(8,128)(2,1)S(1)}, bf16[512,256]{1,0:T(8,128)(2,1)S(1)}) custom-call(bf16[272,256]{1,0:T(8,128)(2,1)S(1)} %get-tuple-element.43.refs_0_.refs_8_, bf16[272,256]{1,0:T(8,128)(2,1)S(1)} %collective-permute-done.refs_1_.refs_9_, bf16[272,256]{1,0:T(8,128)(2,1)S(1)} %collective-permute-done.1.refs_2_.refs_10_, ...), custom_call_target="tpu_custom_call" | custom-call | flops 1 | bytes 1 | tf_op jit(solution)/shard_map/spread/pallas_call | solution.py:199
  27.9 1.8 %collective-permute-done.9.refs_1_.refs_9_ = bf16[272,256]{1,0:T(8,128)(2,1)S(1)} collective-permute-done((bf16[272,256]{1,0:T(8,128)(2,1)S(1)}, bf16[272,256]{1,0:T(8,128)(2,1)S(1)}, u32[]{:S(2)}, u32[]{:S(2)}) %collective-permute-start.9) | collective-permute-done | bytes 139296 | tf_op jit(solution)/shard_map/ppermute | solution.py:255
  31.6 1.0 %spread.3 = (bf16[512,256]{1,0:T(8,128)(2,1)S(1)}, bf16[512,256]{1,0:T(8,128)(2,1)S(1)}) custom-call(bf16[272,256]{1,0:T(8,128)(2,1)S(1)} %get-tuple-element.54.refs_0_.refs_8_, bf16[272,256]{1,0:T(8,128)(2,1)S(1)} %collective-permute-done.9.refs_1_.refs_9_, bf16[272,256]{1,0:T(8,128)(2,1)S(1)} %collective-permute-done.10.refs_2_.refs_10_, ...), custom_call_target="tpu_custom_call" | custom-call | flops 1 | bytes 1 | tf_op jit(solution)/shard_map/spread/pallas_call | solution.py:199
  32.6 1.2 %collective-permute-done.8 = bf16[512,256]{1,0:T(8,128)(2,1)S(1)} collective-permute-done((bf16[512,256]{1,0:T(8,128)(2,1)S(1)}, bf16[512,256]{1,0:T(8,128)(2,1)S(1)}, u32[]{:S(2)}, u32[]{:S(2)}) %collective-permute-start.8) | collective-permute-done | bytes 262176 | tf_op jit(solution)/shard_map/ppermute | solution.py:298
  34.7 2.7 %collective-permute-start.15 = (bf16[256,256]{1,0:T(8,128)(2,1)S(1)}, bf16[256,256]{1,0:T(8,128)(2,1)S(1)}, u32[]{:S(2)}, u32[]{:S(2)}) collective-permute-start(bf16[256,256]{1,0:T(8,128)(2,1)S(1)} %slice.51), channel_id=1, source_target_pairs={{0,4},{1,5},{2,6},{3,7},{4,0},{5,1},{6,2},{7,3},{8,12},{9,13},{10,... | collective-permute-start | bytes 393224 | tf_op jit(solution)/shard_map/ppermute | solution.py:305
  37.3 3.8 %collective-permute-done.16 = bf16[512,256]{1,0:T(8,128)(2,1)S(1)} collective-permute-done((bf16[512,256]{1,0:T(8,128)(2,1)S(1)}, bf16[512,256]{1,0:T(8,128)(2,1)S(1)}, u32[]{:S(2)}, u32[]{:S(2)}) %collective-permute-start.16) | collective-permute-done | bytes 262176 | tf_op jit(solution)/shard_map/ppermute | solution.py:301
  41.2 1.9 %collective-permute-done.15 = bf16[256,256]{1,0:T(8,128)(2,1)S(1)} collective-permute-done((bf16[256,256]{1,0:T(8,128)(2,1)S(1)}, bf16[256,256]{1,0:T(8,128)(2,1)S(1)}, u32[]{:S(2)}, u32[]{:S(2)}) %collective-permute-start.15) | collective-permute-done | bytes 131104 | tf_op jit(solution)/shard_map/ppermute | solution.py:305
  43.9 1.5 %collective-permute-start.19 = (bf16[128,256]{1,0:T(8,128)(2,1)S(1)}, bf16[128,256]{1,0:T(8,128)(2,1)S(1)}, u32[]{:S(2)}, u32[]{:S(2)}) collective-permute-start(bf16[128,256]{1,0:T(8,128)(2,1)S(1)} %get-tuple-element.66), channel_id=1, source_target_pairs={{0,17},{1,16},{2,19},{3,18},{4,21},{5,20},{6,23},{7,22},{8,25},{9,... | collective-permute-start | bytes 196616 | tf_op jit(solution)/shard_map/ppermute | solution.py:255
  45.4 1.6 %collective-permute-start.17 = (bf16[128,256]{1,0:T(8,128)(2,1)S(1)}, bf16[128,256]{1,0:T(8,128)(2,1)S(1)}, u32[]{:S(2)}, u32[]{:S(2)}) collective-permute-start(bf16[128,256]{1,0:T(8,128)(2,1)S(1)} %get-tuple-element.66), channel_id=1, source_target_pairs={{0,1},{1,0},{2,3},{3,2},{4,5},{5,4},{6,7},{7,6},{8,9},{9,8},{10,11... | collective-permute-start | bytes 196616 | tf_op jit(solution)/shard_map/ppermute | solution.py:255
  47.5 1.7 %collective-permute-done.19 = bf16[128,256]{1,0:T(8,128)(2,1)S(1)} collective-permute-done((bf16[128,256]{1,0:T(8,128)(2,1)S(1)}, bf16[128,256]{1,0:T(8,128)(2,1)S(1)}, u32[]{:S(2)}, u32[]{:S(2)}) %collective-permute-start.19) | collective-permute-done | bytes 65568 | tf_op jit(solution)/shard_map/ppermute | solution.py:255
  49.9 1.6 %collective-permute-done.24 = bf16[256,256]{1,0:T(8,128)(2,1)S(1)} collective-permute-done((bf16[256,256]{1,0:T(8,128)(2,1)S(1)}, bf16[256,256]{1,0:T(8,128)(2,1)S(1)}, u32[]{:S(2)}, u32[]{:S(2)}) %collective-permute-start.24) | collective-permute-done | bytes 131104 | tf_op jit(solution)/shard_map/ppermute | solution.py:308
  51.6 2.0 %collective-permute-start.27 = (bf16[128,256]{1,0:T(8,128)(2,1)S(1)}, bf16[128,256]{1,0:T(8,128)(2,1)S(1)}, u32[]{:S(2)}, u32[]{:S(2)}) collective-permute-start(bf16[128,256]{1,0:T(8,128)(2,1)S(1)} %get-tuple-element.64), channel_id=1, source_target_pairs={{0,18},{1,19},{2,16},{3,17},{4,22},{5,23},{6,20},{7,21},{8,26},{9,... | collective-permute-start | bytes 196616 | tf_op jit(solution)/shard_map/ppermute | solution.py:255
  54.1 1.0 %collective-permute-start.26 = (bf16[128,256]{1,0:T(8,128)(2,1)S(1)}, bf16[128,256]{1,0:T(8,128)(2,1)S(1)}, u32[]{:S(2)}, u32[]{:S(2)}) collective-permute-start(bf16[128,256]{1,0:T(8,128)(2,1)S(1)} %get-tuple-element.65), channel_id=1, source_target_pairs={{0,16},{1,17},{2,18},{3,19},{4,20},{5,21},{6,22},{7,23},{8,24},{9,... | collective-permute-start | bytes 196616 | tf_op jit(solution)/shard_map/ppermute | solution.py:255
  55.6 1.2 %collective-permute-done.27 = bf16[128,256]{1,0:T(8,128)(2,1)S(1)} collective-permute-done((bf16[128,256]{1,0:T(8,128)(2,1)S(1)}, bf16[128,256]{1,0:T(8,128)(2,1)S(1)}, u32[]{:S(2)}, u32[]{:S(2)}) %collective-permute-start.27) | collective-permute-done | bytes 65568 | tf_op jit(solution)/shard_map/ppermute | solution.py:255
  59.6 1.1 %assemble.1 = (bf16[4,256,256]{2,1,0:T(8,128)(2,1)}, bf16[4,256,256]{2,1,0:T(8,128)(2,1)}) custom-call(bf16[4,32,256]{2,1,0:T(8,128)(2,1)S(1)} %bitcast.16, bf16[4,32,256]{2,1,0:T(8,128)(2,1)S(1)} %bitcast.19, bf16[4,32,256]{2,1,0:T(8,128)(2,1)S(1)} %bitcast.21, bf16[4,32,256]{2,1,0:T(8,128)(2,1)S(1)} %bitcast.18, bf16[4,32,256]{2,1,0:T(8,128)(2,1)S(1)} %bitcast.20, ...), custom_call_target="tpu_custom_call" | custom-call | tf_op jit(solution)/shard_map/assemble/pallas_call | solution.py:241
  (53 shorter events, 10.4 us)
Async XLA Ops:
  6.1 8.3 %collective-permute-start = (bf16[272,256]{1,0:T(8,128)(2,1)S(1)}, bf16[272,256]{1,0:T(8,128)(2,1)S(1)}, u32[]{:S(2)}, u32[]{:S(2)}) collective-permute-start(bf16[272,256]{1,0:T(8,128)(2,1)S(1)} %get-tuple-element.34), channel_id=1, source_target_pairs={{0,1},{1,0},{2,3},{3,2},{4,5},{5,4},{6,7},{7,6},{8,9},{9,8},{10,11... | collective-permute-start | bytes 417800 | tf_op jit(solution)/shard_map/ppermute | solution.py:255
  9.1 8.1 %collective-permute-start.1 = (bf16[272,256]{1,0:T(8,128)(2,1)S(1)}, bf16[272,256]{1,0:T(8,128)(2,1)S(1)}, u32[]{:S(2)}, u32[]{:S(2)}) collective-permute-start(bf16[272,256]{1,0:T(8,128)(2,1)S(1)} %get-tuple-element.35), channel_id=1, source_target_pairs={{0,16},{1,17},{2,18},{3,19},{4,20},{5,21},{6,22},{7,23},{8,24},{9,... | collective-permute-start | bytes 417800 | tf_op jit(solution)/shard_map/ppermute | solution.py:255
  10.6 6.6 %collective-permute-start.2 = (bf16[272,256]{1,0:T(8,128)(2,1)S(1)}, bf16[272,256]{1,0:T(8,128)(2,1)S(1)}, u32[]{:S(2)}, u32[]{:S(2)}) collective-permute-start(bf16[272,256]{1,0:T(8,128)(2,1)S(1)} %get-tuple-element.36), channel_id=1, source_target_pairs={{0,17},{1,16},{2,19},{3,18},{4,21},{5,20},{6,23},{7,22},{8,25},{9,... | collective-permute-start | bytes 417800 | tf_op jit(solution)/shard_map/ppermute | solution.py:255
  17.2 6.0 %collective-permute-start.7 = (bf16[272,256]{1,0:T(8,128)(2,1)S(1)}, bf16[272,256]{1,0:T(8,128)(2,1)S(1)}, u32[]{:S(2)}, u32[]{:S(2)}) collective-permute-start(bf16[272,256]{1,0:T(8,128)(2,1)S(1)} %get-tuple-element.47), channel_id=1, source_target_pairs={{0,18},{1,19},{2,16},{3,17},{4,22},{5,23},{6,20},{7,21},{8,26},{9,... | collective-permute-start | bytes 417800 | tf_op jit(solution)/shard_map/ppermute | solution.py:255
  19.8 5.0 %collective-permute-start.3 = (bf16[272,256]{1,0:T(8,128)(2,1)S(1)}, bf16[272,256]{1,0:T(8,128)(2,1)S(1)}, u32[]{:S(2)}, u32[]{:S(2)}) collective-permute-start(bf16[272,256]{1,0:T(8,128)(2,1)S(1)} %get-tuple-element.43.refs_0_.refs_8_), channel_id=1, source_target_pairs={{0,8},{1,9},{2,10},{3,11},{4,12},{5,13},{6,14},{7,15},{8,0},{9,1},... | collective-permute-start | bytes 417800 | tf_op jit(solution)/shard_map/ppermute | solution.py:260
  19.8 6.5 %collective-permute-start.4 = (bf16[272,256]{1,0:T(8,128)(2,1)S(1)}, bf16[272,256]{1,0:T(8,128)(2,1)S(1)}, u32[]{:S(2)}, u32[]{:S(2)}) collective-permute-start(bf16[272,256]{1,0:T(8,128)(2,1)S(1)} %collective-permute-done.refs_1_.refs_9_), channel_id=1, source_target_pairs={{0,8},{1,9},{2,10},{3,11},{4,12},{5,13},{6,14},{7,15},{8,0},{9,1},... | collective-permute-start | bytes 417800 | tf_op jit(solution)/shard_map/ppermute | solution.py:260
  20.3 6.0 %collective-permute-start.5 = (bf16[272,256]{1,0:T(8,128)(2,1)S(1)}, bf16[272,256]{1,0:T(8,128)(2,1)S(1)}, u32[]{:S(2)}, u32[]{:S(2)}) collective-permute-start(bf16[272,256]{1,0:T(8,128)(2,1)S(1)} %collective-permute-done.1.refs_2_.refs_10_), channel_id=1, source_target_pairs={{0,8},{1,9},{2,10},{3,11},{4,12},{5,13},{6,14},{7,15},{8,0},{9,1},... | collective-permute-start | bytes 417800 | tf_op jit(solution)/shard_map/ppermute | solution.py:260
  20.3 6.0 %collective-permute-start.6 = (bf16[272,256]{1,0:T(8,128)(2,1)S(1)}, bf16[272,256]{1,0:T(8,128)(2,1)S(1)}, u32[]{:S(2)}, u32[]{:S(2)}) collective-permute-start(bf16[272,256]{1,0:T(8,128)(2,1)S(1)} %collective-permute-done.2.refs_3_.refs_11_), channel_id=1, source_target_pairs={{0,8},{1,9},{2,10},{3,11},{4,12},{5,13},{6,14},{7,15},{8,0},{9,1},... | collective-permute-start | bytes 417800 | tf_op jit(solution)/shard_map/ppermute | solution.py:260
  23.2 6.5 %collective-permute-start.9 = (bf16[272,256]{1,0:T(8,128)(2,1)S(1)}, bf16[272,256]{1,0:T(8,128)(2,1)S(1)}, u32[]{:S(2)}, u32[]{:S(2)}) collective-permute-start(bf16[272,256]{1,0:T(8,128)(2,1)S(1)} %get-tuple-element.55), channel_id=1, source_target_pairs={{0,2},{1,3},{2,0},{3,1},{4,6},{5,7},{6,4},{7,5},{8,10},{9,11},{10,... | collective-permute-start | bytes 417800 | tf_op jit(solution)/shard_map/ppermute | solution.py:255
  24.8 5.1 %collective-permute-start.10 = (bf16[272,256]{1,0:T(8,128)(2,1)S(1)}, bf16[272,256]{1,0:T(8,128)(2,1)S(1)}, u32[]{:S(2)}, u32[]{:S(2)}) collective-permute-start(bf16[272,256]{1,0:T(8,128)(2,1)S(1)} %get-tuple-element.56), channel_id=1, source_target_pairs={{0,16},{1,17},{2,18},{3,19},{4,20},{5,21},{6,22},{7,23},{8,24},{9,... | collective-permute-start | bytes 417800 | tf_op jit(solution)/shard_map/ppermute | solution.py:255
  27.4 6.4 %collective-permute-start.8 = (bf16[512,256]{1,0:T(8,128)(2,1)S(1)}, bf16[512,256]{1,0:T(8,128)(2,1)S(1)}, u32[]{:S(2)}, u32[]{:S(2)}) collective-permute-start(bf16[512,256]{1,0:T(8,128)(2,1)S(1)} %get-tuple-element.53), channel_id=1, source_target_pairs={{0,2},{1,3},{2,0},{3,1},{4,6},{5,7},{6,4},{7,5},{8,10},{9,11},{10,... | collective-permute-start | bytes 786440 | tf_op jit(solution)/shard_map/ppermute | solution.py:298
  33.8 7.3 %collective-permute-start.16 = (bf16[512,256]{1,0:T(8,128)(2,1)S(1)}, bf16[512,256]{1,0:T(8,128)(2,1)S(1)}, u32[]{:S(2)}, u32[]{:S(2)}) collective-permute-start(bf16[512,256]{1,0:T(8,128)(2,1)S(1)} %get-tuple-element.61), channel_id=1, source_target_pairs={{0,1},{1,0},{2,3},{3,2},{4,5},{5,4},{6,7},{7,6},{8,9},{9,8},{10,11... | collective-permute-start | bytes 786440 | tf_op jit(solution)/shard_map/ppermute | solution.py:301
  34.7 8.4 %collective-permute-start.15 = (bf16[256,256]{1,0:T(8,128)(2,1)S(1)}, bf16[256,256]{1,0:T(8,128)(2,1)S(1)}, u32[]{:S(2)}, u32[]{:S(2)}) collective-permute-start(bf16[256,256]{1,0:T(8,128)(2,1)S(1)} %slice.51), channel_id=1, source_target_pairs={{0,4},{1,5},{2,6},{3,7},{4,0},{5,1},{6,2},{7,3},{8,12},{9,13},{10,... | collective-permute-start | bytes 393224 | tf_op jit(solution)/shard_map/ppermute | solution.py:305
  43.1 8.4 %collective-permute-start.24 = (bf16[256,256]{1,0:T(8,128)(2,1)S(1)}, bf16[256,256]{1,0:T(8,128)(2,1)S(1)}, u32[]{:S(2)}, u32[]{:S(2)}) collective-permute-start(bf16[256,256]{1,0:T(8,128)(2,1)S(1)} %slice.50), channel_id=1, source_target_pairs={{0,4},{1,5},{2,6},{3,7},{4,0},{5,1},{6,2},{7,3},{8,12},{9,13},{10,... | collective-permute-start | bytes 393224 | tf_op jit(solution)/shard_map/ppermute | solution.py:308
  43.9 5.2 %collective-permute-start.19 = (bf16[128,256]{1,0:T(8,128)(2,1)S(1)}, bf16[128,256]{1,0:T(8,128)(2,1)S(1)}, u32[]{:S(2)}, u32[]{:S(2)}) collective-permute-start(bf16[128,256]{1,0:T(8,128)(2,1)S(1)} %get-tuple-element.66), channel_id=1, source_target_pairs={{0,17},{1,16},{2,19},{3,18},{4,21},{5,20},{6,23},{7,22},{8,25},{9,... | collective-permute-start | bytes 196616 | tf_op jit(solution)/shard_map/ppermute | solution.py:255
  45.4 4.5 %collective-permute-start.17 = (bf16[128,256]{1,0:T(8,128)(2,1)S(1)}, bf16[128,256]{1,0:T(8,128)(2,1)S(1)}, u32[]{:S(2)}, u32[]{:S(2)}) collective-permute-start(bf16[128,256]{1,0:T(8,128)(2,1)S(1)} %get-tuple-element.66), channel_id=1, source_target_pairs={{0,1},{1,0},{2,3},{3,2},{4,5},{5,4},{6,7},{7,6},{8,9},{9,8},{10,11... | collective-permute-start | bytes 196616 | tf_op jit(solution)/shard_map/ppermute | solution.py:255
  47.0 6.5 %collective-permute-start.20 = (bf16[128,256]{1,0:T(8,128)(2,1)S(1)}, bf16[128,256]{1,0:T(8,128)(2,1)S(1)}, u32[]{:S(2)}, u32[]{:S(2)}) collective-permute-start(bf16[128,256]{1,0:T(8,128)(2,1)S(1)} %get-tuple-element.67), channel_id=1, source_target_pairs={{0,8},{1,9},{2,10},{3,11},{4,12},{5,13},{6,14},{7,15},{8,0},{9,1},... | collective-permute-start | bytes 196616 | tf_op jit(solution)/shard_map/ppermute | solution.py:260
  47.0 7.2 %collective-permute-start.18 = (bf16[128,256]{1,0:T(8,128)(2,1)S(1)}, bf16[128,256]{1,0:T(8,128)(2,1)S(1)}, u32[]{:S(2)}, u32[]{:S(2)}) collective-permute-start(bf16[128,256]{1,0:T(8,128)(2,1)S(1)} %get-tuple-element.67), channel_id=1, source_target_pairs={{0,16},{1,17},{2,18},{3,19},{4,20},{5,21},{6,22},{7,23},{8,24},{9,... | collective-permute-start | bytes 196616 | tf_op jit(solution)/shard_map/ppermute | solution.py:255
  49.1 6.0 %collective-permute-start.23 = (bf16[128,256]{1,0:T(8,128)(2,1)S(1)}, bf16[128,256]{1,0:T(8,128)(2,1)S(1)}, u32[]{:S(2)}, u32[]{:S(2)}) collective-permute-start(bf16[128,256]{1,0:T(8,128)(2,1)S(1)} %collective-permute-done.19), channel_id=1, source_target_pairs={{0,8},{1,9},{2,10},{3,11},{4,12},{5,13},{6,14},{7,15},{8,0},{9,1},... | collective-permute-start | bytes 196616 | tf_op jit(solution)/shard_map/ppermute | solution.py:260
  49.9 5.2 %collective-permute-start.21 = (bf16[128,256]{1,0:T(8,128)(2,1)S(1)}, bf16[128,256]{1,0:T(8,128)(2,1)S(1)}, u32[]{:S(2)}, u32[]{:S(2)}) collective-permute-start(bf16[128,256]{1,0:T(8,128)(2,1)S(1)} %collective-permute-done.17), channel_id=1, source_target_pairs={{0,8},{1,9},{2,10},{3,11},{4,12},{5,13},{6,14},{7,15},{8,0},{9,1},... | collective-permute-start | bytes 196616 | tf_op jit(solution)/shard_map/ppermute | solution.py:260
  51.6 5.3 %collective-permute-start.27 = (bf16[128,256]{1,0:T(8,128)(2,1)S(1)}, bf16[128,256]{1,0:T(8,128)(2,1)S(1)}, u32[]{:S(2)}, u32[]{:S(2)}) collective-permute-start(bf16[128,256]{1,0:T(8,128)(2,1)S(1)} %get-tuple-element.64), channel_id=1, source_target_pairs={{0,18},{1,19},{2,16},{3,17},{4,22},{5,23},{6,20},{7,21},{8,26},{9,... | collective-permute-start | bytes 196616 | tf_op jit(solution)/shard_map/ppermute | solution.py:255
  53.5 4.3 %collective-permute-start.25 = (bf16[128,256]{1,0:T(8,128)(2,1)S(1)}, bf16[128,256]{1,0:T(8,128)(2,1)S(1)}, u32[]{:S(2)}, u32[]{:S(2)}) collective-permute-start(bf16[128,256]{1,0:T(8,128)(2,1)S(1)} %get-tuple-element.64), channel_id=1, source_target_pairs={{0,2},{1,3},{2,0},{3,1},{4,6},{5,7},{6,4},{7,5},{8,10},{9,11},{10,... | collective-permute-start | bytes 196616 | tf_op jit(solution)/shard_map/ppermute | solution.py:255
  54.1 4.3 %collective-permute-start.26 = (bf16[128,256]{1,0:T(8,128)(2,1)S(1)}, bf16[128,256]{1,0:T(8,128)(2,1)S(1)}, u32[]{:S(2)}, u32[]{:S(2)}) collective-permute-start(bf16[128,256]{1,0:T(8,128)(2,1)S(1)} %get-tuple-element.65), channel_id=1, source_target_pairs={{0,16},{1,17},{2,18},{3,19},{4,20},{5,21},{6,22},{7,23},{8,24},{9,... | collective-permute-start | bytes 196616 | tf_op jit(solution)/shard_map/ppermute | solution.py:255
  55.1 3.3 %collective-permute-start.22 = (bf16[128,256]{1,0:T(8,128)(2,1)S(1)}, bf16[128,256]{1,0:T(8,128)(2,1)S(1)}, u32[]{:S(2)}, u32[]{:S(2)}) collective-permute-start(bf16[128,256]{1,0:T(8,128)(2,1)S(1)} %collective-permute-done.18), channel_id=1, source_target_pairs={{0,8},{1,9},{2,10},{3,11},{4,12},{5,13},{6,14},{7,15},{8,0},{9,1},... | collective-permute-start | bytes 196616 | tf_op jit(solution)/shard_map/ppermute | solution.py:260
  (8 other events, 14.0 us)

commit v6 on v5

--- a/solution.py
+++ b/solution.py
@@ -260,6 +260,10 @@
     return [lax.ppermute(x, AXES, plan.swap(1, 0)) for x in own]
 
 
+def after(x, y):
+    return lax.optimization_barrier((x, y))[0]
+
+
 def add(arrived, kept):
     return kept.astype(jnp.float32) + arrived.astype(jnp.float32)
 
@@ -289,22 +293,23 @@
     *pieces, lhs, rhs = contract(plans[0], True, source, target, left, right, first)
     early = across(plans[0], pieces)
     pieces = contract(plans[1], False, source, target, lhs, rhs, second)
-    early, pieces = lax.optimization_barrier((early, pieces))
+    early = after(early, pieces)
     late = across(plans[1], pieces)
 
     forwarded = to_core(plans[0], early)
-    forwarded, late[-1] = lax.optimization_barrier((forwarded, late[-1]))
+    forwarded = after(forwarded, late[-1])
     away, kept = spread(plans[0], early, forwarded)
     arrived = lax.ppermute(away, AXES, plans[0].swap(0, 1 << plans[0].bits[0]))
+    late = after(late, away)
     late_away, late_kept = spread(plans[1], late, to_core(plans[1], late))
-    arrived, late_away = lax.optimization_barrier((arrived, late_away))
+    arrived = after(arrived, late_away)
     late_arrived = lax.ppermute(late_away, AXES, plans[1].swap(0, 1 << plans[1].bits[0]))
 
     for k in range(1, len(plans[0].bits)):
         away, kept = halves(add(arrived, kept))
         arrived = lax.ppermute(away, AXES, plans[0].swap(0, 1 << plans[0].bits[k]))
         away, late_kept = halves(add(late_arrived, late_kept))
-        arrived, away = lax.optimization_barrier((arrived, away))
+        arrived = after(arrived, away)
         late_arrived = lax.ppermute(away, AXES, plans[1].swap(0, 1 << plans[1].bits[k]))
     totals = add(arrived, kept), add(late_arrived, late_kept)
     return tuple(assemble(plans, [gather(plan, total) for plan, total in zip(plans, totals)]))

time: 60.9 us -> 58.3 us (0.957)
  waiting for transfers between devices: 23.2 us -> 16.1 us
  starting transfers between devices: 24.1 us -> 28.6 us
    ppermute x12, waiting for transfers between devices: 12.3 us -> 9.48 us  [across(): own[m] = lax.ppermute(pieces[m], AXES, plan.across(m))]
    ppermute x1, waiting for transfers between devices: 1.89 us -> 0.01 us  [per_device(): arrived = lax.ppermute(away, AXES, plans[0].swap(0, 1 << plans[0].bits[k]))]
    ppermute x1, starting transfers between devices: 0.79 us -> 2.65 us  [per_device(): lax.ppermute(away, AXES, plans[1].swap(0, 1 << plans[1].bits[k]))]
    ppermute x1, waiting for transfers between devices: 1.58 us -> 0.01 us  [per_device(): lax.ppermute(away, AXES, plans[1].swap(0, 1 << plans[1].bits[k]))]
    ppermute x1, waiting for transfers between devices: 1.17 us -> 0.01 us  [per_device(): arrived = lax.ppermute(away, AXES, plans[0].swap(0, 1 << plans[0].bits[0]))]
    ppermute x16, starting transfers between devices: 2.06 us -> 3.04 us  [to_core(): return [lax.ppermute(x, AXES, plan.swap(1, 0)) for x in own]]
    ppermute x12, starting transfers between devices: 17.3 us -> 18.2 us  [across(): own[m] = lax.ppermute(pieces[m], AXES, plan.across(m))]
    ppermute x1, starting transfers between devices: 0.79 us -> 1.56 us  [per_device(): lax.ppermute(late_away, AXES, plans[1].swap(0, 1 << plans[1].bits[0]))]
  transfers between devices with their start and end apart: 32 -> 32, of which waited for: 18 -> 16; matrix products, arithmetic and copies ran while one was open for 0% -> 0% of each run, Pallas kernels for 10% -> 10%
where the time goes in v6:
time: 58.3 us; the launch traced here: 58.1 us
  starting transfers between devices  28.6 us (49%)
  waiting for transfers between devices  16.1 us (28%)
  Pallas kernels  12.4 us (21%)
  between operations  0.76 us (1%)
    ppermute x12, starting transfers between devices, across(): own[m] = lax.ppermute(pieces[m], AXES, plan.across(m))  18.2 us
    ppermute x12, waiting for transfers between devices, across(): own[m] = lax.ppermute(pieces[m], AXES, plan.across(m))  9.48 us
    pallas_call x2, Pallas kernels, contract(): pl.pallas_call(functools.partial(contract_kernel, plan, fetch), in_specs=...  9.27 us
    ppermute x1, waiting for transfers between devices, per_device(): lax.ppermute(late_away, AXES, plans[1].swap(0, 1 << plans[1].bits[0]))  4.29 us
    ppermute x16, starting transfers between devices, to_core(): return [lax.ppermute(x, AXES, plan.swap(1, 0)) for x in own]  3.04 us
    ppermute x1, starting transfers between devices, per_device(): lax.ppermute(away, AXES, plans[1].swap(0, 1 << plans[1].bits[k]))  2.65 us
    ppermute x1, starting transfers between devices, per_device(): arrived = lax.ppermute(away, AXES, plans[0].swap(0, 1 << plans[0].bits[k]))  2.65 us
    ppermute x16, waiting for transfers between devices, to_core(): return [lax.ppermute(x, AXES, plan.swap(1, 0)) for x in own]  2.31 us
  transfers between devices with their start and end apart: 32, of which 16 were waited for; matrix products, arithmetic and copies ran while one was open for 0% of the time, Pallas kernels for 10%

profile of v6, /device:TPU:0, one launch (start us, length us, event | category | flops | bytes accessed | tf_op | source)
XLA Modules:
  0.0 58.1 jit_solution(15797365236595376042)
XLA Ops:
  0.6 5.5 %contract.2 = (bf16[272,256]{1,0:T(8,128)(2,1)S(1)}, bf16[272,256]{1,0:T(8,128)(2,1)S(1)}, bf16[272,256]{1,0:T(8,128)(2,1)S(1)}, bf16[272,256]{1,0:T(8,128)(2,1)...) custom-call(s32[32]{0:T(128)} %refs_0_.3, s32[32]{0:T(128)} %refs_1_.3, ...), custom_call_target="tpu_custom_call" | custom-call | flops 2147483648 | bytes 8388608 | tf_op jit(solution)/shard_map/contract/pallas_call | solution.py:137
  6.1 3.0 %collective-permute-start = (bf16[272,256]{1,0:T(8,128)(2,1)S(1)}, bf16[272,256]{1,0:T(8,128)(2,1)S(1)}, u32[]{:S(2)}, u32[]{:S(2)}) collective-permute-start(bf16[272,256]{1,0:T(8,128)(2,1)S(1)} %get-tuple-element.31), channel_id=1, source_target_pairs={{0,1},{1,0},{2,3},{3,2},{4,5},{5,4},{6,7},{7,6},{8,9},{9,8},{10,11... | collective-permute-start | bytes 417800 | tf_op jit(solution)/shard_map/ppermute | solution.py:255
  9.1 1.5 %collective-permute-start.1 = (bf16[272,256]{1,0:T(8,128)(2,1)S(1)}, bf16[272,256]{1,0:T(8,128)(2,1)S(1)}, u32[]{:S(2)}, u32[]{:S(2)}) collective-permute-start(bf16[272,256]{1,0:T(8,128)(2,1)S(1)} %get-tuple-element.32), channel_id=1, source_target_pairs={{0,16},{1,17},{2,18},{3,19},{4,20},{5,21},{6,22},{7,23},{8,24},{9,... | collective-permute-start | bytes 417800 | tf_op jit(solution)/shard_map/ppermute | solution.py:255
  10.7 3.8 %contract.3 = (bf16[272,256]{1,0:T(8,128)(2,1)S(1)}, bf16[272,256]{1,0:T(8,128)(2,1)S(1)}, bf16[272,256]{1,0:T(8,128)(2,1)S(1)}, bf16[272,256]{1,0:T(8,128)(2,1)S(1)}) custom-call(s32[32]{0:T(128)} %refs_0_.3, s32[32]{0:T(128)} %refs_1_.3, bf16[32,256,256]{2,1,0:T(8,128)(2,1)S(1)} %get-tuple-element.34.refs_2_, ...), custom_call_target="tpu_custom_call" | custom-call | flops 2147483648 | bytes 8192 | tf_op jit(solution)/shard_map/contract/pallas_call | solution.py:137
  14.5 3.1 %collective-permute-start.7 = (bf16[272,256]{1,0:T(8,128)(2,1)S(1)}, bf16[272,256]{1,0:T(8,128)(2,1)S(1)}, u32[]{:S(2)}, u32[]{:S(2)}) collective-permute-start(bf16[272,256]{1,0:T(8,128)(2,1)S(1)} %get-tuple-element.39), channel_id=1, source_target_pairs={{0,18},{1,19},{2,16},{3,17},{4,22},{5,23},{6,20},{7,21},{8,26},{9,... | collective-permute-start | bytes 417800 | tf_op jit(solution)/shard_map/ppermute | solution.py:255
  18.6 1.9 %collective-permute-done.7.refs_3_.refs_11_ = bf16[272,256]{1,0:T(8,128)(2,1)S(1)} collective-permute-done((bf16[272,256]{1,0:T(8,128)(2,1)S(1)}, bf16[272,256]{1,0:T(8,128)(2,1)S(1)}, u32[]{:S(2)}, u32[]{:S(2)}) %collective-permute-start.7) | collective-permute-done | bytes 139296 | tf_op jit(solution)/shard_map/ppermute | solution.py:255
  20.5 2.0 %collective-permute-start.9 = (bf16[272,256]{1,0:T(8,128)(2,1)S(1)}, bf16[272,256]{1,0:T(8,128)(2,1)S(1)}, u32[]{:S(2)}, u32[]{:S(2)}) collective-permute-start(bf16[272,256]{1,0:T(8,128)(2,1)S(1)} %get-tuple-element.37), channel_id=1, source_target_pairs={{0,2},{1,3},{2,0},{3,1},{4,6},{5,7},{6,4},{7,5},{8,10},{9,11},{10,... | collective-permute-start | bytes 417800 | tf_op jit(solution)/shard_map/ppermute | solution.py:255
  22.5 1.5 %collective-permute-start.10 = (bf16[272,256]{1,0:T(8,128)(2,1)S(1)}, bf16[272,256]{1,0:T(8,128)(2,1)S(1)}, u32[]{:S(2)}, u32[]{:S(2)}) collective-permute-start(bf16[272,256]{1,0:T(8,128)(2,1)S(1)} %get-tuple-element.38), channel_id=1, source_target_pairs={{0,16},{1,17},{2,18},{3,19},{4,20},{5,21},{6,22},{7,23},{8,24},{9,... | collective-permute-start | bytes 417800 | tf_op jit(solution)/shard_map/ppermute | solution.py:255
  24.0 1.0 %spread.2 = (bf16[512,256]{1,0:T(8,128)(2,1)S(1)}, bf16[512,256]{1,0:T(8,128)(2,1)S(1)}) custom-call(bf16[272,256]{1,0:T(8,128)(2,1)S(1)} %get-tuple-element.40.refs_0_.refs_8_, bf16[272,256]{1,0:T(8,128)(2,1)S(1)} %collective-permute-done.refs_1_.refs_9_, bf16[272,256]{1,0:T(8,128)(2,1)S(1)} %collective-permute-done.1.refs_2_.refs_10_, ...), custom_call_target="tpu_custom_call" | custom-call | flops 1 | bytes 1 | tf_op jit(solution)/shard_map/spread/pallas_call | solution.py:199
  25.6 0.9 %collective-permute-done.9.refs_1_.refs_9_ = bf16[272,256]{1,0:T(8,128)(2,1)S(1)} collective-permute-done((bf16[272,256]{1,0:T(8,128)(2,1)S(1)}, bf16[272,256]{1,0:T(8,128)(2,1)S(1)}, u32[]{:S(2)}, u32[]{:S(2)}) %collective-permute-start.9) | collective-permute-done | bytes 139296 | tf_op jit(solution)/shard_map/ppermute | solution.py:255
  26.5 1.1 %collective-permute-done.10.refs_2_.refs_10_ = bf16[272,256]{1,0:T(8,128)(2,1)S(1)} collective-permute-done((bf16[272,256]{1,0:T(8,128)(2,1)S(1)}, bf16[272,256]{1,0:T(8,128)(2,1)S(1)}, u32[]{:S(2)}, u32[]{:S(2)}) %collective-permute-start.10) | collective-permute-done | bytes 139296 | tf_op jit(solution)/shard_map/ppermute | solution.py:255
  29.7 1.0 %spread.3 = (bf16[512,256]{1,0:T(8,128)(2,1)S(1)}, bf16[512,256]{1,0:T(8,128)(2,1)S(1)}) custom-call(bf16[272,256]{1,0:T(8,128)(2,1)S(1)} %get-tuple-element.50.refs_0_.refs_8_, bf16[272,256]{1,0:T(8,128)(2,1)S(1)} %collective-permute-done.9.refs_1_.refs_9_, bf16[272,256]{1,0:T(8,128)(2,1)S(1)} %collective-permute-done.10.refs_2_.refs_10_, ...), custom_call_target="tpu_custom_call" | custom-call | flops 1 | bytes 1 | tf_op jit(solution)/shard_map/spread/pallas_call | solution.py:199
  30.7 1.6 %collective-permute-start.16 = (bf16[512,256]{1,0:T(8,128)(2,1)S(1)}, bf16[512,256]{1,0:T(8,128)(2,1)S(1)}, u32[]{:S(2)}, u32[]{:S(2)}) collective-permute-start(bf16[512,256]{1,0:T(8,128)(2,1)S(1)} %get-tuple-element.54), channel_id=1, source_target_pairs={{0,1},{1,0},{2,3},{3,2},{4,5},{5,4},{6,7},{7,6},{8,9},{9,8},{10,11... | collective-permute-start | bytes 786440 | tf_op jit(solution)/shard_map/ppermute | solution.py:306
  32.4 2.7 %collective-permute-start.15 = (bf16[256,256]{1,0:T(8,128)(2,1)S(1)}, bf16[256,256]{1,0:T(8,128)(2,1)S(1)}, u32[]{:S(2)}, u32[]{:S(2)}) collective-permute-start(bf16[256,256]{1,0:T(8,128)(2,1)S(1)} %slice.51), channel_id=1, source_target_pairs={{0,4},{1,5},{2,6},{3,7},{4,0},{5,1},{6,2},{7,3},{8,12},{9,13},{10,... | collective-permute-start | bytes 393224 | tf_op jit(solution)/shard_map/ppermute | solution.py:310
  35.0 4.3 %collective-permute-done.16 = bf16[512,256]{1,0:T(8,128)(2,1)S(1)} collective-permute-done((bf16[512,256]{1,0:T(8,128)(2,1)S(1)}, bf16[512,256]{1,0:T(8,128)(2,1)S(1)}, u32[]{:S(2)}, u32[]{:S(2)}) %collective-permute-start.16) | collective-permute-done | bytes 262176 | tf_op jit(solution)/shard_map/ppermute | solution.py:306
  39.4 2.7 %collective-permute-start.24 = (bf16[256,256]{1,0:T(8,128)(2,1)S(1)}, bf16[256,256]{1,0:T(8,128)(2,1)S(1)}, u32[]{:S(2)}, u32[]{:S(2)}) collective-permute-start(bf16[256,256]{1,0:T(8,128)(2,1)S(1)} %slice.50), channel_id=1, source_target_pairs={{0,4},{1,5},{2,6},{3,7},{4,0},{5,1},{6,2},{7,3},{8,12},{9,13},{10,... | collective-permute-start | bytes 393224 | tf_op jit(solution)/shard_map/ppermute | solution.py:313
  42.1 2.5 %collective-permute-start.19 = (bf16[128,256]{1,0:T(8,128)(2,1)S(1)}, bf16[128,256]{1,0:T(8,128)(2,1)S(1)}, u32[]{:S(2)}, u32[]{:S(2)}) collective-permute-start(bf16[128,256]{1,0:T(8,128)(2,1)S(1)} %get-tuple-element.60), channel_id=1, source_target_pairs={{0,17},{1,16},{2,19},{3,18},{4,21},{5,20},{6,23},{7,22},{8,25},{9,... | collective-permute-start | bytes 196616 | tf_op jit(solution)/shard_map/ppermute | solution.py:255
  45.7 1.8 %collective-permute-done.19 = bf16[128,256]{1,0:T(8,128)(2,1)S(1)} collective-permute-done((bf16[128,256]{1,0:T(8,128)(2,1)S(1)}, bf16[128,256]{1,0:T(8,128)(2,1)S(1)}, u32[]{:S(2)}, u32[]{:S(2)}) %collective-permute-start.19) | collective-permute-done | bytes 65568 | tf_op jit(solution)/shard_map/ppermute | solution.py:255
  47.5 1.4 %collective-permute-done.17 = bf16[128,256]{1,0:T(8,128)(2,1)S(1)} collective-permute-done((bf16[128,256]{1,0:T(8,128)(2,1)S(1)}, bf16[128,256]{1,0:T(8,128)(2,1)S(1)}, u32[]{:S(2)}, u32[]{:S(2)}) %collective-permute-start.17) | collective-permute-done | bytes 65568 | tf_op jit(solution)/shard_map/ppermute | solution.py:255
  48.9 1.5 %collective-permute-start.27 = (bf16[128,256]{1,0:T(8,128)(2,1)S(1)}, bf16[128,256]{1,0:T(8,128)(2,1)S(1)}, u32[]{:S(2)}, u32[]{:S(2)}) collective-permute-start(bf16[128,256]{1,0:T(8,128)(2,1)S(1)} %get-tuple-element.58), channel_id=1, source_target_pairs={{0,18},{1,19},{2,16},{3,17},{4,22},{5,23},{6,20},{7,21},{8,26},{9,... | collective-permute-start | bytes 196616 | tf_op jit(solution)/shard_map/ppermute | solution.py:255
  51.1 1.3 %collective-permute-start.26 = (bf16[128,256]{1,0:T(8,128)(2,1)S(1)}, bf16[128,256]{1,0:T(8,128)(2,1)S(1)}, u32[]{:S(2)}, u32[]{:S(2)}) collective-permute-start(bf16[128,256]{1,0:T(8,128)(2,1)S(1)} %get-tuple-element.59), channel_id=1, source_target_pairs={{0,16},{1,17},{2,18},{3,19},{4,20},{5,21},{6,22},{7,23},{8,24},{9,... | collective-permute-start | bytes 196616 | tf_op jit(solution)/shard_map/ppermute | solution.py:255
  53.0 1.8 %collective-permute-done.27 = bf16[128,256]{1,0:T(8,128)(2,1)S(1)} collective-permute-done((bf16[128,256]{1,0:T(8,128)(2,1)S(1)}, bf16[128,256]{1,0:T(8,128)(2,1)S(1)}, u32[]{:S(2)}, u32[]{:S(2)}) %collective-permute-start.27) | collective-permute-done | bytes 65568 | tf_op jit(solution)/shard_map/ppermute | solution.py:255
  56.2 0.9 %collective-permute-done.30 = bf16[128,256]{1,0:T(8,128)(2,1)S(1)} collective-permute-done((bf16[128,256]{1,0:T(8,128)(2,1)S(1)}, bf16[128,256]{1,0:T(8,128)(2,1)S(1)}, u32[]{:S(2)}, u32[]{:S(2)}) %collective-permute-start.30) | collective-permute-done | bytes 65568 | tf_op jit(solution)/shard_map/ppermute | solution.py:260
  57.0 1.1 %assemble.1 = (bf16[4,256,256]{2,1,0:T(8,128)(2,1)}, bf16[4,256,256]{2,1,0:T(8,128)(2,1)}) custom-call(bf16[4,32,256]{2,1,0:T(8,128)(2,1)S(1)} %bitcast.16, bf16[4,32,256]{2,1,0:T(8,128)(2,1)S(1)} %bitcast.19, bf16[4,32,256]{2,1,0:T(8,128)(2,1)S(1)} %bitcast.21, bf16[4,32,256]{2,1,0:T(8,128)(2,1)S(1)} %bitcast.18, bf16[4,32,256]{2,1,0:T(8,128)(2,1)S(1)} %bitcast.20, ...), custom_call_target="tpu_custom_call" | custom-call | tf_op jit(solution)/shard_map/assemble/pallas_call | solution.py:241
  (53 shorter events, 7.6 us)
Async XLA Ops:
  6.1 11.4 %collective-permute-start = (bf16[272,256]{1,0:T(8,128)(2,1)S(1)}, bf16[272,256]{1,0:T(8,128)(2,1)S(1)}, u32[]{:S(2)}, u32[]{:S(2)}) collective-permute-start(bf16[272,256]{1,0:T(8,128)(2,1)S(1)} %get-tuple-element.31), channel_id=1, source_target_pairs={{0,1},{1,0},{2,3},{3,2},{4,5},{5,4},{6,7},{7,6},{8,9},{9,8},{10,11... | collective-permute-start | bytes 417800 | tf_op jit(solution)/shard_map/ppermute | solution.py:255
  9.1 8.4 %collective-permute-start.1 = (bf16[272,256]{1,0:T(8,128)(2,1)S(1)}, bf16[272,256]{1,0:T(8,128)(2,1)S(1)}, u32[]{:S(2)}, u32[]{:S(2)}) collective-permute-start(bf16[272,256]{1,0:T(8,128)(2,1)S(1)} %get-tuple-element.32), channel_id=1, source_target_pairs={{0,16},{1,17},{2,18},{3,19},{4,20},{5,21},{6,22},{7,23},{8,24},{9,... | collective-permute-start | bytes 417800 | tf_op jit(solution)/shard_map/ppermute | solution.py:255
  10.6 6.9 %collective-permute-start.2 = (bf16[272,256]{1,0:T(8,128)(2,1)S(1)}, bf16[272,256]{1,0:T(8,128)(2,1)S(1)}, u32[]{:S(2)}, u32[]{:S(2)}) collective-permute-start(bf16[272,256]{1,0:T(8,128)(2,1)S(1)} %get-tuple-element.33), channel_id=1, source_target_pairs={{0,17},{1,16},{2,19},{3,18},{4,21},{5,20},{6,23},{7,22},{8,25},{9,... | collective-permute-start | bytes 417800 | tf_op jit(solution)/shard_map/ppermute | solution.py:255
  14.5 6.1 %collective-permute-start.7 = (bf16[272,256]{1,0:T(8,128)(2,1)S(1)}, bf16[272,256]{1,0:T(8,128)(2,1)S(1)}, u32[]{:S(2)}, u32[]{:S(2)}) collective-permute-start(bf16[272,256]{1,0:T(8,128)(2,1)S(1)} %get-tuple-element.39), channel_id=1, source_target_pairs={{0,18},{1,19},{2,16},{3,17},{4,22},{5,23},{6,20},{7,21},{8,26},{9,... | collective-permute-start | bytes 417800 | tf_op jit(solution)/shard_map/ppermute | solution.py:255
  17.5 5.0 %collective-permute-start.3 = (bf16[272,256]{1,0:T(8,128)(2,1)S(1)}, bf16[272,256]{1,0:T(8,128)(2,1)S(1)}, u32[]{:S(2)}, u32[]{:S(2)}) collective-permute-start(bf16[272,256]{1,0:T(8,128)(2,1)S(1)} %get-tuple-element.40.refs_0_.refs_8_), channel_id=1, source_target_pairs={{0,8},{1,9},{2,10},{3,11},{4,12},{5,13},{6,14},{7,15},{8,0},{9,1},... | collective-permute-start | bytes 417800 | tf_op jit(solution)/shard_map/ppermute | solution.py:260
  17.6 6.4 %collective-permute-start.4 = (bf16[272,256]{1,0:T(8,128)(2,1)S(1)}, bf16[272,256]{1,0:T(8,128)(2,1)S(1)}, u32[]{:S(2)}, u32[]{:S(2)}) collective-permute-start(bf16[272,256]{1,0:T(8,128)(2,1)S(1)} %collective-permute-done.refs_1_.refs_9_), channel_id=1, source_target_pairs={{0,8},{1,9},{2,10},{3,11},{4,12},{5,13},{6,14},{7,15},{8,0},{9,1},... | collective-permute-start | bytes 417800 | tf_op jit(solution)/shard_map/ppermute | solution.py:260
  18.1 5.9 %collective-permute-start.5 = (bf16[272,256]{1,0:T(8,128)(2,1)S(1)}, bf16[272,256]{1,0:T(8,128)(2,1)S(1)}, u32[]{:S(2)}, u32[]{:S(2)}) collective-permute-start(bf16[272,256]{1,0:T(8,128)(2,1)S(1)} %collective-permute-done.1.refs_2_.refs_10_), channel_id=1, source_target_pairs={{0,8},{1,9},{2,10},{3,11},{4,12},{5,13},{6,14},{7,15},{8,0},{9,1},... | collective-permute-start | bytes 417800 | tf_op jit(solution)/shard_map/ppermute | solution.py:260
  18.2 5.9 %collective-permute-start.6 = (bf16[272,256]{1,0:T(8,128)(2,1)S(1)}, bf16[272,256]{1,0:T(8,128)(2,1)S(1)}, u32[]{:S(2)}, u32[]{:S(2)}) collective-permute-start(bf16[272,256]{1,0:T(8,128)(2,1)S(1)} %collective-permute-done.2.refs_3_.refs_11_), channel_id=1, source_target_pairs={{0,8},{1,9},{2,10},{3,11},{4,12},{5,13},{6,14},{7,15},{8,0},{9,1},... | collective-permute-start | bytes 417800 | tf_op jit(solution)/shard_map/ppermute | solution.py:260
  20.5 6.0 %collective-permute-start.9 = (bf16[272,256]{1,0:T(8,128)(2,1)S(1)}, bf16[272,256]{1,0:T(8,128)(2,1)S(1)}, u32[]{:S(2)}, u32[]{:S(2)}) collective-permute-start(bf16[272,256]{1,0:T(8,128)(2,1)S(1)} %get-tuple-element.37), channel_id=1, source_target_pairs={{0,2},{1,3},{2,0},{3,1},{4,6},{5,7},{6,4},{7,5},{8,10},{9,11},{10,... | collective-permute-start | bytes 417800 | tf_op jit(solution)/shard_map/ppermute | solution.py:255
  22.5 5.1 %collective-permute-start.10 = (bf16[272,256]{1,0:T(8,128)(2,1)S(1)}, bf16[272,256]{1,0:T(8,128)(2,1)S(1)}, u32[]{:S(2)}, u32[]{:S(2)}) collective-permute-start(bf16[272,256]{1,0:T(8,128)(2,1)S(1)} %get-tuple-element.38), channel_id=1, source_target_pairs={{0,16},{1,17},{2,18},{3,19},{4,20},{5,21},{6,22},{7,23},{8,24},{9,... | collective-permute-start | bytes 417800 | tf_op jit(solution)/shard_map/ppermute | solution.py:255
  25.1 7.2 %collective-permute-start.8 = (bf16[512,256]{1,0:T(8,128)(2,1)S(1)}, bf16[512,256]{1,0:T(8,128)(2,1)S(1)}, u32[]{:S(2)}, u32[]{:S(2)}) collective-permute-start(bf16[512,256]{1,0:T(8,128)(2,1)S(1)} %get-tuple-element.49), channel_id=1, source_target_pairs={{0,2},{1,3},{2,0},{3,1},{4,6},{5,7},{6,4},{7,5},{8,10},{9,11},{10,... | collective-permute-start | bytes 786440 | tf_op jit(solution)/shard_map/ppermute | solution.py:302
  30.7 8.6 %collective-permute-start.16 = (bf16[512,256]{1,0:T(8,128)(2,1)S(1)}, bf16[512,256]{1,0:T(8,128)(2,1)S(1)}, u32[]{:S(2)}, u32[]{:S(2)}) collective-permute-start(bf16[512,256]{1,0:T(8,128)(2,1)S(1)} %get-tuple-element.54), channel_id=1, source_target_pairs={{0,1},{1,0},{2,3},{3,2},{4,5},{5,4},{6,7},{7,6},{8,9},{9,8},{10,11... | collective-permute-start | bytes 786440 | tf_op jit(solution)/shard_map/ppermute | solution.py:306
  32.4 9.7 %collective-permute-start.15 = (bf16[256,256]{1,0:T(8,128)(2,1)S(1)}, bf16[256,256]{1,0:T(8,128)(2,1)S(1)}, u32[]{:S(2)}, u32[]{:S(2)}) collective-permute-start(bf16[256,256]{1,0:T(8,128)(2,1)S(1)} %slice.51), channel_id=1, source_target_pairs={{0,4},{1,5},{2,6},{3,7},{4,0},{5,1},{6,2},{7,3},{8,12},{9,13},{10,... | collective-permute-start | bytes 393224 | tf_op jit(solution)/shard_map/ppermute | solution.py:310
  39.4 9.5 %collective-permute-start.24 = (bf16[256,256]{1,0:T(8,128)(2,1)S(1)}, bf16[256,256]{1,0:T(8,128)(2,1)S(1)}, u32[]{:S(2)}, u32[]{:S(2)}) collective-permute-start(bf16[256,256]{1,0:T(8,128)(2,1)S(1)} %slice.50), channel_id=1, source_target_pairs={{0,4},{1,5},{2,6},{3,7},{4,0},{5,1},{6,2},{7,3},{8,12},{9,13},{10,... | collective-permute-start | bytes 393224 | tf_op jit(solution)/shard_map/ppermute | solution.py:313
  42.1 5.4 %collective-permute-start.19 = (bf16[128,256]{1,0:T(8,128)(2,1)S(1)}, bf16[128,256]{1,0:T(8,128)(2,1)S(1)}, u32[]{:S(2)}, u32[]{:S(2)}) collective-permute-start(bf16[128,256]{1,0:T(8,128)(2,1)S(1)} %get-tuple-element.60), channel_id=1, source_target_pairs={{0,17},{1,16},{2,19},{3,18},{4,21},{5,20},{6,23},{7,22},{8,25},{9,... | collective-permute-start | bytes 196616 | tf_op jit(solution)/shard_map/ppermute | solution.py:255
  44.6 4.3 %collective-permute-start.17 = (bf16[128,256]{1,0:T(8,128)(2,1)S(1)}, bf16[128,256]{1,0:T(8,128)(2,1)S(1)}, u32[]{:S(2)}, u32[]{:S(2)}) collective-permute-start(bf16[128,256]{1,0:T(8,128)(2,1)S(1)} %get-tuple-element.60), channel_id=1, source_target_pairs={{0,1},{1,0},{2,3},{3,2},{4,5},{5,4},{6,7},{7,6},{8,9},{9,8},{10,11... | collective-permute-start | bytes 196616 | tf_op jit(solution)/shard_map/ppermute | solution.py:255
  45.1 5.3 %collective-permute-start.20 = (bf16[128,256]{1,0:T(8,128)(2,1)S(1)}, bf16[128,256]{1,0:T(8,128)(2,1)S(1)}, u32[]{:S(2)}, u32[]{:S(2)}) collective-permute-start(bf16[128,256]{1,0:T(8,128)(2,1)S(1)} %get-tuple-element.61), channel_id=1, source_target_pairs={{0,8},{1,9},{2,10},{3,11},{4,12},{5,13},{6,14},{7,15},{8,0},{9,1},... | collective-permute-start | bytes 196616 | tf_op jit(solution)/shard_map/ppermute | solution.py:260
  45.1 6.0 %collective-permute-start.18 = (bf16[128,256]{1,0:T(8,128)(2,1)S(1)}, bf16[128,256]{1,0:T(8,128)(2,1)S(1)}, u32[]{:S(2)}, u32[]{:S(2)}) collective-permute-start(bf16[128,256]{1,0:T(8,128)(2,1)S(1)} %get-tuple-element.61), channel_id=1, source_target_pairs={{0,16},{1,17},{2,18},{3,19},{4,20},{5,21},{6,22},{7,23},{8,24},{9,... | collective-permute-start | bytes 196616 | tf_op jit(solution)/shard_map/ppermute | solution.py:255
  47.5 5.0 %collective-permute-start.23 = (bf16[128,256]{1,0:T(8,128)(2,1)S(1)}, bf16[128,256]{1,0:T(8,128)(2,1)S(1)}, u32[]{:S(2)}, u32[]{:S(2)}) collective-permute-start(bf16[128,256]{1,0:T(8,128)(2,1)S(1)} %collective-permute-done.19), channel_id=1, source_target_pairs={{0,8},{1,9},{2,10},{3,11},{4,12},{5,13},{6,14},{7,15},{8,0},{9,1},... | collective-permute-start | bytes 196616 | tf_op jit(solution)/shard_map/ppermute | solution.py:260
  48.9 3.6 %collective-permute-start.21 = (bf16[128,256]{1,0:T(8,128)(2,1)S(1)}, bf16[128,256]{1,0:T(8,128)(2,1)S(1)}, u32[]{:S(2)}, u32[]{:S(2)}) collective-permute-start(bf16[128,256]{1,0:T(8,128)(2,1)S(1)} %collective-permute-done.17), channel_id=1, source_target_pairs={{0,8},{1,9},{2,10},{3,11},{4,12},{5,13},{6,14},{7,15},{8,0},{9,1},... | collective-permute-start | bytes 196616 | tf_op jit(solution)/shard_map/ppermute | solution.py:260
  48.9 5.9 %collective-permute-start.27 = (bf16[128,256]{1,0:T(8,128)(2,1)S(1)}, bf16[128,256]{1,0:T(8,128)(2,1)S(1)}, u32[]{:S(2)}, u32[]{:S(2)}) collective-permute-start(bf16[128,256]{1,0:T(8,128)(2,1)S(1)} %get-tuple-element.58), channel_id=1, source_target_pairs={{0,18},{1,19},{2,16},{3,17},{4,22},{5,23},{6,20},{7,21},{8,26},{9,... | collective-permute-start | bytes 196616 | tf_op jit(solution)/shard_map/ppermute | solution.py:255
  50.4 4.4 %collective-permute-start.25 = (bf16[128,256]{1,0:T(8,128)(2,1)S(1)}, bf16[128,256]{1,0:T(8,128)(2,1)S(1)}, u32[]{:S(2)}, u32[]{:S(2)}) collective-permute-start(bf16[128,256]{1,0:T(8,128)(2,1)S(1)} %get-tuple-element.58), channel_id=1, source_target_pairs={{0,2},{1,3},{2,0},{3,1},{4,6},{5,7},{6,4},{7,5},{8,10},{9,11},{10,... | collective-permute-start | bytes 196616 | tf_op jit(solution)/shard_map/ppermute | solution.py:255
  51.1 4.6 %collective-permute-start.26 = (bf16[128,256]{1,0:T(8,128)(2,1)S(1)}, bf16[128,256]{1,0:T(8,128)(2,1)S(1)}, u32[]{:S(2)}, u32[]{:S(2)}) collective-permute-start(bf16[128,256]{1,0:T(8,128)(2,1)S(1)} %get-tuple-element.59), channel_id=1, source_target_pairs={{0,16},{1,17},{2,18},{3,19},{4,20},{5,21},{6,22},{7,23},{8,24},{9,... | collective-permute-start | bytes 196616 | tf_op jit(solution)/shard_map/ppermute | solution.py:255
  52.5 3.3 %collective-permute-start.22 = (bf16[128,256]{1,0:T(8,128)(2,1)S(1)}, bf16[128,256]{1,0:T(8,128)(2,1)S(1)}, u32[]{:S(2)}, u32[]{:S(2)}) collective-permute-start(bf16[128,256]{1,0:T(8,128)(2,1)S(1)} %collective-permute-done.18), channel_id=1, source_target_pairs={{0,8},{1,9},{2,10},{3,11},{4,12},{5,13},{6,14},{7,15},{8,0},{9,1},... | collective-permute-start | bytes 196616 | tf_op jit(solution)/shard_map/ppermute | solution.py:260
  (8 other events, 13.0 us)

commit v7 on v3

v7 whole, which is shorter than its diff:
```python
import functools

import jax
import jax.numpy as jnp
from jax import lax
from jax.experimental import pallas as pl
from jax.experimental.pallas import tpu as pltpu
from jax.sharding import PartitionSpec as P

VMEM_LIMIT = 16 * 1024 * 1024
LABEL_ROWS = 16
AXES = ("op", "sec")


class Plan:
    def __init__(self, mesh, psi, terms):
        self.op, self.sec = mesh.shape["op"], mesh.shape["sec"]
        self.held, self.blk = psi.shape[0], psi.shape[1]
        self.terms = terms
        self.slots = self.sec // 2
        self.extra = 0
        while self.slots * self.op * 2**self.extra < self.held * self.sec:
            self.extra += 1
        order = list(range(self.sec.bit_length() - 1))
        orders = [order, [order[1], order[0], *order[2:]]]
        self.inside = [x[: self.extra] for x in orders]
        self.bits = [x[self.extra :] for x in orders]
        self.places = (self.op // 2) * 2**self.extra
        self.rows = self.blk // (2 * self.places)
        self.part = self.slots * self.rows
        self.step, self.window = 8, 2

    def inner(self, core, sec):
        total = sec * 0
        for i, b in enumerate(self.inside[core]):
            total = total + (((sec >> b) & 1) << i)
        return total

    def here(self):
        op, sec = lax.axis_index("op"), lax.axis_index("sec")
        core = op % 2
        first, second = ((op // 2) * 2**self.extra + self.inner(c, sec) for c in range(2))
        own = jnp.where(core == 0, first, second)
        return core, sec, own, first + second - own

    def row(self, place, core):
        return pl.multiple_of((place * 2 + core) * self.rows, self.rows)

    def partners(self, op_mask, sec_masks):
        pairs = []
        for op in range(self.op):
            for sec in range(self.sec):
                other = (op ^ op_mask) * self.sec + (sec ^ sec_masks[op % 2])
                pairs.append((op * self.sec + sec, other))
        return pairs

    def to_core(self, x):
        return lax.ppermute(x, AXES, self.partners(1, (0, 0)))

    def across(self, x, mask):
        if mask == 0:
            return x
        sec_masks = [sum(((mask >> i) & 1) << b for i, b in enumerate(inside)) for inside in self.inside]
        return lax.ppermute(x, AXES, self.partners((mask >> self.extra) << 1, sec_masks))

    def halve(self, k, x):
        return lax.ppermute(x, AXES, self.partners(0, [1 << bits[k] for bits in self.bits]))


def contract_kernel(plan, fetch, *refs):
    source, target, left, right, vector = refs[:5]
    keep, give, refs = refs[5], refs[6], refs[7:]
    if fetch:
        lhs, rhs, refs = refs[0], refs[1], refs[2:]
    else:
        lhs, rhs = left, right
    src, tgt, psi, acc, slot_of, labels, seen, sems, first_sems = refs
    blk, terms, step = plan.blk, plan.terms, plan.step
    chunks = terms // step if fetch else 0

    heads = [
        pltpu.make_async_copy(x, y, first_sems.at[i])
        for i, (x, y) in enumerate(((target, tgt), (source, src), (vector, psi)))
    ]
    for copy in heads:
        copy.start()

    def loads(c):
        part = pl.ds(c * step, step)
        return [
            pltpu.make_async_copy(left.at[part], lhs.at[part], sems.at[0, c]),
            pltpu.make_async_copy(right.at[part], rhs.at[part], sems.at[1, c]),
        ]

    def begin(c):
        if c < chunks:
            for copy in loads(c):
                copy.start()

    for c in range(plan.window):
        begin(c)
    for h in range(plan.sec):
        seen[h] = -1
    acc[...] = jnp.zeros_like(acc)
    heads[0].wait()

    def name(t, count):
        goal = tgt[t]
        holder = goal // plan.held
        fresh = seen[holder] < 0
        slot = jnp.where(fresh, count, seen[holder])
        seen[holder] = slot
        labels[slot] = goal
        slot_of[t] = slot
        return count + fresh.astype(jnp.int32)

    lax.fori_loop(0, terms, name, jnp.int32(0))
    for copy in heads[1:]:
        copy.wait()

    for t in range(terms):
        if fetch and t % step == 0:
            for copy in loads(t // step):
                copy.wait()
            begin(t // step + plan.window)
        half = jnp.dot(lhs[t], psi[src[t]], preferred_element_type=jnp.float32).astype(jnp.bfloat16)
        acc[slot_of[t]] += lax.dot_general(
            half, rhs[t], (((1,), (1,)), ((), ())), preferred_element_type=jnp.float32
        )

    core, _, place, other_place = plan.here()
    lane = lax.broadcasted_iota(jnp.int32, (LABEL_ROWS, blk), 1)
    tile = jnp.zeros((LABEL_ROWS, blk), jnp.float32)
    for j in range(plan.slots):
        tile = jnp.where(lane == core * plan.slots + j, labels[j].astype(jnp.float32), tile)
    tile = tile.astype(jnp.bfloat16)
    for m in range(plan.places):
        for out, row in ((keep, plan.row(place ^ m, core)), (give, plan.row(other_place ^ m, 1 - core))):
            for j in range(plan.slots):
                block = acc[j, pl.ds(row, plan.rows), :].astype(jnp.bfloat16)
                out[m, pl.ds(j * plan.rows, plan.rows), :] = block
            out[m, pl.ds(plan.part, LABEL_ROWS), :] = tile


def contract(plan, fetch, source, target, left, right, vector):
    blk, terms = plan.blk, plan.terms
    bf16 = jnp.bfloat16
    spaces = [pltpu.HBM, pltpu.HBM, *[pltpu.HBM if fetch else pltpu.VMEM] * 2, pltpu.HBM]
    arrays = [
        pltpu.with_memory_space_constraint(x, space)
        for x, space in zip((source, target, left, right, vector), spaces)
    ]
    out_shape = [pltpu.VMEM((plan.places, plan.part + LABEL_ROWS, blk), bf16)] * 2
    if fetch:
        out_shape += [pltpu.VMEM((terms, blk, blk), bf16)] * 2
    return pl.pallas_call(
        functools.partial(contract_kernel, plan, fetch),
        in_specs=[pl.BlockSpec(memory_space=space) for space in spaces],
        out_specs=[pl.BlockSpec(memory_space=pltpu.VMEM)] * len(out_shape),
        out_shape=out_shape,
        scratch_shapes=[
            pltpu.SMEM((terms,), jnp.int32),
            pltpu.SMEM((terms,), jnp.int32),
            pltpu.VMEM((plan.held, blk, blk), bf16),
            pltpu.VMEM((plan.slots, blk, blk), jnp.float32),
            pltpu.SMEM((terms,), jnp.int32),
            pltpu.SMEM((plan.slots,), jnp.int32),
            pltpu.SMEM((plan.sec,), jnp.int32),
            pltpu.SemaphoreType.DMA((2, terms // plan.step)),
            pltpu.SemaphoreType.DMA((3,)),
        ],
        cost_estimate=pl.CostEstimate(
            flops=4 * terms * blk**3,
            bytes_accessed=4 * terms * blk * blk if fetch else terms * blk,
            transcendentals=0,
        ),
        compiler_params=pltpu.CompilerParams(vmem_limit_bytes=VMEM_LIMIT),
        name="contract",
    )(*arrays)


def merge_kernel(plan, kept, got, *outs):
    part = plan.part
    for m, out in enumerate(outs):
        out[pl.ds(0, part), :] = kept[m, pl.ds(0, part), :]
        out[pl.ds(part, part), :] = got[m, pl.ds(0, part), :]
        tail = pl.ds(part, LABEL_ROWS)
        out[pl.ds(2 * part, LABEL_ROWS), :] = kept[m, tail, :] + got[m, tail, :]


def merge(plan, kept, got):
    whole = pl.BlockSpec(memory_space=pltpu.VMEM)
    return pl.pallas_call(
        functools.partial(merge_kernel, plan),
        in_specs=[whole] * 2,
        out_specs=[whole] * plan.places,
        out_shape=[pltpu.VMEM((2 * plan.part + LABEL_ROWS, plan.blk), jnp.bfloat16)] * plan.places,
        cost_estimate=pl.CostEstimate(flops=1, bytes_accessed=1, transcendentals=0),
        compiler_params=pltpu.CompilerParams(vmem_limit_bytes=VMEM_LIMIT),
        name="merge",
    )(*(pltpu.with_memory_space_constraint(x, pltpu.VMEM) for x in (kept, got)))


def spread_kernel(plan, *refs):
    n = plan.places
    blocks, outs = refs[:n], refs[n : n + 2]
    acc, spots_vector, spots, sem = refs[n + 2 :]
    core, sec, _, _ = plan.here()
    for i in range(n):
        tile = blocks[i][pl.ds(2 * plan.part, LABEL_ROWS), :].astype(jnp.float32)
        spots_vector[pl.ds(i, 1), :] = jnp.max(tile, axis=0, keepdims=True)[:, :128].astype(jnp.int32)
    labels = spots_vector[...]
    shift = plan.held.bit_length() - 1
    away = (labels >> shift) ^ sec
    by_core = []
    for c in range(2):
        index = labels * 0
        for b in plan.bits[c]:
            index = index * 2 + ((away >> b) & 1)
        by_core.append(index * 2**plan.extra + plan.inner(c, away))
    spots_vector[...] = jnp.where(core == 0, *by_core) * plan.held + (labels & (plan.held - 1))
    copy = pltpu.make_async_copy(spots_vector, spots, sem)
    copy.start()
    acc[...] = jnp.zeros_like(acc)
    copy.wait()
    for i in range(n):
        for h in range(2):
            for j in range(plan.slots):
                block = blocks[i][pl.ds(h * plan.part + j * plan.rows, plan.rows), :]
                acc[spots[i, (core ^ h) * plan.slots + j]] += block.astype(jnp.float32)
    half = acc.shape[0] // 2
    for k, out in enumerate(outs):
        out[...] = acc[pl.ds((1 - k) * half, half)].astype(jnp.bfloat16).reshape(out.shape)


def spread(plan, pieces):
    blk, rows = plan.blk, plan.rows
    sectors = plan.held * plan.sec
    whole = pl.BlockSpec(memory_space=pltpu.VMEM)
    return pl.pallas_call(
        functools.partial(spread_kernel, plan),
        in_specs=[whole] * len(pieces),
        out_specs=[whole] * 2,
        out_shape=[pltpu.VMEM((sectors // 2 * rows, blk), jnp.bfloat16)] * 2,
        scratch_shapes=[
            pltpu.VMEM((sectors, rows, blk), jnp.float32),
            pltpu.VMEM((plan.places, 128), jnp.int32),
            pltpu.SMEM((plan.places, 128), jnp.int32),
            pltpu.SemaphoreType.DMA,
        ],
        cost_estimate=pl.CostEstimate(flops=1, bytes_accessed=1, transcendentals=0),
        compiler_params=pltpu.CompilerParams(vmem_limit_bytes=VMEM_LIMIT),
        name="spread",
    )(*(pltpu.with_memory_space_constraint(x, pltpu.VMEM) for x in pieces))


def place_kernel(plan, *refs):
    n = 2 * plan.places
    inputs, outs, sems = refs[: 2 * n], refs[2 * n : -1], refs[-1]
    core, _, place, other_place = plan.here()
    moving = []
    for v, out in enumerate(outs):
        for m in range(plan.places):
            for h, row in enumerate((plan.row(place ^ m, core), plan.row(other_place ^ m, 1 - core))):
                i = h * plan.places + m
                part = out.at[:, pl.ds(row, plan.rows), :]
                moving.append(pltpu.make_async_copy(inputs[v * n + i], part, sems.at[v, i]))
    for copy in moving:
        copy.start()
    for copy in moving:
        copy.wait()


def assemble(plan, gathered):
    pieces = [
        pltpu.with_memory_space_constraint(x.reshape(plan.held, plan.rows, plan.blk), pltpu.VMEM)
        for pieces in gathered
        for x in pieces
    ]
    return pl.pallas_call(
        functools.partial(place_kernel, plan),
        in_specs=[pl.BlockSpec(memory_space=pltpu.VMEM)] * len(pieces),
        out_specs=[pl.BlockSpec(memory_space=pl.ANY)] * 2,
        out_shape=[jax.ShapeDtypeStruct((plan.held, plan.blk, plan.blk), jnp.bfloat16)] * 2,
        scratch_shapes=[pltpu.SemaphoreType.DMA((2, 2 * plan.places))],
        compiler_params=pltpu.CompilerParams(vmem_limit_bytes=VMEM_LIMIT),
        name="assemble",
    )(*pieces)


def after(x, y):
    return lax.optimization_barrier((x, y))[0]


def add(arrived, kept):
    return kept.astype(jnp.float32) + arrived.astype(jnp.float32)


def halves(total):
    middle = total.shape[0] // 2
    return total[middle:].astype(jnp.bfloat16), total[:middle]


def trade(plan, kept, given):
    pieces = merge(plan, kept, plan.to_core(given))
    return pieces, [plan.across(pieces[m], m) for m in range(plan.places)]


def gather(plan, total):
    total = total.astype(jnp.bfloat16)
    size = plan.held * plan.rows
    own = []
    for m in range(plan.places):
        inner = m % 2**plan.extra
        own.append(plan.across(total[inner * size : (inner + 1) * size], m))
    return own + [plan.to_core(x) for x in own]


def per_device(mesh, first, second, left, right, source, target):
    plan = Plan(mesh, first, left.shape[0])
    kept, given, lhs, rhs = contract(plan, True, source, target, left, right, first)
    pieces, early = trade(plan, kept, given)
    kept, given = contract(plan, False, after(source, pieces[-1]), target, lhs, rhs, second)
    early = after(early, kept)
    _, late = trade(plan, kept, after(given, early))

    away, kept = spread(plan, early)
    arrived = plan.halve(0, away)
    for k in range(1, len(plan.bits[0])):
        away, kept = halves(add(arrived, kept))
        arrived = plan.halve(k, away)

    late_away, late_kept = spread(plan, after(late, away))
    late_arrived = plan.halve(0, late_away)
    for k in range(1, len(plan.bits[0])):
        late_away, late_kept = halves(add(late_arrived, late_kept))
        late_arrived = plan.halve(k, late_away)
    return tuple(assemble(plan, [gather(plan, add(arrived, kept)), gather(plan, add(late_arrived, late_kept))]))


def solution(mesh):
    in_specs = (
        P("sec", None, None),
        P("sec", None, None),
        P(AXES, None, None),
        P(AXES, None, None),
        P(AXES),
        P(AXES),
    )
    out_specs = (P("sec", None, None), P("sec", None, None))
    return jax.shard_map(
        functools.partial(per_device, mesh),
        mesh=mesh,
        in_specs=in_specs,
        out_specs=out_specs,
        check_vma=False,
    )
```

time: 66.9 us -> 57.3 us (0.86)
  waiting for transfers between devices: 27.3 us -> 19.5 us
  Pallas kernels: 16.6 us -> 12.3 us
  starting transfers between devices: 21.8 us -> 24.5 us
    ppermute x32 -> x26, waiting for transfers between devices: 27.3 us -> 19.5 us  [the longest x4 8.57 us: halve(): lax.ppermute(x, AXES, self.partners(0, [1 << bits[k] for bits in self.bit...]
    pallas_call x2, Pallas kernels: 12.9 us -> 9.31 us  [contract(): pl.pallas_call(functools.partial(contract_kernel, plan, fetch), in_specs=...]
    ppermute x32 -> x26, starting transfers between devices: 21.8 us -> 24.5 us  [the longest x12 15.2 us: across(): lax.ppermute(x, AXES, self.partners(mask >> self.extra << 1, sec_masks))]
    pallas_call x2 -> x1, Pallas kernels: 1.7 us -> 1.09 us  [assemble(): pl.pallas_call(functools.partial(place_kernel, plan), in_specs=[pl.BlockS...]
    pallas_call x2 -> x4, Pallas kernels: 2.09 us -> 1.86 us  [the longest x2 1.79 us: spread(): pl.pallas_call(functools.partial(spread_kernel, plan), in_specs=[whole] *...]
  transfers between devices with their start and end apart: 32 -> 26, of which waited for: 17 -> 13; matrix products, arithmetic and copies ran while one was open for 0% -> 0% of each run, Pallas kernels for 9% -> 10%
where the time goes in v7:
time: 57.3 us; the launch traced here: 57.2 us
  starting transfers between devices  24.5 us (43%)
  waiting for transfers between devices  19.5 us (34%)
  Pallas kernels  12.3 us (21%)
  between operations  0.76 us (1%)
    ppermute x12, starting transfers between devices, across(): lax.ppermute(x, AXES, self.partners(mask >> self.extra << 1, sec_masks))  15.2 us
    pallas_call x2, Pallas kernels, contract(): pl.pallas_call(functools.partial(contract_kernel, plan, fetch), in_specs=...  9.31 us
    ppermute x4, waiting for transfers between devices, halve(): lax.ppermute(x, AXES, self.partners(0, [1 << bits[k] for bits in self.bit...  8.57 us
    ppermute x12, waiting for transfers between devices, across(): lax.ppermute(x, AXES, self.partners(mask >> self.extra << 1, sec_masks))  8.45 us
    ppermute x4, starting transfers between devices, halve(): lax.ppermute(x, AXES, self.partners(0, [1 << bits[k] for bits in self.bit...  8.08 us
    ppermute x10, waiting for transfers between devices, to_core(): return lax.ppermute(x, AXES, self.partners(1, (0, 0)))  2.45 us
    pallas_call x2, Pallas kernels, spread(): pl.pallas_call(functools.partial(spread_kernel, plan), in_specs=[whole] *...  1.79 us
    ppermute x10, starting transfers between devices, to_core(): return lax.ppermute(x, AXES, self.partners(1, (0, 0)))  1.2 us
  transfers between devices with their start and end apart: 26, of which 13 were waited for; matrix products, arithmetic and copies ran while one was open for 0% of the time, Pallas kernels for 10%

profile of v7, /device:TPU:0, one launch (start us, length us, event | category | flops | bytes accessed | tf_op | source)
XLA Modules:
  0.0 57.2 jit_solution(9312310418666898853)
XLA Ops:
  0.6 5.5 %contract.2 = (bf16[4,144,256]{2,1,0:T(8,128)(2,1)S(1)}, bf16[4,144,256]{2,1,0:T(8,128)(2,1)S(1)}, bf16[32,256,256]{2,1,0:T(8,128)(2,1)S(1)}, bf16[32,256,256]{2,1,0:T(8,128)(2,1)S(1)}) custom-call(s32[32]{0:T(128)} %refs_0_.2, s32[32]{0:T(128)} %refs_1_.3, bf16[32,256,256]{2,1,0:T(8,128)(2,1)} %refs_2_.1, bf16[32,256,256]{2,1,0:T(8,128)(2,1)} %refs_3_.1, ...), custom_call_target="tpu_custom_call" | custom-call | flops 2147483648 | bytes 8388608 | tf_op jit(solution)/shard_map/contract/pallas_call | solution.py:156
  6.7 1.2 %collective-permute-done.got = bf16[4,144,256]{2,1,0:T(8,128)(2,1)S(1)} collective-permute-done((bf16[4,144,256]{2,1,0:T(8,128)(2,1)S(1)}, bf16[4,144,256]{2,1,0:T(8,128)(2,1)S(1)}, u32[]{:S(2)}, u32[]{:S(2)}) %collective-permute-start) | collective-permute-done | bytes 294944 | tf_op jit(solution)/shard_map/ppermute | solution.py:58
  7.9 3.9 %collective-permute-start.3 = (bf16[272,256]{1,0:T(8,128)(2,1)S(1)}, bf16[272,256]{1,0:T(8,128)(2,1)S(1)}, u32[]{:S(2)}, u32[]{:S(2)}) collective-permute-start(bf16[272,256]{1,0:T(8,128)(2,1)S(1)} %get-tuple-element.35), channel_id=1, source_target_pairs={{0,17},{1,16},{2,19},{3,18},{4,21},{5,20},{6,23},{7,22},{8,26},{9,... | collective-permute-start | bytes 417800 | tf_op jit(solution)/shard_map/ppermute | solution.py:64
  12.4 3.8 %contract.3 = (bf16[4,144,256]{2,1,0:T(8,128)(2,1)S(1)}, bf16[4,144,256]{2,1,0:T(8,128)(2,1)S(1)}) custom-call(s32[32]{0:T(128)} %refs_0_.2, s32[32]{0:T(128)} %refs_1_.3, bf16[32,256,256]{2,1,0:T(8,128)(2,1)S(1)} %get-tuple-element.37.refs_2_, bf16[32,256,256]{2,1,0:T(8,128)(2,1)S(1)} %get-tuple-element.38.refs_3_, bf16[4,256,256]{2,1,0:T(8,128)(2,1)} %refs_4_.3), custom_call_target="tpu_custom_call" | custom-call | flops 2147483648 | bytes 8192 | tf_op jit(solution)/shard_map/contract/pallas_call | solution.py:156
  16.2 1.2 %collective-permute-done.1.refs_1_ = bf16[272,256]{1,0:T(8,128)(2,1)S(1)} collective-permute-done((bf16[272,256]{1,0:T(8,128)(2,1)S(1)}, bf16[272,256]{1,0:T(8,128)(2,1)S(1)}, u32[]{:S(2)}, u32[]{:S(2)}) %collective-permute-start.1) | collective-permute-done | bytes 139296 | tf_op jit(solution)/shard_map/ppermute | solution.py:64
  17.4 1.4 %collective-permute-done.2.refs_2_ = bf16[272,256]{1,0:T(8,128)(2,1)S(1)} collective-permute-done((bf16[272,256]{1,0:T(8,128)(2,1)S(1)}, bf16[272,256]{1,0:T(8,128)(2,1)S(1)}, u32[]{:S(2)}, u32[]{:S(2)}) %collective-permute-start.2) | collective-permute-done | bytes 139296 | tf_op jit(solution)/shard_map/ppermute | solution.py:64
  19.8 1.7 %collective-permute-start.4 = (bf16[512,256]{1,0:T(8,128)(2,1)S(1)}, bf16[512,256]{1,0:T(8,128)(2,1)S(1)}, u32[]{:S(2)}, u32[]{:S(2)}) collective-permute-start(bf16[512,256]{1,0:T(8,128)(2,1)S(1)} %get-tuple-element.45), channel_id=1, source_target_pairs={{0,2},{1,3},{2,0},{3,1},{4,6},{5,7},{6,4},{7,5},{8,9},{9,8},{10,11... | collective-permute-start | bytes 786440 | tf_op jit(solution)/shard_map/ppermute | solution.py:67
  21.5 1.6 %collective-permute-start.14 = (bf16[272,256]{1,0:T(8,128)(2,1)S(1)}, bf16[272,256]{1,0:T(8,128)(2,1)S(1)}, u32[]{:S(2)}, u32[]{:S(2)}) collective-permute-start(bf16[272,256]{1,0:T(8,128)(2,1)S(1)} %get-tuple-element.49), channel_id=1, source_target_pairs={{0,1},{1,0},{2,3},{3,2},{4,5},{5,4},{6,7},{7,6},{8,10},{9,11},{10,... | collective-permute-start | bytes 417800 | tf_op jit(solution)/shard_map/ppermute | solution.py:64
  23.1 1.5 %collective-permute-start.15 = (bf16[272,256]{1,0:T(8,128)(2,1)S(1)}, bf16[272,256]{1,0:T(8,128)(2,1)S(1)}, u32[]{:S(2)}, u32[]{:S(2)}) collective-permute-start(bf16[272,256]{1,0:T(8,128)(2,1)S(1)} %get-tuple-element.50), channel_id=1, source_target_pairs={{0,16},{1,17},{2,18},{3,19},{4,20},{5,21},{6,22},{7,23},{8,24},{9,... | collective-permute-start | bytes 417800 | tf_op jit(solution)/shard_map/ppermute | solution.py:64
  25.1 3.0 %collective-permute-done.4 = bf16[512,256]{1,0:T(8,128)(2,1)S(1)} collective-permute-done((bf16[512,256]{1,0:T(8,128)(2,1)S(1)}, bf16[512,256]{1,0:T(8,128)(2,1)S(1)}, u32[]{:S(2)}, u32[]{:S(2)}) %collective-permute-start.4) | collective-permute-done | bytes 262176 | tf_op jit(solution)/shard_map/ppermute | solution.py:67
  28.1 2.9 %collective-permute-start.5 = (bf16[256,256]{1,0:T(8,128)(2,1)S(1)}, bf16[256,256]{1,0:T(8,128)(2,1)S(1)}, u32[]{:S(2)}, u32[]{:S(2)}) collective-permute-start(bf16[256,256]{1,0:T(8,128)(2,1)S(1)} %slice.55), channel_id=1, source_target_pairs={{0,4},{1,5},{2,6},{3,7},{4,0},{5,1},{6,2},{7,3},{8,12},{9,13},{10,... | collective-permute-start | bytes 393224 | tf_op jit(solution)/shard_map/ppermute | solution.py:67
  32.6 1.0 %collective-permute-start.17 = (bf16[512,256]{1,0:T(8,128)(2,1)S(1)}, bf16[512,256]{1,0:T(8,128)(2,1)S(1)}, u32[]{:S(2)}, u32[]{:S(2)}) collective-permute-start(bf16[512,256]{1,0:T(8,128)(2,1)S(1)} %get-tuple-element.57), channel_id=1, source_target_pairs={{0,2},{1,3},{2,0},{3,1},{4,6},{5,7},{6,4},{7,5},{8,9},{9,8},{10,11... | collective-permute-start | bytes 786440 | tf_op jit(solution)/shard_map/ppermute | solution.py:67
  33.6 2.9 %collective-permute-done.5 = bf16[256,256]{1,0:T(8,128)(2,1)S(1)} collective-permute-done((bf16[256,256]{1,0:T(8,128)(2,1)S(1)}, bf16[256,256]{1,0:T(8,128)(2,1)S(1)}, u32[]{:S(2)}, u32[]{:S(2)}) %collective-permute-start.5) | collective-permute-done | bytes 131104 | tf_op jit(solution)/shard_map/ppermute | solution.py:67
  36.5 2.8 %collective-permute-done.17 = bf16[512,256]{1,0:T(8,128)(2,1)S(1)} collective-permute-done((bf16[512,256]{1,0:T(8,128)(2,1)S(1)}, bf16[512,256]{1,0:T(8,128)(2,1)S(1)}, u32[]{:S(2)}, u32[]{:S(2)}) %collective-permute-start.17) | collective-permute-done | bytes 262176 | tf_op jit(solution)/shard_map/ppermute | solution.py:67
  39.3 2.4 %collective-permute-start.18 = (bf16[256,256]{1,0:T(8,128)(2,1)S(1)}, bf16[256,256]{1,0:T(8,128)(2,1)S(1)}, u32[]{:S(2)}, u32[]{:S(2)}) collective-permute-start(bf16[256,256]{1,0:T(8,128)(2,1)S(1)} %slice.54), channel_id=1, source_target_pairs={{0,4},{1,5},{2,6},{3,7},{4,0},{5,1},{6,2},{7,3},{8,12},{9,13},{10,... | collective-permute-start | bytes 393224 | tf_op jit(solution)/shard_map/ppermute | solution.py:67
  41.7 1.5 %collective-permute-start.8 = (bf16[128,256]{1,0:T(8,128)(2,1)S(1)}, bf16[128,256]{1,0:T(8,128)(2,1)S(1)}, u32[]{:S(2)}, u32[]{:S(2)}) collective-permute-start(bf16[128,256]{1,0:T(8,128)(2,1)S(1)} %get-tuple-element.60), channel_id=1, source_target_pairs={{0,17},{1,16},{2,19},{3,18},{4,21},{5,20},{6,23},{7,22},{8,26},{9,... | collective-permute-start | bytes 196616 | tf_op jit(solution)/shard_map/ppermute | solution.py:64
  43.2 1.5 %collective-permute-start.6 = (bf16[128,256]{1,0:T(8,128)(2,1)S(1)}, bf16[128,256]{1,0:T(8,128)(2,1)S(1)}, u32[]{:S(2)}, u32[]{:S(2)}) collective-permute-start(bf16[128,256]{1,0:T(8,128)(2,1)S(1)} %get-tuple-element.60), channel_id=1, source_target_pairs={{0,1},{1,0},{2,3},{3,2},{4,5},{5,4},{6,7},{7,6},{8,10},{9,11},{10,... | collective-permute-start | bytes 196616 | tf_op jit(solution)/shard_map/ppermute | solution.py:64
  45.3 1.7 %collective-permute-done.8 = bf16[128,256]{1,0:T(8,128)(2,1)S(1)} collective-permute-done((bf16[128,256]{1,0:T(8,128)(2,1)S(1)}, bf16[128,256]{1,0:T(8,128)(2,1)S(1)}, u32[]{:S(2)}, u32[]{:S(2)}) %collective-permute-start.8) | collective-permute-done | bytes 65568 | tf_op jit(solution)/shard_map/ppermute | solution.py:64
  47.7 1.6 %collective-permute-start.21 = (bf16[128,256]{1,0:T(8,128)(2,1)S(1)}, bf16[128,256]{1,0:T(8,128)(2,1)S(1)}, u32[]{:S(2)}, u32[]{:S(2)}) collective-permute-start(bf16[128,256]{1,0:T(8,128)(2,1)S(1)} %get-tuple-element.58), channel_id=1, source_target_pairs={{0,17},{1,16},{2,19},{3,18},{4,21},{5,20},{6,23},{7,22},{8,26},{9,... | collective-permute-start | bytes 196616 | tf_op jit(solution)/shard_map/ppermute | solution.py:64
  49.3 1.2 %collective-permute-start.19 = (bf16[128,256]{1,0:T(8,128)(2,1)S(1)}, bf16[128,256]{1,0:T(8,128)(2,1)S(1)}, u32[]{:S(2)}, u32[]{:S(2)}) collective-permute-start(bf16[128,256]{1,0:T(8,128)(2,1)S(1)} %get-tuple-element.58), channel_id=1, source_target_pairs={{0,1},{1,0},{2,3},{3,2},{4,5},{5,4},{6,7},{7,6},{8,10},{9,11},{10,... | collective-permute-start | bytes 196616 | tf_op jit(solution)/shard_map/ppermute | solution.py:64
  51.8 1.4 %collective-permute-done.21 = bf16[128,256]{1,0:T(8,128)(2,1)S(1)} collective-permute-done((bf16[128,256]{1,0:T(8,128)(2,1)S(1)}, bf16[128,256]{1,0:T(8,128)(2,1)S(1)}, u32[]{:S(2)}, u32[]{:S(2)}) %collective-permute-start.21) | collective-permute-done | bytes 65568 | tf_op jit(solution)/shard_map/ppermute | solution.py:64
  53.7 1.1 %collective-permute-done.20 = bf16[128,256]{1,0:T(8,128)(2,1)S(1)} collective-permute-done((bf16[128,256]{1,0:T(8,128)(2,1)S(1)}, bf16[128,256]{1,0:T(8,128)(2,1)S(1)}, u32[]{:S(2)}, u32[]{:S(2)}) %collective-permute-start.20) | collective-permute-done | bytes 65568 | tf_op jit(solution)/shard_map/ppermute | solution.py:64
  54.9 1.2 %collective-permute-done.24 = bf16[128,256]{1,0:T(8,128)(2,1)S(1)} collective-permute-done((bf16[128,256]{1,0:T(8,128)(2,1)S(1)}, bf16[128,256]{1,0:T(8,128)(2,1)S(1)}, u32[]{:S(2)}, u32[]{:S(2)}) %collective-permute-start.24) | collective-permute-done | bytes 65568 | tf_op jit(solution)/shard_map/ppermute | solution.py:58
  56.1 1.1 %assemble.1 = (bf16[4,256,256]{2,1,0:T(8,128)(2,1)}, bf16[4,256,256]{2,1,0:T(8,128)(2,1)}) custom-call(bf16[4,32,256]{2,1,0:T(8,128)(2,1)S(1)} %bitcast.16, bf16[4,32,256]{2,1,0:T(8,128)(2,1)S(1)} %bitcast.19, bf16[4,32,256]{2,1,0:T(8,128)(2,1)S(1)} %bitcast.21, bf16[4,32,256]{2,1,0:T(8,128)(2,1)S(1)} %bitcast.18, bf16[4,32,256]{2,1,0:T(8,128)(2,1)S(1)} %bitcast.20, ...), custom_call_target="tpu_custom_call" | custom-call | tf_op jit(solution)/shard_map/assemble/pallas_call | solution.py:280
  (43 shorter events, 7.5 us)
Async XLA Ops:
  6.1 1.7 %collective-permute-start = (bf16[4,144,256]{2,1,0:T(8,128)(2,1)S(1)}, bf16[4,144,256]{2,1,0:T(8,128)(2,1)S(1)}, u32[]{:S(2)}, u32[]{:S(2)}) collective-permute-start(bf16[4,144,256]{2,1,0:T(8,128)(2,1)S(1)} %get-tuple-element.31), channel_id=1, source_target_pairs={{0,8},{1,9},{2,10},{3,11},{4,12},{5,13},{6,14},{7,15},{8,0},{9,1},... | collective-permute-start | bytes 884744 | tf_op jit(solution)/shard_map/ppermute | solution.py:58
  7.9 10.9 %collective-permute-start.3 = (bf16[272,256]{1,0:T(8,128)(2,1)S(1)}, bf16[272,256]{1,0:T(8,128)(2,1)S(1)}, u32[]{:S(2)}, u32[]{:S(2)}) collective-permute-start(bf16[272,256]{1,0:T(8,128)(2,1)S(1)} %get-tuple-element.35), channel_id=1, source_target_pairs={{0,17},{1,16},{2,19},{3,18},{4,21},{5,20},{6,23},{7,22},{8,26},{9,... | collective-permute-start | bytes 417800 | tf_op jit(solution)/shard_map/ppermute | solution.py:64
  11.8 5.6 %collective-permute-start.1 = (bf16[272,256]{1,0:T(8,128)(2,1)S(1)}, bf16[272,256]{1,0:T(8,128)(2,1)S(1)}, u32[]{:S(2)}, u32[]{:S(2)}) collective-permute-start(bf16[272,256]{1,0:T(8,128)(2,1)S(1)} %get-tuple-element.33), channel_id=1, source_target_pairs={{0,1},{1,0},{2,3},{3,2},{4,5},{5,4},{6,7},{7,6},{8,10},{9,11},{10,... | collective-permute-start | bytes 417800 | tf_op jit(solution)/shard_map/ppermute | solution.py:64
  12.3 6.5 %collective-permute-start.2 = (bf16[272,256]{1,0:T(8,128)(2,1)S(1)}, bf16[272,256]{1,0:T(8,128)(2,1)S(1)}, u32[]{:S(2)}, u32[]{:S(2)}) collective-permute-start(bf16[272,256]{1,0:T(8,128)(2,1)S(1)} %get-tuple-element.34), channel_id=1, source_target_pairs={{0,16},{1,17},{2,18},{3,19},{4,20},{5,21},{6,22},{7,23},{8,24},{9,... | collective-permute-start | bytes 417800 | tf_op jit(solution)/shard_map/ppermute | solution.py:64
  18.8 2.7 %collective-permute-start.13 = (bf16[4,144,256]{2,1,0:T(8,128)(2,1)S(1)}, bf16[4,144,256]{2,1,0:T(8,128)(2,1)S(1)}, u32[]{:S(2)}, u32[]{:S(2)}) collective-permute-start(bf16[4,144,256]{2,1,0:T(8,128)(2,1)S(1)} %get-tuple-element.47), channel_id=1, source_target_pairs={{0,8},{1,9},{2,10},{3,11},{4,12},{5,13},{6,14},{7,15},{8,0},{9,1},... | collective-permute-start | bytes 884744 | tf_op jit(solution)/shard_map/ppermute | solution.py:58
  19.8 8.3 %collective-permute-start.4 = (bf16[512,256]{1,0:T(8,128)(2,1)S(1)}, bf16[512,256]{1,0:T(8,128)(2,1)S(1)}, u32[]{:S(2)}, u32[]{:S(2)}) collective-permute-start(bf16[512,256]{1,0:T(8,128)(2,1)S(1)} %get-tuple-element.45), channel_id=1, source_target_pairs={{0,2},{1,3},{2,0},{3,1},{4,6},{5,7},{6,4},{7,5},{8,9},{9,8},{10,11... | collective-permute-start | bytes 786440 | tf_op jit(solution)/shard_map/ppermute | solution.py:67
  21.5 9.5 %collective-permute-start.14 = (bf16[272,256]{1,0:T(8,128)(2,1)S(1)}, bf16[272,256]{1,0:T(8,128)(2,1)S(1)}, u32[]{:S(2)}, u32[]{:S(2)}) collective-permute-start(bf16[272,256]{1,0:T(8,128)(2,1)S(1)} %get-tuple-element.49), channel_id=1, source_target_pairs={{0,1},{1,0},{2,3},{3,2},{4,5},{5,4},{6,7},{7,6},{8,10},{9,11},{10,... | collective-permute-start | bytes 417800 | tf_op jit(solution)/shard_map/ppermute | solution.py:64
  23.1 7.9 %collective-permute-start.15 = (bf16[272,256]{1,0:T(8,128)(2,1)S(1)}, bf16[272,256]{1,0:T(8,128)(2,1)S(1)}, u32[]{:S(2)}, u32[]{:S(2)}) collective-permute-start(bf16[272,256]{1,0:T(8,128)(2,1)S(1)} %get-tuple-element.50), channel_id=1, source_target_pairs={{0,16},{1,17},{2,18},{3,19},{4,20},{5,21},{6,22},{7,23},{8,24},{9,... | collective-permute-start | bytes 417800 | tf_op jit(solution)/shard_map/ppermute | solution.py:64
  24.6 7.0 %collective-permute-start.16 = (bf16[272,256]{1,0:T(8,128)(2,1)S(1)}, bf16[272,256]{1,0:T(8,128)(2,1)S(1)}, u32[]{:S(2)}, u32[]{:S(2)}) collective-permute-start(bf16[272,256]{1,0:T(8,128)(2,1)S(1)} %get-tuple-element.51), channel_id=1, source_target_pairs={{0,17},{1,16},{2,19},{3,18},{4,21},{5,20},{6,23},{7,22},{8,26},{9,... | collective-permute-start | bytes 417800 | tf_op jit(solution)/shard_map/ppermute | solution.py:64
  28.1 8.3 %collective-permute-start.5 = (bf16[256,256]{1,0:T(8,128)(2,1)S(1)}, bf16[256,256]{1,0:T(8,128)(2,1)S(1)}, u32[]{:S(2)}, u32[]{:S(2)}) collective-permute-start(bf16[256,256]{1,0:T(8,128)(2,1)S(1)} %slice.55), channel_id=1, source_target_pairs={{0,4},{1,5},{2,6},{3,7},{4,0},{5,1},{6,2},{7,3},{8,12},{9,13},{10,... | collective-permute-start | bytes 393224 | tf_op jit(solution)/shard_map/ppermute | solution.py:67
  32.6 6.7 %collective-permute-start.17 = (bf16[512,256]{1,0:T(8,128)(2,1)S(1)}, bf16[512,256]{1,0:T(8,128)(2,1)S(1)}, u32[]{:S(2)}, u32[]{:S(2)}) collective-permute-start(bf16[512,256]{1,0:T(8,128)(2,1)S(1)} %get-tuple-element.57), channel_id=1, source_target_pairs={{0,2},{1,3},{2,0},{3,1},{4,6},{5,7},{6,4},{7,5},{8,9},{9,8},{10,11... | collective-permute-start | bytes 786440 | tf_op jit(solution)/shard_map/ppermute | solution.py:67
  39.3 8.4 %collective-permute-start.18 = (bf16[256,256]{1,0:T(8,128)(2,1)S(1)}, bf16[256,256]{1,0:T(8,128)(2,1)S(1)}, u32[]{:S(2)}, u32[]{:S(2)}) collective-permute-start(bf16[256,256]{1,0:T(8,128)(2,1)S(1)} %slice.54), channel_id=1, source_target_pairs={{0,4},{1,5},{2,6},{3,7},{4,0},{5,1},{6,2},{7,3},{8,12},{9,13},{10,... | collective-permute-start | bytes 393224 | tf_op jit(solution)/shard_map/ppermute | solution.py:67
  41.7 5.2 %collective-permute-start.8 = (bf16[128,256]{1,0:T(8,128)(2,1)S(1)}, bf16[128,256]{1,0:T(8,128)(2,1)S(1)}, u32[]{:S(2)}, u32[]{:S(2)}) collective-permute-start(bf16[128,256]{1,0:T(8,128)(2,1)S(1)} %get-tuple-element.60), channel_id=1, source_target_pairs={{0,17},{1,16},{2,19},{3,18},{4,21},{5,20},{6,23},{7,22},{8,26},{9,... | collective-permute-start | bytes 196616 | tf_op jit(solution)/shard_map/ppermute | solution.py:64
  43.2 4.4 %collective-permute-start.6 = (bf16[128,256]{1,0:T(8,128)(2,1)S(1)}, bf16[128,256]{1,0:T(8,128)(2,1)S(1)}, u32[]{:S(2)}, u32[]{:S(2)}) collective-permute-start(bf16[128,256]{1,0:T(8,128)(2,1)S(1)} %get-tuple-element.60), channel_id=1, source_target_pairs={{0,1},{1,0},{2,3},{3,2},{4,5},{5,4},{6,7},{7,6},{8,10},{9,11},{10,... | collective-permute-start | bytes 196616 | tf_op jit(solution)/shard_map/ppermute | solution.py:64
  44.7 4.6 %collective-permute-start.9 = (bf16[128,256]{1,0:T(8,128)(2,1)S(1)}, bf16[128,256]{1,0:T(8,128)(2,1)S(1)}, u32[]{:S(2)}, u32[]{:S(2)}) collective-permute-start(bf16[128,256]{1,0:T(8,128)(2,1)S(1)} %get-tuple-element.61), channel_id=1, source_target_pairs={{0,8},{1,9},{2,10},{3,11},{4,12},{5,13},{6,14},{7,15},{8,0},{9,1},... | collective-permute-start | bytes 196616 | tf_op jit(solution)/shard_map/ppermute | solution.py:58
  44.7 5.8 %collective-permute-start.7 = (bf16[128,256]{1,0:T(8,128)(2,1)S(1)}, bf16[128,256]{1,0:T(8,128)(2,1)S(1)}, u32[]{:S(2)}, u32[]{:S(2)}) collective-permute-start(bf16[128,256]{1,0:T(8,128)(2,1)S(1)} %get-tuple-element.61), channel_id=1, source_target_pairs={{0,16},{1,17},{2,18},{3,19},{4,20},{5,21},{6,22},{7,23},{8,24},{9,... | collective-permute-start | bytes 196616 | tf_op jit(solution)/shard_map/ppermute | solution.py:64
  47.0 4.3 %collective-permute-start.12 = (bf16[128,256]{1,0:T(8,128)(2,1)S(1)}, bf16[128,256]{1,0:T(8,128)(2,1)S(1)}, u32[]{:S(2)}, u32[]{:S(2)}) collective-permute-start(bf16[128,256]{1,0:T(8,128)(2,1)S(1)} %collective-permute-done.8), channel_id=1, source_target_pairs={{0,8},{1,9},{2,10},{3,11},{4,12},{5,13},{6,14},{7,15},{8,0},{9,1},... | collective-permute-start | bytes 196616 | tf_op jit(solution)/shard_map/ppermute | solution.py:58
  47.7 3.6 %collective-permute-start.10 = (bf16[128,256]{1,0:T(8,128)(2,1)S(1)}, bf16[128,256]{1,0:T(8,128)(2,1)S(1)}, u32[]{:S(2)}, u32[]{:S(2)}) collective-permute-start(bf16[128,256]{1,0:T(8,128)(2,1)S(1)} %collective-permute-done.6), channel_id=1, source_target_pairs={{0,8},{1,9},{2,10},{3,11},{4,12},{5,13},{6,14},{7,15},{8,0},{9,1},... | collective-permute-start | bytes 196616 | tf_op jit(solution)/shard_map/ppermute | solution.py:58
  47.7 5.5 %collective-permute-start.21 = (bf16[128,256]{1,0:T(8,128)(2,1)S(1)}, bf16[128,256]{1,0:T(8,128)(2,1)S(1)}, u32[]{:S(2)}, u32[]{:S(2)}) collective-permute-start(bf16[128,256]{1,0:T(8,128)(2,1)S(1)} %get-tuple-element.58), channel_id=1, source_target_pairs={{0,17},{1,16},{2,19},{3,18},{4,21},{5,20},{6,23},{7,22},{8,26},{9,... | collective-permute-start | bytes 196616 | tf_op jit(solution)/shard_map/ppermute | solution.py:64
  49.3 4.3 %collective-permute-start.19 = (bf16[128,256]{1,0:T(8,128)(2,1)S(1)}, bf16[128,256]{1,0:T(8,128)(2,1)S(1)}, u32[]{:S(2)}, u32[]{:S(2)}) collective-permute-start(bf16[128,256]{1,0:T(8,128)(2,1)S(1)} %get-tuple-element.58), channel_id=1, source_target_pairs={{0,1},{1,0},{2,3},{3,2},{4,5},{5,4},{6,7},{7,6},{8,10},{9,11},{10,... | collective-permute-start | bytes 196616 | tf_op jit(solution)/shard_map/ppermute | solution.py:64
  50.6 4.3 %collective-permute-start.20 = (bf16[128,256]{1,0:T(8,128)(2,1)S(1)}, bf16[128,256]{1,0:T(8,128)(2,1)S(1)}, u32[]{:S(2)}, u32[]{:S(2)}) collective-permute-start(bf16[128,256]{1,0:T(8,128)(2,1)S(1)} %get-tuple-element.59), channel_id=1, source_target_pairs={{0,16},{1,17},{2,18},{3,19},{4,20},{5,21},{6,22},{7,23},{8,24},{9,... | collective-permute-start | bytes 196616 | tf_op jit(solution)/shard_map/ppermute | solution.py:64
  51.3 3.5 %collective-permute-start.11 = (bf16[128,256]{1,0:T(8,128)(2,1)S(1)}, bf16[128,256]{1,0:T(8,128)(2,1)S(1)}, u32[]{:S(2)}, u32[]{:S(2)}) collective-permute-start(bf16[128,256]{1,0:T(8,128)(2,1)S(1)} %collective-permute-done.7), channel_id=1, source_target_pairs={{0,8},{1,9},{2,10},{3,11},{4,12},{5,13},{6,14},{7,15},{8,0},{9,1},... | collective-permute-start | bytes 196616 | tf_op jit(solution)/shard_map/ppermute | solution.py:58
  51.3 3.5 %collective-permute-start.22 = (bf16[128,256]{1,0:T(8,128)(2,1)S(1)}, bf16[128,256]{1,0:T(8,128)(2,1)S(1)}, u32[]{:S(2)}, u32[]{:S(2)}) collective-permute-start(bf16[128,256]{1,0:T(8,128)(2,1)S(1)} %get-tuple-element.59), channel_id=1, source_target_pairs={{0,8},{1,9},{2,10},{3,11},{4,12},{5,13},{6,14},{7,15},{8,0},{9,1},... | collective-permute-start | bytes 196616 | tf_op jit(solution)/shard_map/ppermute | solution.py:58
  53.2 1.6 %collective-permute-start.25 = (bf16[128,256]{1,0:T(8,128)(2,1)S(1)}, bf16[128,256]{1,0:T(8,128)(2,1)S(1)}, u32[]{:S(2)}, u32[]{:S(2)}) collective-permute-start(bf16[128,256]{1,0:T(8,128)(2,1)S(1)} %collective-permute-done.21), channel_id=1, source_target_pairs={{0,8},{1,9},{2,10},{3,11},{4,12},{5,13},{6,14},{7,15},{8,0},{9,1},... | collective-permute-start | bytes 196616 | tf_op jit(solution)/shard_map/ppermute | solution.py:58
  (2 other events, 2.5 us)

commit v8 on v7

--- a/solution.py
+++ b/solution.py
@@ -13,7 +13,7 @@
 
 
 class Plan:
-    def __init__(self, mesh, psi, terms):
+    def __init__(self, mesh, psi, terms, swapped):
         self.op, self.sec = mesh.shape["op"], mesh.shape["sec"]
         self.held, self.blk = psi.shape[0], psi.shape[1]
         self.terms = terms
@@ -22,7 +22,7 @@
         while self.slots * self.op * 2**self.extra < self.held * self.sec:
             self.extra += 1
         order = list(range(self.sec.bit_length() - 1))
-        orders = [order, [order[1], order[0], *order[2:]]]
+        orders = [[order[1], order[0], *order[2:]] if swap else order for swap in swapped]
         self.inside = [x[: self.extra] for x in orders]
         self.bits = [x[self.extra :] for x in orders]
         self.places = (self.op // 2) * 2**self.extra
@@ -69,7 +69,8 @@
 
 def contract_kernel(plan, fetch, *refs):
     source, target, left, right, vector = refs[:5]
-    keep, give, refs = refs[5], refs[6], refs[7:]
+    count = 2 if fetch else plan.places
+    outs, refs = refs[5 : 5 + count], refs[5 + count :]
     if fetch:
         lhs, rhs, refs = refs[0], refs[1], refs[2:]
     else:
@@ -135,11 +136,13 @@
         tile = jnp.where(lane == core * plan.slots + j, labels[j].astype(jnp.float32), tile)
     tile = tile.astype(jnp.bfloat16)
     for m in range(plan.places):
-        for out, row in ((keep, plan.row(place ^ m, core)), (give, plan.row(other_place ^ m, 1 - core))):
+        for h, row in enumerate((plan.row(place ^ m, core), plan.row(other_place ^ m, 1 - core))):
+            out, base = (outs[h].at[m], 0) if fetch else (outs[m], h * plan.part)
             for j in range(plan.slots):
                 block = acc[j, pl.ds(row, plan.rows), :].astype(jnp.bfloat16)
-                out[m, pl.ds(j * plan.rows, plan.rows), :] = block
-            out[m, pl.ds(plan.part, LABEL_ROWS), :] = tile
+                out[pl.ds(base + j * plan.rows, plan.rows), :] = block
+            if fetch or h == 1:
+                out[pl.ds(base + plan.part, LABEL_ROWS), :] = tile
 
 
 def contract(plan, fetch, source, target, left, right, vector):
@@ -150,9 +153,11 @@
         pltpu.with_memory_space_constraint(x, space)
         for x, space in zip((source, target, left, right, vector), spaces)
     ]
-    out_shape = [pltpu.VMEM((plan.places, plan.part + LABEL_ROWS, blk), bf16)] * 2
     if fetch:
+        out_shape = [pltpu.VMEM((plan.places, plan.part + LABEL_ROWS, blk), bf16)] * 2
         out_shape += [pltpu.VMEM((terms, blk, blk), bf16)] * 2
+    else:
+        out_shape = [pltpu.VMEM((2 * plan.part + LABEL_ROWS, blk), bf16)] * plan.places
     return pl.pallas_call(
         functools.partial(contract_kernel, plan, fetch),
         in_specs=[pl.BlockSpec(memory_space=space) for space in spaces],
@@ -201,8 +206,8 @@
     )(*(pltpu.with_memory_space_constraint(x, pltpu.VMEM) for x in (kept, got)))
 
 
-def spread_kernel(plan, *refs):
-    n = plan.places
+def spread_kernel(plan, parts, *refs):
+    n = 1 + max(i for i, _ in parts)
     blocks, outs = refs[:n], refs[n : n + 2]
     acc, spots_vector, spots, sem = refs[n + 2 :]
     core, sec, _, _ = plan.here()
@@ -223,43 +228,42 @@
     copy.start()
     acc[...] = jnp.zeros_like(acc)
     copy.wait()
-    for i in range(n):
-        for h in range(2):
-            for j in range(plan.slots):
-                block = blocks[i][pl.ds(h * plan.part + j * plan.rows, plan.rows), :]
-                acc[spots[i, (core ^ h) * plan.slots + j]] += block.astype(jnp.float32)
+    for i, h in parts:
+        for j in range(plan.slots):
+            block = blocks[i][pl.ds(h * plan.part + j * plan.rows, plan.rows), :]
+            acc[spots[i, (core ^ h) * plan.slots + j]] += block.astype(jnp.float32)
     half = acc.shape[0] // 2
     for k, out in enumerate(outs):
         out[...] = acc[pl.ds((1 - k) * half, half)].astype(jnp.bfloat16).reshape(out.shape)
 
 
-def spread(plan, pieces):
+def spread(plan, pieces, parts, weight):
     blk, rows = plan.blk, plan.rows
     sectors = plan.held * plan.sec
     whole = pl.BlockSpec(memory_space=pltpu.VMEM)
     return pl.pallas_call(
-        functools.partial(spread_kernel, plan),
+        functools.partial(spread_kernel, plan, parts),
         in_specs=[whole] * len(pieces),
         out_specs=[whole] * 2,
         out_shape=[pltpu.VMEM((sectors // 2 * rows, blk), jnp.bfloat16)] * 2,
         scratch_shapes=[
             pltpu.VMEM((sectors, rows, blk), jnp.float32),
-            pltpu.VMEM((plan.places, 128), jnp.int32),
-            pltpu.SMEM((plan.places, 128), jnp.int32),
+            pltpu.VMEM((len(pieces), 128), jnp.int32),
+            pltpu.SMEM((len(pieces), 128), jnp.int32),
             pltpu.SemaphoreType.DMA,
         ],
-        cost_estimate=pl.CostEstimate(flops=1, bytes_accessed=1, transcendentals=0),
+        cost_estimate=pl.CostEstimate(flops=1, bytes_accessed=weight, transcendentals=0),
         compiler_params=pltpu.CompilerParams(vmem_limit_bytes=VMEM_LIMIT),
         name="spread",
     )(*(pltpu.with_memory_space_constraint(x, pltpu.VMEM) for x in pieces))
 
 
-def place_kernel(plan, *refs):
-    n = 2 * plan.places
+def place_kernel(plans, *refs):
+    n = 2 * plans[0].places
     inputs, outs, sems = refs[: 2 * n], refs[2 * n : -1], refs[-1]
-    core, _, place, other_place = plan.here()
     moving = []
-    for v, out in enumerate(outs):
+    for v, (plan, out) in enumerate(zip(plans, outs)):
+        core, _, place, other_place = plan.here()
         for m in range(plan.places):
             for h, row in enumerate((plan.row(place ^ m, core), plan.row(other_place ^ m, 1 - core))):
                 i = h * plan.places + m
@@ -271,14 +275,15 @@
         copy.wait()
 
 
-def assemble(plan, gathered):
+def assemble(plans, gathered):
+    plan = plans[0]
     pieces = [
         pltpu.with_memory_space_constraint(x.reshape(plan.held, plan.rows, plan.blk), pltpu.VMEM)
         for pieces in gathered
         for x in pieces
     ]
     return pl.pallas_call(
-        functools.partial(place_kernel, plan),
+        functools.partial(place_kernel, plans),
         in_specs=[pl.BlockSpec(memory_space=pltpu.VMEM)] * len(pieces),
         out_specs=[pl.BlockSpec(memory_space=pl.ANY)] * 2,
         out_shape=[jax.ShapeDtypeStruct((plan.held, plan.blk, plan.blk), jnp.bfloat16)] * 2,
@@ -301,9 +306,8 @@
     return total[middle:].astype(jnp.bfloat16), total[:middle]
 
 
-def trade(plan, kept, given):
-    pieces = merge(plan, kept, plan.to_core(given))
-    return pieces, [plan.across(pieces[m], m) for m in range(plan.places)]
+def trade(plan, pieces):
+    return [plan.across(x, m) for m, x in enumerate(pieces)]
 
 
 def gather(plan, total):
@@ -317,25 +321,33 @@
 
 
 def per_device(mesh, first, second, left, right, source, target):
-    plan = Plan(mesh, first, left.shape[0])
+    plan = Plan(mesh, first, left.shape[0], (False, True))
+    late_plan = Plan(mesh, first, left.shape[0], (True, True))
+    places = range(plan.places)
+
     kept, given, lhs, rhs = contract(plan, True, source, target, left, right, first)
-    pieces, early = trade(plan, kept, given)
-    kept, given = contract(plan, False, after(source, pieces[-1]), target, lhs, rhs, second)
-    early = after(early, kept)
-    _, late = trade(plan, kept, after(given, early))
-
-    away, kept = spread(plan, early)
+    merged = merge(plan, kept, plan.to_core(given))
+    early = trade(plan, merged)
+    pieces = contract(late_plan, False, after(source, merged[-1]), target, lhs, rhs, second)
+    early = after(early, pieces)
+    late = trade(late_plan, pieces)
+
+    away, kept = spread(plan, early, [(m, h) for m in places for h in range(2)], 3000000)
     arrived = plan.halve(0, away)
+    late = late[:1] + after(late[1:], away)
+    parts = [(h * plan.places + m, h) for h in range(2) for m in places]
+    late_away, late_kept = spread(late_plan, late + [late_plan.to_core(x) for x in late], parts, 100000000)
+    arrived = after(arrived, late_away)
+    late_arrived = late_plan.halve(0, late_away)
+
     for k in range(1, len(plan.bits[0])):
         away, kept = halves(add(arrived, kept))
         arrived = plan.halve(k, away)
-
-    late_away, late_kept = spread(plan, after(late, away))
-    late_arrived = plan.halve(0, late_away)
-    for k in range(1, len(plan.bits[0])):
-        late_away, late_kept = halves(add(late_arrived, late_kept))
-        late_arrived = plan.halve(k, late_away)
-    return tuple(assemble(plan, [gather(plan, add(arrived, kept)), gather(plan, add(late_arrived, late_kept))]))
+        away, late_kept = halves(add(late_arrived, late_kept))
+        arrived = after(arrived, away)
+        late_arrived = late_plan.halve(k, away)
+    gathered = gather(plan, add(arrived, kept)), gather(late_plan, add(late_arrived, late_kept))
+    return tuple(assemble((plan, late_plan), gathered))
 
 
 def solution(mesh):

time: 57.3 us -> 56.3 us (0.983)
  waiting for transfers between devices: 19.5 us -> 16.9 us
  starting transfers between devices: 24.5 us -> 26 us
    ppermute x4, waiting for transfers between devices: 8.57 us -> 4.19 us  [halve(): lax.ppermute(x, AXES, self.partners(0, [1 << bits[k] for bits in self.bit...]
    ppermute x10 -> x13, waiting for transfers between devices: 2.45 us -> 3.82 us  [to_core(): return lax.ppermute(x, AXES, self.partners(1, (0, 0)))]
    ppermute x4, starting transfers between devices: 8.08 us -> 8.88 us  [halve(): lax.ppermute(x, AXES, self.partners(0, [1 << bits[k] for bits in self.bit...]
    ppermute x10 -> x13, starting transfers between devices: 1.2 us -> 1.92 us  [to_core(): return lax.ppermute(x, AXES, self.partners(1, (0, 0)))]
  transfers between devices with their start and end apart: 26 -> 29, of which waited for: 13 -> 14; matrix products, arithmetic and copies ran while one was open for 0% -> 0% of each run, Pallas kernels for 10% -> 10%
where the time goes in v8:
time: 56.3 us; the launch traced here: 56.1 us
  starting transfers between devices  26 us (46%)
  waiting for transfers between devices  16.9 us (30%)
  Pallas kernels  12.3 us (22%)
  between operations  0.75 us (1%)
    ppermute x12, starting transfers between devices, across(): lax.ppermute(x, AXES, self.partners(mask >> self.extra << 1, sec_masks))  15.2 us
    pallas_call x2, Pallas kernels, contract(): pl.pallas_call(functools.partial(contract_kernel, plan, fetch), in_specs=...  9.3 us
    ppermute x4, starting transfers between devices, halve(): lax.ppermute(x, AXES, self.partners(0, [1 << bits[k] for bits in self.bit...  8.88 us
    ppermute x12, waiting for transfers between devices, across(): lax.ppermute(x, AXES, self.partners(mask >> self.extra << 1, sec_masks))  8.86 us
    ppermute x4, waiting for transfers between devices, halve(): lax.ppermute(x, AXES, self.partners(0, [1 << bits[k] for bits in self.bit...  4.19 us
    ppermute x13, waiting for transfers between devices, to_core(): return lax.ppermute(x, AXES, self.partners(1, (0, 0)))  3.82 us
    ppermute x13, starting transfers between devices, to_core(): return lax.ppermute(x, AXES, self.partners(1, (0, 0)))  1.92 us
    pallas_call x2, Pallas kernels, spread(): pl.pallas_call(functools.partial(spread_kernel, plan, parts), in_specs=[w...  1.82 us
  transfers between devices with their start and end apart: 29, of which 14 were waited for; matrix products, arithmetic and copies ran while one was open for 0% of the time, Pallas kernels for 10%

profile of v8, /device:TPU:0, one launch (start us, length us, event | category | flops | bytes accessed | tf_op | source)
XLA Modules:
  0.0 56.1 jit_solution(549626098685102536)
XLA Ops:
  0.6 5.5 %contract.2 = (bf16[4,144,256]{2,1,0:T(8,128)(2,1)S(1)}, bf16[4,144,256]{2,1,0:T(8,128)(2,1)S(1)}, bf16[32,256,256]{2,1,0:T(8,128)(2,1)S(1)}, bf16[32,256,256]{2,1,0:T(8,128)(2,1)S(1)}) custom-call(s32[32]{0:T(128)} %refs_0_.2, s32[32]{0:T(128)} %refs_1_.3, bf16[32,256,256]{2,1,0:T(8,128)(2,1)} %refs_2_.1, bf16[32,256,256]{2,1,0:T(8,128)(2,1)} %refs_3_.1, ...), custom_call_target="tpu_custom_call" | custom-call | flops 2147483648 | bytes 8388608 | tf_op jit(solution)/shard_map/contract/pallas_call | solution.py:161
  6.7 1.2 %collective-permute-done.got = bf16[4,144,256]{2,1,0:T(8,128)(2,1)S(1)} collective-permute-done((bf16[4,144,256]{2,1,0:T(8,128)(2,1)S(1)}, bf16[4,144,256]{2,1,0:T(8,128)(2,1)S(1)}, u32[]{:S(2)}, u32[]{:S(2)}) %collective-permute-start) | collective-permute-done | bytes 294944 | tf_op jit(solution)/shard_map/ppermute | solution.py:58
  7.9 3.9 %collective-permute-start.3 = (bf16[272,256]{1,0:T(8,128)(2,1)S(1)}, bf16[272,256]{1,0:T(8,128)(2,1)S(1)}, u32[]{:S(2)}, u32[]{:S(2)}) collective-permute-start(bf16[272,256]{1,0:T(8,128)(2,1)S(1)} %get-tuple-element.33), channel_id=1, source_target_pairs={{0,17},{1,16},{2,19},{3,18},{4,21},{5,20},{6,23},{7,22},{8,26},{9,... | collective-permute-start | bytes 417800 | tf_op jit(solution)/shard_map/ppermute | solution.py:64
  12.4 3.8 %contract.3 = (bf16[272,256]{1,0:T(8,128)(2,1)S(1)}, bf16[272,256]{1,0:T(8,128)(2,1)S(1)}, bf16[272,256]{1,0:T(8,128)(2,1)S(1)}, bf16[272,256]{1,0:T(8,128)(2,1)S(1)}) custom-call(s32[32]{0:T(128)} %refs_0_.2, s32[32]{0:T(128)} %refs_1_.3, bf16[32,256,256]{2,1,0:T(8,128)(2,1)S(1)} %get-tuple-element.35.refs_2_, ...), custom_call_target="tpu_custom_call" | custom-call | flops 2147483648 | bytes 8192 | tf_op jit(solution)/shard_map/contract/pallas_call | solution.py:161
  16.2 2.0 %collective-permute-start.5 = (bf16[272,256]{1,0:T(8,128)(2,1)S(1)}, bf16[272,256]{1,0:T(8,128)(2,1)S(1)}, u32[]{:S(2)}, u32[]{:S(2)}) collective-permute-start(bf16[272,256]{1,0:T(8,128)(2,1)S(1)} %get-tuple-element.38), channel_id=1, source_target_pairs={{0,2},{1,3},{2,0},{3,1},{4,6},{5,7},{6,4},{7,5},{8,10},{9,11},{10,... | collective-permute-start | bytes 417800 | tf_op jit(solution)/shard_map/ppermute | solution.py:64
  18.3 1.5 %collective-permute-start.6 = (bf16[272,256]{1,0:T(8,128)(2,1)S(1)}, bf16[272,256]{1,0:T(8,128)(2,1)S(1)}, u32[]{:S(2)}, u32[]{:S(2)}) collective-permute-start(bf16[272,256]{1,0:T(8,128)(2,1)S(1)} %get-tuple-element.39), channel_id=1, source_target_pairs={{0,16},{1,17},{2,18},{3,19},{4,20},{5,21},{6,22},{7,23},{8,24},{9,... | collective-permute-start | bytes 417800 | tf_op jit(solution)/shard_map/ppermute | solution.py:64
  19.8 0.9 %spread.2 = (bf16[512,256]{1,0:T(8,128)(2,1)S(1)}, bf16[512,256]{1,0:T(8,128)(2,1)S(1)}) custom-call(bf16[272,256]{1,0:T(8,128)(2,1)S(1)} %get-tuple-element.41.refs_0_, bf16[272,256]{1,0:T(8,128)(2,1)S(1)} %collective-permute-done.1.refs_1_, bf16[272,256]{1,0:T(8,128)(2,1)S(1)} %collective-permute-done.2.refs_2_, ...), custom_call_target="tpu_custom_call" | custom-call | flops 1 | bytes 3000000 | tf_op jit(solution)/shard_map/spread/pallas_call | solution.py:244
  20.7 2.0 %collective-permute-start.4 = (bf16[512,256]{1,0:T(8,128)(2,1)S(1)}, bf16[512,256]{1,0:T(8,128)(2,1)S(1)}, u32[]{:S(2)}, u32[]{:S(2)}) collective-permute-start(bf16[512,256]{1,0:T(8,128)(2,1)S(1)} %get-tuple-element.46), channel_id=1, source_target_pairs={{0,2},{1,3},{2,0},{3,1},{4,6},{5,7},{6,4},{7,5},{8,9},{9,8},{10,11... | collective-permute-start | bytes 786440 | tf_op jit(solution)/shard_map/ppermute | solution.py:67
  22.8 3.6 %collective-permute-done.6.refs_2_ = bf16[272,256]{1,0:T(8,128)(2,1)S(1)} collective-permute-done((bf16[272,256]{1,0:T(8,128)(2,1)S(1)}, bf16[272,256]{1,0:T(8,128)(2,1)S(1)}, u32[]{:S(2)}, u32[]{:S(2)}) %collective-permute-start.6) | collective-permute-done | bytes 139296 | tf_op jit(solution)/shard_map/ppermute | solution.py:64
  26.8 0.8 %collective-permute-done.9.refs_5_ = bf16[272,256]{1,0:T(8,128)(2,1)S(1)} collective-permute-done((bf16[272,256]{1,0:T(8,128)(2,1)S(1)}, bf16[272,256]{1,0:T(8,128)(2,1)S(1)}, u32[]{:S(2)}, u32[]{:S(2)}) %collective-permute-start.9) | collective-permute-done | bytes 139296 | tf_op jit(solution)/shard_map/ppermute | solution.py:58
  28.2 0.9 %spread.3 = (bf16[512,256]{1,0:T(8,128)(2,1)S(1)}, bf16[512,256]{1,0:T(8,128)(2,1)S(1)}) custom-call(bf16[272,256]{1,0:T(8,128)(2,1)S(1)} %get-tuple-element.37.refs_0_, bf16[272,256]{1,0:T(8,128)(2,1)S(1)} %collective-permute-done.5.refs_1_, bf16[272,256]{1,0:T(8,128)(2,1)S(1)} %collective-permute-done.6.refs_2_, ...), custom_call_target="tpu_custom_call" | custom-call | flops 1 | bytes 100000000 | tf_op jit(solution)/shard_map/spread/pallas_call | solution.py:244
  29.1 1.6 %collective-permute-start.13 = (bf16[512,256]{1,0:T(8,128)(2,1)S(1)}, bf16[512,256]{1,0:T(8,128)(2,1)S(1)}, u32[]{:S(2)}, u32[]{:S(2)}) collective-permute-start(bf16[512,256]{1,0:T(8,128)(2,1)S(1)} %get-tuple-element.50), channel_id=1, source_target_pairs={{0,1},{1,0},{2,3},{3,2},{4,5},{5,4},{6,7},{7,6},{8,9},{9,8},{10,11... | collective-permute-start | bytes 786440 | tf_op jit(solution)/shard_map/ppermute | solution.py:67
  30.8 2.7 %collective-permute-start.12 = (bf16[256,256]{1,0:T(8,128)(2,1)S(1)}, bf16[256,256]{1,0:T(8,128)(2,1)S(1)}, u32[]{:S(2)}, u32[]{:S(2)}) collective-permute-start(bf16[256,256]{1,0:T(8,128)(2,1)S(1)} %slice.55), channel_id=1, source_target_pairs={{0,4},{1,5},{2,6},{3,7},{4,0},{5,1},{6,2},{7,3},{8,12},{9,13},{10,... | collective-permute-start | bytes 393224 | tf_op jit(solution)/shard_map/ppermute | solution.py:67
  33.4 4.2 %collective-permute-done.13 = bf16[512,256]{1,0:T(8,128)(2,1)S(1)} collective-permute-done((bf16[512,256]{1,0:T(8,128)(2,1)S(1)}, bf16[512,256]{1,0:T(8,128)(2,1)S(1)}, u32[]{:S(2)}, u32[]{:S(2)}) %collective-permute-start.13) | collective-permute-done | bytes 262176 | tf_op jit(solution)/shard_map/ppermute | solution.py:67
  37.7 2.7 %collective-permute-start.21 = (bf16[256,256]{1,0:T(8,128)(2,1)S(1)}, bf16[256,256]{1,0:T(8,128)(2,1)S(1)}, u32[]{:S(2)}, u32[]{:S(2)}) collective-permute-start(bf16[256,256]{1,0:T(8,128)(2,1)S(1)} %slice.54), channel_id=1, source_target_pairs={{0,4},{1,5},{2,6},{3,7},{4,0},{5,1},{6,2},{7,3},{8,12},{9,13},{10,... | collective-permute-start | bytes 393224 | tf_op jit(solution)/shard_map/ppermute | solution.py:67
  40.4 2.1 %collective-permute-start.16 = (bf16[128,256]{1,0:T(8,128)(2,1)S(1)}, bf16[128,256]{1,0:T(8,128)(2,1)S(1)}, u32[]{:S(2)}, u32[]{:S(2)}) collective-permute-start(bf16[128,256]{1,0:T(8,128)(2,1)S(1)} %get-tuple-element.56), channel_id=1, source_target_pairs={{0,17},{1,16},{2,19},{3,18},{4,21},{5,20},{6,23},{7,22},{8,26},{9,... | collective-permute-start | bytes 196616 | tf_op jit(solution)/shard_map/ppermute | solution.py:64
  43.0 0.9 %collective-permute-start.15 = (bf16[128,256]{1,0:T(8,128)(2,1)S(1)}, bf16[128,256]{1,0:T(8,128)(2,1)S(1)}, u32[]{:S(2)}, u32[]{:S(2)}) collective-permute-start(bf16[128,256]{1,0:T(8,128)(2,1)S(1)} %get-tuple-element.57), channel_id=1, source_target_pairs={{0,16},{1,17},{2,18},{3,19},{4,20},{5,21},{6,22},{7,23},{8,24},{9,... | collective-permute-start | bytes 196616 | tf_op jit(solution)/shard_map/ppermute | solution.py:64
  44.0 1.7 %collective-permute-done.16 = bf16[128,256]{1,0:T(8,128)(2,1)S(1)} collective-permute-done((bf16[128,256]{1,0:T(8,128)(2,1)S(1)}, bf16[128,256]{1,0:T(8,128)(2,1)S(1)}, u32[]{:S(2)}, u32[]{:S(2)}) %collective-permute-start.16) | collective-permute-done | bytes 65568 | tf_op jit(solution)/shard_map/ppermute | solution.py:64
  45.7 1.1 %collective-permute-done.14 = bf16[128,256]{1,0:T(8,128)(2,1)S(1)} collective-permute-done((bf16[128,256]{1,0:T(8,128)(2,1)S(1)}, bf16[128,256]{1,0:T(8,128)(2,1)S(1)}, u32[]{:S(2)}, u32[]{:S(2)}) %collective-permute-start.14) | collective-permute-done | bytes 65568 | tf_op jit(solution)/shard_map/ppermute | solution.py:64
  47.0 1.0 %collective-permute-start.24 = (bf16[128,256]{1,0:T(8,128)(2,1)S(1)}, bf16[128,256]{1,0:T(8,128)(2,1)S(1)}, u32[]{:S(2)}, u32[]{:S(2)}) collective-permute-start(bf16[128,256]{1,0:T(8,128)(2,1)S(1)} %get-tuple-element.54), channel_id=1, source_target_pairs={{0,18},{1,19},{2,16},{3,17},{4,22},{5,23},{6,20},{7,21},{8,26},{9,... | collective-permute-start | bytes 196616 | tf_op jit(solution)/shard_map/ppermute | solution.py:64
  48.0 1.5 %collective-permute-start.22 = (bf16[128,256]{1,0:T(8,128)(2,1)S(1)}, bf16[128,256]{1,0:T(8,128)(2,1)S(1)}, u32[]{:S(2)}, u32[]{:S(2)}) collective-permute-start(bf16[128,256]{1,0:T(8,128)(2,1)S(1)} %get-tuple-element.54), channel_id=1, source_target_pairs={{0,2},{1,3},{2,0},{3,1},{4,6},{5,7},{6,4},{7,5},{8,10},{9,11},{10,... | collective-permute-start | bytes 196616 | tf_op jit(solution)/shard_map/ppermute | solution.py:64
  49.5 1.1 %collective-permute-start.23 = (bf16[128,256]{1,0:T(8,128)(2,1)S(1)}, bf16[128,256]{1,0:T(8,128)(2,1)S(1)}, u32[]{:S(2)}, u32[]{:S(2)}) collective-permute-start(bf16[128,256]{1,0:T(8,128)(2,1)S(1)} %get-tuple-element.55), channel_id=1, source_target_pairs={{0,16},{1,17},{2,18},{3,19},{4,20},{5,21},{6,22},{7,23},{8,24},{9,... | collective-permute-start | bytes 196616 | tf_op jit(solution)/shard_map/ppermute | solution.py:64
  51.1 1.8 %collective-permute-done.24 = bf16[128,256]{1,0:T(8,128)(2,1)S(1)} collective-permute-done((bf16[128,256]{1,0:T(8,128)(2,1)S(1)}, bf16[128,256]{1,0:T(8,128)(2,1)S(1)}, u32[]{:S(2)}, u32[]{:S(2)}) %collective-permute-start.24) | collective-permute-done | bytes 65568 | tf_op jit(solution)/shard_map/ppermute | solution.py:64
  55.0 1.1 %assemble.1 = (bf16[4,256,256]{2,1,0:T(8,128)(2,1)}, bf16[4,256,256]{2,1,0:T(8,128)(2,1)}) custom-call(bf16[4,32,256]{2,1,0:T(8,128)(2,1)S(1)} %bitcast.16, bf16[4,32,256]{2,1,0:T(8,128)(2,1)S(1)} %bitcast.19, bf16[4,32,256]{2,1,0:T(8,128)(2,1)S(1)} %bitcast.21, bf16[4,32,256]{2,1,0:T(8,128)(2,1)S(1)} %bitcast.18, bf16[4,32,256]{2,1,0:T(8,128)(2,1)S(1)} %bitcast.20, ...), custom_call_target="tpu_custom_call" | custom-call | tf_op jit(solution)/shard_map/assemble/pallas_call | solution.py:285
  (48 shorter events, 5.9 us)
Async XLA Ops:
  6.1 1.7 %collective-permute-start = (bf16[4,144,256]{2,1,0:T(8,128)(2,1)S(1)}, bf16[4,144,256]{2,1,0:T(8,128)(2,1)S(1)}, u32[]{:S(2)}, u32[]{:S(2)}) collective-permute-start(bf16[4,144,256]{2,1,0:T(8,128)(2,1)S(1)} %get-tuple-element.29), channel_id=1, source_target_pairs={{0,8},{1,9},{2,10},{3,11},{4,12},{5,13},{6,14},{7,15},{8,0},{9,1},... | collective-permute-start | bytes 884744 | tf_op jit(solution)/shard_map/ppermute | solution.py:58
  7.9 11.9 %collective-permute-start.3 = (bf16[272,256]{1,0:T(8,128)(2,1)S(1)}, bf16[272,256]{1,0:T(8,128)(2,1)S(1)}, u32[]{:S(2)}, u32[]{:S(2)}) collective-permute-start(bf16[272,256]{1,0:T(8,128)(2,1)S(1)} %get-tuple-element.33), channel_id=1, source_target_pairs={{0,17},{1,16},{2,19},{3,18},{4,21},{5,20},{6,23},{7,22},{8,26},{9,... | collective-permute-start | bytes 417800 | tf_op jit(solution)/shard_map/ppermute | solution.py:64
  11.8 8.0 %collective-permute-start.1 = (bf16[272,256]{1,0:T(8,128)(2,1)S(1)}, bf16[272,256]{1,0:T(8,128)(2,1)S(1)}, u32[]{:S(2)}, u32[]{:S(2)}) collective-permute-start(bf16[272,256]{1,0:T(8,128)(2,1)S(1)} %get-tuple-element.31), channel_id=1, source_target_pairs={{0,1},{1,0},{2,3},{3,2},{4,5},{5,4},{6,7},{7,6},{8,10},{9,11},{10,... | collective-permute-start | bytes 417800 | tf_op jit(solution)/shard_map/ppermute | solution.py:64
  12.3 7.5 %collective-permute-start.2 = (bf16[272,256]{1,0:T(8,128)(2,1)S(1)}, bf16[272,256]{1,0:T(8,128)(2,1)S(1)}, u32[]{:S(2)}, u32[]{:S(2)}) collective-permute-start(bf16[272,256]{1,0:T(8,128)(2,1)S(1)} %get-tuple-element.32), channel_id=1, source_target_pairs={{0,16},{1,17},{2,18},{3,19},{4,20},{5,21},{6,22},{7,23},{8,24},{9,... | collective-permute-start | bytes 417800 | tf_op jit(solution)/shard_map/ppermute | solution.py:64
  16.2 6.5 %collective-permute-start.5 = (bf16[272,256]{1,0:T(8,128)(2,1)S(1)}, bf16[272,256]{1,0:T(8,128)(2,1)S(1)}, u32[]{:S(2)}, u32[]{:S(2)}) collective-permute-start(bf16[272,256]{1,0:T(8,128)(2,1)S(1)} %get-tuple-element.38), channel_id=1, source_target_pairs={{0,2},{1,3},{2,0},{3,1},{4,6},{5,7},{6,4},{7,5},{8,10},{9,11},{10,... | collective-permute-start | bytes 417800 | tf_op jit(solution)/shard_map/ppermute | solution.py:64
  18.3 8.0 %collective-permute-start.6 = (bf16[272,256]{1,0:T(8,128)(2,1)S(1)}, bf16[272,256]{1,0:T(8,128)(2,1)S(1)}, u32[]{:S(2)}, u32[]{:S(2)}) collective-permute-start(bf16[272,256]{1,0:T(8,128)(2,1)S(1)} %get-tuple-element.39), channel_id=1, source_target_pairs={{0,16},{1,17},{2,18},{3,19},{4,20},{5,21},{6,22},{7,23},{8,24},{9,... | collective-permute-start | bytes 417800 | tf_op jit(solution)/shard_map/ppermute | solution.py:64
  19.8 6.5 %collective-permute-start.7 = (bf16[272,256]{1,0:T(8,128)(2,1)S(1)}, bf16[272,256]{1,0:T(8,128)(2,1)S(1)}, u32[]{:S(2)}, u32[]{:S(2)}) collective-permute-start(bf16[272,256]{1,0:T(8,128)(2,1)S(1)} %get-tuple-element.40), channel_id=1, source_target_pairs={{0,18},{1,19},{2,16},{3,17},{4,22},{5,23},{6,20},{7,21},{8,26},{9,... | collective-permute-start | bytes 417800 | tf_op jit(solution)/shard_map/ppermute | solution.py:64
  20.7 10.0 %collective-permute-start.4 = (bf16[512,256]{1,0:T(8,128)(2,1)S(1)}, bf16[512,256]{1,0:T(8,128)(2,1)S(1)}, u32[]{:S(2)}, u32[]{:S(2)}) collective-permute-start(bf16[512,256]{1,0:T(8,128)(2,1)S(1)} %get-tuple-element.46), channel_id=1, source_target_pairs={{0,2},{1,3},{2,0},{3,1},{4,6},{5,7},{6,4},{7,5},{8,9},{9,8},{10,11... | collective-permute-start | bytes 786440 | tf_op jit(solution)/shard_map/ppermute | solution.py:67
  22.8 4.1 %collective-permute-start.8 = (bf16[272,256]{1,0:T(8,128)(2,1)S(1)}, bf16[272,256]{1,0:T(8,128)(2,1)S(1)}, u32[]{:S(2)}, u32[]{:S(2)}) collective-permute-start(bf16[272,256]{1,0:T(8,128)(2,1)S(1)} %get-tuple-element.37.refs_0_), channel_id=1, source_target_pairs={{0,8},{1,9},{2,10},{3,11},{4,12},{5,13},{6,14},{7,15},{8,0},{9,1},... | collective-permute-start | bytes 417800 | tf_op jit(solution)/shard_map/ppermute | solution.py:58
  26.3 1.6 %collective-permute-start.10 = (bf16[272,256]{1,0:T(8,128)(2,1)S(1)}, bf16[272,256]{1,0:T(8,128)(2,1)S(1)}, u32[]{:S(2)}, u32[]{:S(2)}) collective-permute-start(bf16[272,256]{1,0:T(8,128)(2,1)S(1)} %collective-permute-done.6.refs_2_), channel_id=1, source_target_pairs={{0,8},{1,9},{2,10},{3,11},{4,12},{5,13},{6,14},{7,15},{8,0},{9,1},... | collective-permute-start | bytes 417800 | tf_op jit(solution)/shard_map/ppermute | solution.py:58
  29.1 8.5 %collective-permute-start.13 = (bf16[512,256]{1,0:T(8,128)(2,1)S(1)}, bf16[512,256]{1,0:T(8,128)(2,1)S(1)}, u32[]{:S(2)}, u32[]{:S(2)}) collective-permute-start(bf16[512,256]{1,0:T(8,128)(2,1)S(1)} %get-tuple-element.50), channel_id=1, source_target_pairs={{0,1},{1,0},{2,3},{3,2},{4,5},{5,4},{6,7},{7,6},{8,9},{9,8},{10,11... | collective-permute-start | bytes 786440 | tf_op jit(solution)/shard_map/ppermute | solution.py:67
  30.8 9.6 %collective-permute-start.12 = (bf16[256,256]{1,0:T(8,128)(2,1)S(1)}, bf16[256,256]{1,0:T(8,128)(2,1)S(1)}, u32[]{:S(2)}, u32[]{:S(2)}) collective-permute-start(bf16[256,256]{1,0:T(8,128)(2,1)S(1)} %slice.55), channel_id=1, source_target_pairs={{0,4},{1,5},{2,6},{3,7},{4,0},{5,1},{6,2},{7,3},{8,12},{9,13},{10,... | collective-permute-start | bytes 393224 | tf_op jit(solution)/shard_map/ppermute | solution.py:67
  37.7 9.2 %collective-permute-start.21 = (bf16[256,256]{1,0:T(8,128)(2,1)S(1)}, bf16[256,256]{1,0:T(8,128)(2,1)S(1)}, u32[]{:S(2)}, u32[]{:S(2)}) collective-permute-start(bf16[256,256]{1,0:T(8,128)(2,1)S(1)} %slice.54), channel_id=1, source_target_pairs={{0,4},{1,5},{2,6},{3,7},{4,0},{5,1},{6,2},{7,3},{8,12},{9,13},{10,... | collective-permute-start | bytes 393224 | tf_op jit(solution)/shard_map/ppermute | solution.py:67
  40.4 5.2 %collective-permute-start.16 = (bf16[128,256]{1,0:T(8,128)(2,1)S(1)}, bf16[128,256]{1,0:T(8,128)(2,1)S(1)}, u32[]{:S(2)}, u32[]{:S(2)}) collective-permute-start(bf16[128,256]{1,0:T(8,128)(2,1)S(1)} %get-tuple-element.56), channel_id=1, source_target_pairs={{0,17},{1,16},{2,19},{3,18},{4,21},{5,20},{6,23},{7,22},{8,26},{9,... | collective-permute-start | bytes 196616 | tf_op jit(solution)/shard_map/ppermute | solution.py:64
  42.5 4.3 %collective-permute-start.14 = (bf16[128,256]{1,0:T(8,128)(2,1)S(1)}, bf16[128,256]{1,0:T(8,128)(2,1)S(1)}, u32[]{:S(2)}, u32[]{:S(2)}) collective-permute-start(bf16[128,256]{1,0:T(8,128)(2,1)S(1)} %get-tuple-element.56), channel_id=1, source_target_pairs={{0,1},{1,0},{2,3},{3,2},{4,5},{5,4},{6,7},{7,6},{8,10},{9,11},{10,... | collective-permute-start | bytes 196616 | tf_op jit(solution)/shard_map/ppermute | solution.py:64
  43.0 5.0 %collective-permute-start.17 = (bf16[128,256]{1,0:T(8,128)(2,1)S(1)}, bf16[128,256]{1,0:T(8,128)(2,1)S(1)}, u32[]{:S(2)}, u32[]{:S(2)}) collective-permute-start(bf16[128,256]{1,0:T(8,128)(2,1)S(1)} %get-tuple-element.57), channel_id=1, source_target_pairs={{0,8},{1,9},{2,10},{3,11},{4,12},{5,13},{6,14},{7,15},{8,0},{9,1},... | collective-permute-start | bytes 196616 | tf_op jit(solution)/shard_map/ppermute | solution.py:58
  43.0 6.5 %collective-permute-start.15 = (bf16[128,256]{1,0:T(8,128)(2,1)S(1)}, bf16[128,256]{1,0:T(8,128)(2,1)S(1)}, u32[]{:S(2)}, u32[]{:S(2)}) collective-permute-start(bf16[128,256]{1,0:T(8,128)(2,1)S(1)} %get-tuple-element.57), channel_id=1, source_target_pairs={{0,16},{1,17},{2,18},{3,19},{4,20},{5,21},{6,22},{7,23},{8,24},{9,... | collective-permute-start | bytes 196616 | tf_op jit(solution)/shard_map/ppermute | solution.py:64
  45.6 4.9 %collective-permute-start.20 = (bf16[128,256]{1,0:T(8,128)(2,1)S(1)}, bf16[128,256]{1,0:T(8,128)(2,1)S(1)}, u32[]{:S(2)}, u32[]{:S(2)}) collective-permute-start(bf16[128,256]{1,0:T(8,128)(2,1)S(1)} %collective-permute-done.16), channel_id=1, source_target_pairs={{0,8},{1,9},{2,10},{3,11},{4,12},{5,13},{6,14},{7,15},{8,0},{9,1},... | collective-permute-start | bytes 196616 | tf_op jit(solution)/shard_map/ppermute | solution.py:58
  46.8 3.8 %collective-permute-start.18 = (bf16[128,256]{1,0:T(8,128)(2,1)S(1)}, bf16[128,256]{1,0:T(8,128)(2,1)S(1)}, u32[]{:S(2)}, u32[]{:S(2)}) collective-permute-start(bf16[128,256]{1,0:T(8,128)(2,1)S(1)} %collective-permute-done.14), channel_id=1, source_target_pairs={{0,8},{1,9},{2,10},{3,11},{4,12},{5,13},{6,14},{7,15},{8,0},{9,1},... | collective-permute-start | bytes 196616 | tf_op jit(solution)/shard_map/ppermute | solution.py:58
  47.0 5.9 %collective-permute-start.24 = (bf16[128,256]{1,0:T(8,128)(2,1)S(1)}, bf16[128,256]{1,0:T(8,128)(2,1)S(1)}, u32[]{:S(2)}, u32[]{:S(2)}) collective-permute-start(bf16[128,256]{1,0:T(8,128)(2,1)S(1)} %get-tuple-element.54), channel_id=1, source_target_pairs={{0,18},{1,19},{2,16},{3,17},{4,22},{5,23},{6,20},{7,21},{8,26},{9,... | collective-permute-start | bytes 196616 | tf_op jit(solution)/shard_map/ppermute | solution.py:64
  48.0 5.1 %collective-permute-start.22 = (bf16[128,256]{1,0:T(8,128)(2,1)S(1)}, bf16[128,256]{1,0:T(8,128)(2,1)S(1)}, u32[]{:S(2)}, u32[]{:S(2)}) collective-permute-start(bf16[128,256]{1,0:T(8,128)(2,1)S(1)} %get-tuple-element.54), channel_id=1, source_target_pairs={{0,2},{1,3},{2,0},{3,1},{4,6},{5,7},{6,4},{7,5},{8,10},{9,11},{10,... | collective-permute-start | bytes 196616 | tf_op jit(solution)/shard_map/ppermute | solution.py:64
  49.5 4.3 %collective-permute-start.23 = (bf16[128,256]{1,0:T(8,128)(2,1)S(1)}, bf16[128,256]{1,0:T(8,128)(2,1)S(1)}, u32[]{:S(2)}, u32[]{:S(2)}) collective-permute-start(bf16[128,256]{1,0:T(8,128)(2,1)S(1)} %get-tuple-element.55), channel_id=1, source_target_pairs={{0,16},{1,17},{2,18},{3,19},{4,20},{5,21},{6,22},{7,23},{8,24},{9,... | collective-permute-start | bytes 196616 | tf_op jit(solution)/shard_map/ppermute | solution.py:64
  50.6 3.2 %collective-permute-start.19 = (bf16[128,256]{1,0:T(8,128)(2,1)S(1)}, bf16[128,256]{1,0:T(8,128)(2,1)S(1)}, u32[]{:S(2)}, u32[]{:S(2)}) collective-permute-start(bf16[128,256]{1,0:T(8,128)(2,1)S(1)} %collective-permute-done.15), channel_id=1, source_target_pairs={{0,8},{1,9},{2,10},{3,11},{4,12},{5,13},{6,14},{7,15},{8,0},{9,1},... | collective-permute-start | bytes 196616 | tf_op jit(solution)/shard_map/ppermute | solution.py:58
  50.6 3.2 %collective-permute-start.25 = (bf16[128,256]{1,0:T(8,128)(2,1)S(1)}, bf16[128,256]{1,0:T(8,128)(2,1)S(1)}, u32[]{:S(2)}, u32[]{:S(2)}) collective-permute-start(bf16[128,256]{1,0:T(8,128)(2,1)S(1)} %get-tuple-element.55), channel_id=1, source_target_pairs={{0,8},{1,9},{2,10},{3,11},{4,12},{5,13},{6,14},{7,15},{8,0},{9,1},... | collective-permute-start | bytes 196616 | tf_op jit(solution)/shard_map/ppermute | solution.py:58
  (5 other events, 6.5 us)

commit v9 on v8

--- a/solution.py
+++ b/solution.py
@@ -68,23 +68,28 @@
 
 
 def contract_kernel(plan, fetch, *refs):
-    source, target, left, right, vector = refs[:5]
+    blk, terms, step = plan.blk, plan.terms, plan.step
+    if fetch:
+        source, target, left, right, vector, later, *refs = refs
+    else:
+        notes, lhs, rhs, psi, *refs = refs
     count = 2 if fetch else plan.places
-    outs, refs = refs[5 : 5 + count], refs[5 + count :]
-    if fetch:
-        lhs, rhs, refs = refs[0], refs[1], refs[2:]
-    else:
-        lhs, rhs = left, right
-    src, tgt, psi, acc, slot_of, labels, seen, sems, first_sems = refs
-    blk, terms, step = plan.blk, plan.terms, plan.step
+    outs, refs = refs[:count], refs[count:]
+    if fetch:
+        notes, lhs, rhs, psi_out, *refs = refs
+        tgt, src, seen, psi, sems, first_sems, *refs = refs
+    table, acc, sem = refs
     chunks = terms // step if fetch else 0
-
-    heads = [
-        pltpu.make_async_copy(x, y, first_sems.at[i])
-        for i, (x, y) in enumerate(((target, tgt), (source, src), (vector, psi)))
-    ]
-    for copy in heads:
-        copy.start()
+    acc[...] = jnp.zeros_like(acc)
+
+    if fetch:
+        heads = [
+            pltpu.make_async_copy(x, y, first_sems.at[i])
+            for i, (x, y) in enumerate(((target, tgt), (source, src), (vector, psi)))
+        ]
+        tail = pltpu.make_async_copy(later, psi_out, first_sems.at[3])
+        for copy in heads:
+            copy.start()
 
     def loads(c):
         part = pl.ds(c * step, step)
@@ -97,13 +102,8 @@
         if c < chunks:
             for copy in loads(c):
                 copy.start()
-
-    for c in range(plan.window):
-        begin(c)
-    for h in range(plan.sec):
-        seen[h] = -1
-    acc[...] = jnp.zeros_like(acc)
-    heads[0].wait()
+        elif c == chunks:
+            tail.start()
 
     def name(t, count):
         goal = tgt[t]
@@ -111,21 +111,34 @@
         fresh = seen[holder] < 0
         slot = jnp.where(fresh, count, seen[holder])
         seen[holder] = slot
-        labels[slot] = goal
-        slot_of[t] = slot
+        table[2, slot] = goal
+        table[1, t] = slot
+        table[0, t] = src[t]
         return count + fresh.astype(jnp.int32)
 
-    lax.fori_loop(0, terms, name, jnp.int32(0))
-    for copy in heads[1:]:
+    if fetch:
+        for c in range(plan.window):
+            begin(c)
+        for h in range(plan.sec):
+            seen[h] = -1
+        heads[0].wait()
+        heads[1].wait()
+        lax.fori_loop(0, terms, name, jnp.int32(0))
+        heads[2].wait()
+        copy = pltpu.make_async_copy(table, notes, sem)
+        copy.start()
+    else:
+        copy = pltpu.make_async_copy(notes, table, sem)
+        copy.start()
         copy.wait()
 
     for t in range(terms):
         if fetch and t % step == 0:
-            for copy in loads(t // step):
-                copy.wait()
+            for part in loads(t // step):
+                part.wait()
             begin(t // step + plan.window)
-        half = jnp.dot(lhs[t], psi[src[t]], preferred_element_type=jnp.float32).astype(jnp.bfloat16)
-        acc[slot_of[t]] += lax.dot_general(
+        half = jnp.dot(lhs[t], psi[table[0, t]], preferred_element_type=jnp.float32).astype(jnp.bfloat16)
+        acc[table[1, t]] += lax.dot_general(
             half, rhs[t], (((1,), (1,)), ((), ())), preferred_element_type=jnp.float32
         )
 
@@ -133,7 +146,7 @@
     lane = lax.broadcasted_iota(jnp.int32, (LABEL_ROWS, blk), 1)
     tile = jnp.zeros((LABEL_ROWS, blk), jnp.float32)
     for j in range(plan.slots):
-        tile = jnp.where(lane == core * plan.slots + j, labels[j].astype(jnp.float32), tile)
+        tile = jnp.where(lane == core * plan.slots + j, table[2, j].astype(jnp.float32), tile)
     tile = tile.astype(jnp.bfloat16)
     for m in range(plan.places):
         for h, row in enumerate((plan.row(place ^ m, core), plan.row(other_place ^ m, 1 - core))):
@@ -143,37 +156,43 @@
                 out[pl.ds(base + j * plan.rows, plan.rows), :] = block
             if fetch or h == 1:
                 out[pl.ds(base + plan.part, LABEL_ROWS), :] = tile
-
-
-def contract(plan, fetch, source, target, left, right, vector):
+    if fetch:
+        copy.wait()
+        tail.wait()
+
+
+def contract(plan, fetch, *arrays):
     blk, terms = plan.blk, plan.terms
     bf16 = jnp.bfloat16
-    spaces = [pltpu.HBM, pltpu.HBM, *[pltpu.HBM if fetch else pltpu.VMEM] * 2, pltpu.HBM]
-    arrays = [
-        pltpu.with_memory_space_constraint(x, space)
-        for x, space in zip((source, target, left, right, vector), spaces)
+    space = pltpu.HBM if fetch else pltpu.VMEM
+    scratch = [
+        pltpu.SMEM((8, 128), jnp.int32),
+        pltpu.VMEM((plan.slots, blk, blk), jnp.float32),
+        pltpu.SemaphoreType.DMA,
     ]
     if fetch:
         out_shape = [pltpu.VMEM((plan.places, plan.part + LABEL_ROWS, blk), bf16)] * 2
-        out_shape += [pltpu.VMEM((terms, blk, blk), bf16)] * 2
+        out_shape += [
+            pltpu.VMEM((8, 128), jnp.int32),
+            *[pltpu.VMEM((terms, blk, blk), bf16)] * 2,
+            pltpu.VMEM((plan.held, blk, blk), bf16),
+        ]
+        scratch = [
+            pltpu.SMEM((terms,), jnp.int32),
+            pltpu.SMEM((terms,), jnp.int32),
+            pltpu.SMEM((plan.sec,), jnp.int32),
+            pltpu.VMEM((plan.held, blk, blk), bf16),
+            pltpu.SemaphoreType.DMA((2, terms // plan.step)),
+            pltpu.SemaphoreType.DMA((4,)),
+        ] + scratch
     else:
         out_shape = [pltpu.VMEM((2 * plan.part + LABEL_ROWS, blk), bf16)] * plan.places
     return pl.pallas_call(
         functools.partial(contract_kernel, plan, fetch),
-        in_specs=[pl.BlockSpec(memory_space=space) for space in spaces],
+        in_specs=[pl.BlockSpec(memory_space=space)] * len(arrays),
         out_specs=[pl.BlockSpec(memory_space=pltpu.VMEM)] * len(out_shape),
         out_shape=out_shape,
-        scratch_shapes=[
-            pltpu.SMEM((terms,), jnp.int32),
-            pltpu.SMEM((terms,), jnp.int32),
-            pltpu.VMEM((plan.held, blk, blk), bf16),
-            pltpu.VMEM((plan.slots, blk, blk), jnp.float32),
-            pltpu.SMEM((terms,), jnp.int32),
-            pltpu.SMEM((plan.slots,), jnp.int32),
-            pltpu.SMEM((plan.sec,), jnp.int32),
-            pltpu.SemaphoreType.DMA((2, terms // plan.step)),
-            pltpu.SemaphoreType.DMA((3,)),
-        ],
+        scratch_shapes=scratch,
         cost_estimate=pl.CostEstimate(
             flops=4 * terms * blk**3,
             bytes_accessed=4 * terms * blk * blk if fetch else terms * blk,
@@ -181,7 +200,7 @@
         ),
         compiler_params=pltpu.CompilerParams(vmem_limit_bytes=VMEM_LIMIT),
         name="contract",
-    )(*arrays)
+    )(*(pltpu.with_memory_space_constraint(x, space) for x in arrays))
 
 
 def merge_kernel(plan, kept, got, *outs):
@@ -325,16 +344,16 @@
     late_plan = Plan(mesh, first, left.shape[0], (True, True))
     places = range(plan.places)
 
-    kept, given, lhs, rhs = contract(plan, True, source, target, left, right, first)
+    kept, given, notes, *operands = contract(plan, True, source, target, left, right, first, second)
     merged = merge(plan, kept, plan.to_core(given))
     early = trade(plan, merged)
-    pieces = contract(late_plan, False, after(source, merged[-1]), target, lhs, rhs, second)
+    pieces = contract(late_plan, False, after(notes, merged[-1]), *operands)
     early = after(early, pieces)
     late = trade(late_plan, pieces)
 
     away, kept = spread(plan, early, [(m, h) for m in places for h in range(2)], 3000000)
     arrived = plan.halve(0, away)
-    late = late[:1] + after(late[1:], away)
+    late = late[:1] + [after(x, away) for x in late[1:]]
     parts = [(h * plan.places + m, h) for h in range(2) for m in places]
     late_away, late_kept = spread(late_plan, late + [late_plan.to_core(x) for x in late], parts, 100000000)
     arrived = after(arrived, late_away)

time: 56.3 us -> 55.3 us (0.982)
  Pallas kernels: 12.3 us -> 11.7 us
  transfers between devices with their start and end apart: 29 -> 29, of which waited for: 14 -> 15; matrix products, arithmetic and copies ran while one was open for 0% -> 0% of each run, Pallas kernels for 10% -> 9%
where the time goes in v9:
time: 55.3 us; the launch traced here: 55.1 us
  starting transfers between devices  25.8 us (47%)
  waiting for transfers between devices  16.6 us (30%)
  Pallas kernels  11.7 us (21%)
  between operations  0.75 us (1%)
    ppermute x12, starting transfers between devices, across(): lax.ppermute(x, AXES, self.partners(mask >> self.extra << 1, sec_masks))  15.3 us
    ppermute x4, starting transfers between devices, halve(): lax.ppermute(x, AXES, self.partners(0, [1 << bits[k] for bits in self.bit...  8.82 us
    pallas_call x2, Pallas kernels, contract(): pl.pallas_call(functools.partial(contract_kernel, plan, fetch), in_specs=...  8.76 us
    ppermute x12, waiting for transfers between devices, across(): lax.ppermute(x, AXES, self.partners(mask >> self.extra << 1, sec_masks))  8.62 us
    ppermute x4, waiting for transfers between devices, halve(): lax.ppermute(x, AXES, self.partners(0, [1 << bits[k] for bits in self.bit...  4.19 us
    ppermute x13, waiting for transfers between devices, to_core(): return lax.ppermute(x, AXES, self.partners(1, (0, 0)))  3.81 us
    pallas_call x2, Pallas kernels, spread(): pl.pallas_call(functools.partial(spread_kernel, plan, parts), in_specs=[w...  1.82 us
    ppermute x13, starting transfers between devices, to_core(): return lax.ppermute(x, AXES, self.partners(1, (0, 0)))  1.72 us
  transfers between devices with their start and end apart: 29, of which 15 were waited for; matrix products, arithmetic and copies ran while one was open for 0% of the time, Pallas kernels for 9%

profile of v9, /device:TPU:0, one launch (start us, length us, event | category | flops | bytes accessed | tf_op | source)
XLA Modules:
  0.0 55.1 jit_solution(14858170828919001229)
XLA Ops:
  0.6 5.6 %contract.2 = (bf16[4,144,256]{2,1,0:T(8,128)(2,1)S(1)}, bf16[4,144,256]{2,1,0:T(8,128)(2,1)S(1)}, s32[8,128]{1,0:T(8,128)S(1)}, bf16[32,256,256]{2,1,0:T(8,128)...) custom-call(s32[32]{0:T(128)} %refs_0_.1, s32[32]{0:T(128)} %refs_1_.1, ...), custom_call_target="tpu_custom_call" | custom-call | flops 2147483648 | bytes 8388608 | tf_op jit(solution)/shard_map/contract/pallas_call | solution.py:190
  6.7 1.2 %collective-permute-done.got = bf16[4,144,256]{2,1,0:T(8,128)(2,1)S(1)} collective-permute-done((bf16[4,144,256]{2,1,0:T(8,128)(2,1)S(1)}, bf16[4,144,256]{2,1,0:T(8,128)(2,1)S(1)}, u32[]{:S(2)}, u32[]{:S(2)}) %collective-permute-start) | collective-permute-done | bytes 294944 | tf_op jit(solution)/shard_map/ppermute | solution.py:58
  8.0 3.9 %collective-permute-start.3 = (bf16[272,256]{1,0:T(8,128)(2,1)S(1)}, bf16[272,256]{1,0:T(8,128)(2,1)S(1)}, u32[]{:S(2)}, u32[]{:S(2)}) collective-permute-start(bf16[272,256]{1,0:T(8,128)(2,1)S(1)} %get-tuple-element.35), channel_id=1, source_target_pairs={{0,17},{1,16},{2,19},{3,18},{4,21},{5,20},{6,23},{7,22},{8,26},{9,... | collective-permute-start | bytes 417800 | tf_op jit(solution)/shard_map/ppermute | solution.py:64
  12.5 3.2 %contract.3 = (bf16[272,256]{1,0:T(8,128)(2,1)S(1)}, bf16[272,256]{1,0:T(8,128)(2,1)S(1)}, bf16[272,256]{1,0:T(8,128)(2,1)S(1)}, bf16[272,256]{1,0:T(8,128)(2,1)S(1)}) custom-call(s32[8,128]{1,0:T(8,128)S(1)} %get-tuple-element.37.refs_0_, bf16[32,256,256]{2,1,0:T(8,128)(2,1)S(1)} %get-tuple-element.38.refs_1_, ...), custom_call_target="tpu_custom_call" | custom-call | flops 2147483648 | bytes 8192 | tf_op jit(solution)/shard_map/contract/pallas_call | solution.py:190
  15.7 3.0 %collective-permute-start.7 = (bf16[272,256]{1,0:T(8,128)(2,1)S(1)}, bf16[272,256]{1,0:T(8,128)(2,1)S(1)}, u32[]{:S(2)}, u32[]{:S(2)}) collective-permute-start(bf16[272,256]{1,0:T(8,128)(2,1)S(1)} %get-tuple-element.44), channel_id=1, source_target_pairs={{0,18},{1,19},{2,16},{3,17},{4,22},{5,23},{6,20},{7,21},{8,26},{9,... | collective-permute-start | bytes 417800 | tf_op jit(solution)/shard_map/ppermute | solution.py:64
  19.3 0.9 %spread.2 = (bf16[512,256]{1,0:T(8,128)(2,1)S(1)}, bf16[512,256]{1,0:T(8,128)(2,1)S(1)}) custom-call(bf16[272,256]{1,0:T(8,128)(2,1)S(1)} %get-tuple-element.45.refs_0_, bf16[272,256]{1,0:T(8,128)(2,1)S(1)} %collective-permute-done.1.refs_1_, bf16[272,256]{1,0:T(8,128)(2,1)S(1)} %collective-permute-done.2.refs_2_, ...), custom_call_target="tpu_custom_call" | custom-call | flops 1 | bytes 3000000 | tf_op jit(solution)/shard_map/spread/pallas_call | solution.py:263
  20.3 2.0 %collective-permute-start.4 = (bf16[512,256]{1,0:T(8,128)(2,1)S(1)}, bf16[512,256]{1,0:T(8,128)(2,1)S(1)}, u32[]{:S(2)}, u32[]{:S(2)}) collective-permute-start(bf16[512,256]{1,0:T(8,128)(2,1)S(1)} %get-tuple-element.50), channel_id=1, source_target_pairs={{0,2},{1,3},{2,0},{3,1},{4,6},{5,7},{6,4},{7,5},{8,9},{9,8},{10,11... | collective-permute-start | bytes 786440 | tf_op jit(solution)/shard_map/ppermute | solution.py:67
  22.6 2.3 %collective-permute-done.6.refs_2_ = bf16[272,256]{1,0:T(8,128)(2,1)S(1)} collective-permute-done((bf16[272,256]{1,0:T(8,128)(2,1)S(1)}, bf16[272,256]{1,0:T(8,128)(2,1)S(1)}, u32[]{:S(2)}, u32[]{:S(2)}) %collective-permute-start.6) | collective-permute-done | bytes 139296 | tf_op jit(solution)/shard_map/ppermute | solution.py:64
  25.5 0.8 %collective-permute-done.9.refs_5_ = bf16[272,256]{1,0:T(8,128)(2,1)S(1)} collective-permute-done((bf16[272,256]{1,0:T(8,128)(2,1)S(1)}, bf16[272,256]{1,0:T(8,128)(2,1)S(1)}, u32[]{:S(2)}, u32[]{:S(2)}) %collective-permute-start.9) | collective-permute-done | bytes 139296 | tf_op jit(solution)/shard_map/ppermute | solution.py:58
  26.9 0.9 %spread.3 = (bf16[512,256]{1,0:T(8,128)(2,1)S(1)}, bf16[512,256]{1,0:T(8,128)(2,1)S(1)}) custom-call(bf16[272,256]{1,0:T(8,128)(2,1)S(1)} %get-tuple-element.41.refs_0_, bf16[272,256]{1,0:T(8,128)(2,1)S(1)} %collective-permute-done.5.refs_1_, bf16[272,256]{1,0:T(8,128)(2,1)S(1)} %collective-permute-done.6.refs_2_, ...), custom_call_target="tpu_custom_call" | custom-call | flops 1 | bytes 100000000 | tf_op jit(solution)/shard_map/spread/pallas_call | solution.py:263
  27.8 1.6 %collective-permute-start.13 = (bf16[512,256]{1,0:T(8,128)(2,1)S(1)}, bf16[512,256]{1,0:T(8,128)(2,1)S(1)}, u32[]{:S(2)}, u32[]{:S(2)}) collective-permute-start(bf16[512,256]{1,0:T(8,128)(2,1)S(1)} %get-tuple-element.54), channel_id=1, source_target_pairs={{0,1},{1,0},{2,3},{3,2},{4,5},{5,4},{6,7},{7,6},{8,9},{9,8},{10,11... | collective-permute-start | bytes 786440 | tf_op jit(solution)/shard_map/ppermute | solution.py:67
  29.5 2.7 %collective-permute-start.12 = (bf16[256,256]{1,0:T(8,128)(2,1)S(1)}, bf16[256,256]{1,0:T(8,128)(2,1)S(1)}, u32[]{:S(2)}, u32[]{:S(2)}) collective-permute-start(bf16[256,256]{1,0:T(8,128)(2,1)S(1)} %slice.55), channel_id=1, source_target_pairs={{0,4},{1,5},{2,6},{3,7},{4,0},{5,1},{6,2},{7,3},{8,12},{9,13},{10,... | collective-permute-start | bytes 393224 | tf_op jit(solution)/shard_map/ppermute | solution.py:67
  32.1 4.2 %collective-permute-done.13 = bf16[512,256]{1,0:T(8,128)(2,1)S(1)} collective-permute-done((bf16[512,256]{1,0:T(8,128)(2,1)S(1)}, bf16[512,256]{1,0:T(8,128)(2,1)S(1)}, u32[]{:S(2)}, u32[]{:S(2)}) %collective-permute-start.13) | collective-permute-done | bytes 262176 | tf_op jit(solution)/shard_map/ppermute | solution.py:67
  36.4 2.7 %collective-permute-start.21 = (bf16[256,256]{1,0:T(8,128)(2,1)S(1)}, bf16[256,256]{1,0:T(8,128)(2,1)S(1)}, u32[]{:S(2)}, u32[]{:S(2)}) collective-permute-start(bf16[256,256]{1,0:T(8,128)(2,1)S(1)} %slice.54), channel_id=1, source_target_pairs={{0,4},{1,5},{2,6},{3,7},{4,0},{5,1},{6,2},{7,3},{8,12},{9,13},{10,... | collective-permute-start | bytes 393224 | tf_op jit(solution)/shard_map/ppermute | solution.py:67
  39.1 2.5 %collective-permute-start.16 = (bf16[128,256]{1,0:T(8,128)(2,1)S(1)}, bf16[128,256]{1,0:T(8,128)(2,1)S(1)}, u32[]{:S(2)}, u32[]{:S(2)}) collective-permute-start(bf16[128,256]{1,0:T(8,128)(2,1)S(1)} %get-tuple-element.60), channel_id=1, source_target_pairs={{0,17},{1,16},{2,19},{3,18},{4,21},{5,20},{6,23},{7,22},{8,26},{9,... | collective-permute-start | bytes 196616 | tf_op jit(solution)/shard_map/ppermute | solution.py:64
  42.1 0.5 collective-permute-start.15
  42.7 1.7 %collective-permute-done.16 = bf16[128,256]{1,0:T(8,128)(2,1)S(1)} collective-permute-done((bf16[128,256]{1,0:T(8,128)(2,1)S(1)}, bf16[128,256]{1,0:T(8,128)(2,1)S(1)}, u32[]{:S(2)}, u32[]{:S(2)}) %collective-permute-start.16) | collective-permute-done | bytes 65568 | tf_op jit(solution)/shard_map/ppermute | solution.py:64
  44.3 1.5 %collective-permute-done.14 = bf16[128,256]{1,0:T(8,128)(2,1)S(1)} collective-permute-done((bf16[128,256]{1,0:T(8,128)(2,1)S(1)}, bf16[128,256]{1,0:T(8,128)(2,1)S(1)}, u32[]{:S(2)}, u32[]{:S(2)}) %collective-permute-start.14) | collective-permute-done | bytes 65568 | tf_op jit(solution)/shard_map/ppermute | solution.py:64
  45.9 1.6 %collective-permute-start.24 = (bf16[128,256]{1,0:T(8,128)(2,1)S(1)}, bf16[128,256]{1,0:T(8,128)(2,1)S(1)}, u32[]{:S(2)}, u32[]{:S(2)}) collective-permute-start(bf16[128,256]{1,0:T(8,128)(2,1)S(1)} %get-tuple-element.58), channel_id=1, source_target_pairs={{0,18},{1,19},{2,16},{3,17},{4,22},{5,23},{6,20},{7,21},{8,26},{9,... | collective-permute-start | bytes 196616 | tf_op jit(solution)/shard_map/ppermute | solution.py:64
  48.0 1.5 %collective-permute-start.23 = (bf16[128,256]{1,0:T(8,128)(2,1)S(1)}, bf16[128,256]{1,0:T(8,128)(2,1)S(1)}, u32[]{:S(2)}, u32[]{:S(2)}) collective-permute-start(bf16[128,256]{1,0:T(8,128)(2,1)S(1)} %get-tuple-element.59), channel_id=1, source_target_pairs={{0,16},{1,17},{2,18},{3,19},{4,20},{5,21},{6,22},{7,23},{8,24},{9,... | collective-permute-start | bytes 196616 | tf_op jit(solution)/shard_map/ppermute | solution.py:64
  50.0 1.5 %collective-permute-done.24 = bf16[128,256]{1,0:T(8,128)(2,1)S(1)} collective-permute-done((bf16[128,256]{1,0:T(8,128)(2,1)S(1)}, bf16[128,256]{1,0:T(8,128)(2,1)S(1)}, u32[]{:S(2)}, u32[]{:S(2)}) %collective-permute-start.24) | collective-permute-done | bytes 65568 | tf_op jit(solution)/shard_map/ppermute | solution.py:64
  52.0 0.8 %collective-permute-done.23 = bf16[128,256]{1,0:T(8,128)(2,1)S(1)} collective-permute-done((bf16[128,256]{1,0:T(8,128)(2,1)S(1)}, bf16[128,256]{1,0:T(8,128)(2,1)S(1)}, u32[]{:S(2)}, u32[]{:S(2)}) %collective-permute-start.23) | collective-permute-done | bytes 65568 | tf_op jit(solution)/shard_map/ppermute | solution.py:64
  53.1 0.9 %collective-permute-done.27 = bf16[128,256]{1,0:T(8,128)(2,1)S(1)} collective-permute-done((bf16[128,256]{1,0:T(8,128)(2,1)S(1)}, bf16[128,256]{1,0:T(8,128)(2,1)S(1)}, u32[]{:S(2)}, u32[]{:S(2)}) %collective-permute-start.27) | collective-permute-done | bytes 65568 | tf_op jit(solution)/shard_map/ppermute | solution.py:58
  54.0 1.1 %assemble.1 = (bf16[4,256,256]{2,1,0:T(8,128)(2,1)}, bf16[4,256,256]{2,1,0:T(8,128)(2,1)}) custom-call(bf16[4,32,256]{2,1,0:T(8,128)(2,1)S(1)} %bitcast.16, bf16[4,32,256]{2,1,0:T(8,128)(2,1)S(1)} %bitcast.19, bf16[4,32,256]{2,1,0:T(8,128)(2,1)S(1)} %bitcast.21, bf16[4,32,256]{2,1,0:T(8,128)(2,1)S(1)} %bitcast.18, bf16[4,32,256]{2,1,0:T(8,128)(2,1)S(1)} %bitcast.20, ...), custom_call_target="tpu_custom_call" | custom-call | tf_op jit(solution)/shard_map/assemble/pallas_call | solution.py:304
  (48 shorter events, 6.0 us)
Async XLA Ops:
  6.2 1.7 %collective-permute-start = (bf16[4,144,256]{2,1,0:T(8,128)(2,1)S(1)}, bf16[4,144,256]{2,1,0:T(8,128)(2,1)S(1)}, u32[]{:S(2)}, u32[]{:S(2)}) collective-permute-start(bf16[4,144,256]{2,1,0:T(8,128)(2,1)S(1)} %get-tuple-element.31), channel_id=1, source_target_pairs={{0,8},{1,9},{2,10},{3,11},{4,12},{5,13},{6,14},{7,15},{8,0},{9,1},... | collective-permute-start | bytes 884744 | tf_op jit(solution)/shard_map/ppermute | solution.py:58
  8.0 11.4 %collective-permute-start.3 = (bf16[272,256]{1,0:T(8,128)(2,1)S(1)}, bf16[272,256]{1,0:T(8,128)(2,1)S(1)}, u32[]{:S(2)}, u32[]{:S(2)}) collective-permute-start(bf16[272,256]{1,0:T(8,128)(2,1)S(1)} %get-tuple-element.35), channel_id=1, source_target_pairs={{0,17},{1,16},{2,19},{3,18},{4,21},{5,20},{6,23},{7,22},{8,26},{9,... | collective-permute-start | bytes 417800 | tf_op jit(solution)/shard_map/ppermute | solution.py:64
  11.8 7.4 %collective-permute-start.1 = (bf16[272,256]{1,0:T(8,128)(2,1)S(1)}, bf16[272,256]{1,0:T(8,128)(2,1)S(1)}, u32[]{:S(2)}, u32[]{:S(2)}) collective-permute-start(bf16[272,256]{1,0:T(8,128)(2,1)S(1)} %get-tuple-element.33), channel_id=1, source_target_pairs={{0,1},{1,0},{2,3},{3,2},{4,5},{5,4},{6,7},{7,6},{8,10},{9,11},{10,... | collective-permute-start | bytes 417800 | tf_op jit(solution)/shard_map/ppermute | solution.py:64
  12.4 7.0 %collective-permute-start.2 = (bf16[272,256]{1,0:T(8,128)(2,1)S(1)}, bf16[272,256]{1,0:T(8,128)(2,1)S(1)}, u32[]{:S(2)}, u32[]{:S(2)}) collective-permute-start(bf16[272,256]{1,0:T(8,128)(2,1)S(1)} %get-tuple-element.34), channel_id=1, source_target_pairs={{0,16},{1,17},{2,18},{3,19},{4,20},{5,21},{6,22},{7,23},{8,24},{9,... | collective-permute-start | bytes 417800 | tf_op jit(solution)/shard_map/ppermute | solution.py:64
  15.7 6.9 %collective-permute-start.7 = (bf16[272,256]{1,0:T(8,128)(2,1)S(1)}, bf16[272,256]{1,0:T(8,128)(2,1)S(1)}, u32[]{:S(2)}, u32[]{:S(2)}) collective-permute-start(bf16[272,256]{1,0:T(8,128)(2,1)S(1)} %get-tuple-element.44), channel_id=1, source_target_pairs={{0,18},{1,19},{2,16},{3,17},{4,22},{5,23},{6,20},{7,21},{8,26},{9,... | collective-permute-start | bytes 417800 | tf_op jit(solution)/shard_map/ppermute | solution.py:64
  18.7 6.2 %collective-permute-start.6 = (bf16[272,256]{1,0:T(8,128)(2,1)S(1)}, bf16[272,256]{1,0:T(8,128)(2,1)S(1)}, u32[]{:S(2)}, u32[]{:S(2)}) collective-permute-start(bf16[272,256]{1,0:T(8,128)(2,1)S(1)} %get-tuple-element.43), channel_id=1, source_target_pairs={{0,16},{1,17},{2,18},{3,19},{4,20},{5,21},{6,22},{7,23},{8,24},{9,... | collective-permute-start | bytes 417800 | tf_op jit(solution)/shard_map/ppermute | solution.py:64
  19.2 5.8 %collective-permute-start.5 = (bf16[272,256]{1,0:T(8,128)(2,1)S(1)}, bf16[272,256]{1,0:T(8,128)(2,1)S(1)}, u32[]{:S(2)}, u32[]{:S(2)}) collective-permute-start(bf16[272,256]{1,0:T(8,128)(2,1)S(1)} %get-tuple-element.42), channel_id=1, source_target_pairs={{0,2},{1,3},{2,0},{3,1},{4,6},{5,7},{6,4},{7,5},{8,10},{9,11},{10,... | collective-permute-start | bytes 417800 | tf_op jit(solution)/shard_map/ppermute | solution.py:64
  20.3 9.1 %collective-permute-start.4 = (bf16[512,256]{1,0:T(8,128)(2,1)S(1)}, bf16[512,256]{1,0:T(8,128)(2,1)S(1)}, u32[]{:S(2)}, u32[]{:S(2)}) collective-permute-start(bf16[512,256]{1,0:T(8,128)(2,1)S(1)} %get-tuple-element.50), channel_id=1, source_target_pairs={{0,2},{1,3},{2,0},{3,1},{4,6},{5,7},{6,4},{7,5},{8,9},{9,8},{10,11... | collective-permute-start | bytes 786440 | tf_op jit(solution)/shard_map/ppermute | solution.py:67
  22.2 3.3 %collective-permute-start.8 = (bf16[272,256]{1,0:T(8,128)(2,1)S(1)}, bf16[272,256]{1,0:T(8,128)(2,1)S(1)}, u32[]{:S(2)}, u32[]{:S(2)}) collective-permute-start(bf16[272,256]{1,0:T(8,128)(2,1)S(1)} %get-tuple-element.41.refs_0_), channel_id=1, source_target_pairs={{0,8},{1,9},{2,10},{3,11},{4,12},{5,13},{6,14},{7,15},{8,0},{9,1},... | collective-permute-start | bytes 417800 | tf_op jit(solution)/shard_map/ppermute | solution.py:58
  25.0 1.6 %collective-permute-start.10 = (bf16[272,256]{1,0:T(8,128)(2,1)S(1)}, bf16[272,256]{1,0:T(8,128)(2,1)S(1)}, u32[]{:S(2)}, u32[]{:S(2)}) collective-permute-start(bf16[272,256]{1,0:T(8,128)(2,1)S(1)} %collective-permute-done.6.refs_2_), channel_id=1, source_target_pairs={{0,8},{1,9},{2,10},{3,11},{4,12},{5,13},{6,14},{7,15},{8,0},{9,1},... | collective-permute-start | bytes 417800 | tf_op jit(solution)/shard_map/ppermute | solution.py:58
  27.8 8.5 %collective-permute-start.13 = (bf16[512,256]{1,0:T(8,128)(2,1)S(1)}, bf16[512,256]{1,0:T(8,128)(2,1)S(1)}, u32[]{:S(2)}, u32[]{:S(2)}) collective-permute-start(bf16[512,256]{1,0:T(8,128)(2,1)S(1)} %get-tuple-element.54), channel_id=1, source_target_pairs={{0,1},{1,0},{2,3},{3,2},{4,5},{5,4},{6,7},{7,6},{8,9},{9,8},{10,11... | collective-permute-start | bytes 786440 | tf_op jit(solution)/shard_map/ppermute | solution.py:67
  29.5 9.6 %collective-permute-start.12 = (bf16[256,256]{1,0:T(8,128)(2,1)S(1)}, bf16[256,256]{1,0:T(8,128)(2,1)S(1)}, u32[]{:S(2)}, u32[]{:S(2)}) collective-permute-start(bf16[256,256]{1,0:T(8,128)(2,1)S(1)} %slice.55), channel_id=1, source_target_pairs={{0,4},{1,5},{2,6},{3,7},{4,0},{5,1},{6,2},{7,3},{8,12},{9,13},{10,... | collective-permute-start | bytes 393224 | tf_op jit(solution)/shard_map/ppermute | solution.py:67
  36.4 9.5 %collective-permute-start.21 = (bf16[256,256]{1,0:T(8,128)(2,1)S(1)}, bf16[256,256]{1,0:T(8,128)(2,1)S(1)}, u32[]{:S(2)}, u32[]{:S(2)}) collective-permute-start(bf16[256,256]{1,0:T(8,128)(2,1)S(1)} %slice.54), channel_id=1, source_target_pairs={{0,4},{1,5},{2,6},{3,7},{4,0},{5,1},{6,2},{7,3},{8,12},{9,13},{10,... | collective-permute-start | bytes 393224 | tf_op jit(solution)/shard_map/ppermute | solution.py:67
  39.1 5.2 %collective-permute-start.16 = (bf16[128,256]{1,0:T(8,128)(2,1)S(1)}, bf16[128,256]{1,0:T(8,128)(2,1)S(1)}, u32[]{:S(2)}, u32[]{:S(2)}) collective-permute-start(bf16[128,256]{1,0:T(8,128)(2,1)S(1)} %get-tuple-element.60), channel_id=1, source_target_pairs={{0,17},{1,16},{2,19},{3,18},{4,21},{5,20},{6,23},{7,22},{8,26},{9,... | collective-permute-start | bytes 196616 | tf_op jit(solution)/shard_map/ppermute | solution.py:64
  41.6 4.3 %collective-permute-start.14 = (bf16[128,256]{1,0:T(8,128)(2,1)S(1)}, bf16[128,256]{1,0:T(8,128)(2,1)S(1)}, u32[]{:S(2)}, u32[]{:S(2)}) collective-permute-start(bf16[128,256]{1,0:T(8,128)(2,1)S(1)} %get-tuple-element.60), channel_id=1, source_target_pairs={{0,1},{1,0},{2,3},{3,2},{4,5},{5,4},{6,7},{7,6},{8,10},{9,11},{10,... | collective-permute-start | bytes 196616 | tf_op jit(solution)/shard_map/ppermute | solution.py:64
  42.1 5.4 %collective-permute-start.17 = (bf16[128,256]{1,0:T(8,128)(2,1)S(1)}, bf16[128,256]{1,0:T(8,128)(2,1)S(1)}, u32[]{:S(2)}, u32[]{:S(2)}) collective-permute-start(bf16[128,256]{1,0:T(8,128)(2,1)S(1)} %get-tuple-element.61), channel_id=1, source_target_pairs={{0,8},{1,9},{2,10},{3,11},{4,12},{5,13},{6,14},{7,15},{8,0},{9,1},... | collective-permute-start | bytes 196616 | tf_op jit(solution)/shard_map/ppermute | solution.py:58
  42.1 5.9 %collective-permute-start.15 = (bf16[128,256]{1,0:T(8,128)(2,1)S(1)}, bf16[128,256]{1,0:T(8,128)(2,1)S(1)}, u32[]{:S(2)}, u32[]{:S(2)}) collective-permute-start(bf16[128,256]{1,0:T(8,128)(2,1)S(1)} %get-tuple-element.61), channel_id=1, source_target_pairs={{0,16},{1,17},{2,18},{3,19},{4,20},{5,21},{6,22},{7,23},{8,24},{9,... | collective-permute-start | bytes 196616 | tf_op jit(solution)/shard_map/ppermute | solution.py:64
  44.3 5.1 %collective-permute-start.20 = (bf16[128,256]{1,0:T(8,128)(2,1)S(1)}, bf16[128,256]{1,0:T(8,128)(2,1)S(1)}, u32[]{:S(2)}, u32[]{:S(2)}) collective-permute-start(bf16[128,256]{1,0:T(8,128)(2,1)S(1)} %collective-permute-done.16), channel_id=1, source_target_pairs={{0,8},{1,9},{2,10},{3,11},{4,12},{5,13},{6,14},{7,15},{8,0},{9,1},... | collective-permute-start | bytes 196616 | tf_op jit(solution)/shard_map/ppermute | solution.py:58
  45.8 3.6 %collective-permute-start.18 = (bf16[128,256]{1,0:T(8,128)(2,1)S(1)}, bf16[128,256]{1,0:T(8,128)(2,1)S(1)}, u32[]{:S(2)}, u32[]{:S(2)}) collective-permute-start(bf16[128,256]{1,0:T(8,128)(2,1)S(1)} %collective-permute-done.14), channel_id=1, source_target_pairs={{0,8},{1,9},{2,10},{3,11},{4,12},{5,13},{6,14},{7,15},{8,0},{9,1},... | collective-permute-start | bytes 196616 | tf_op jit(solution)/shard_map/ppermute | solution.py:58
  45.9 5.6 %collective-permute-start.24 = (bf16[128,256]{1,0:T(8,128)(2,1)S(1)}, bf16[128,256]{1,0:T(8,128)(2,1)S(1)}, u32[]{:S(2)}, u32[]{:S(2)}) collective-permute-start(bf16[128,256]{1,0:T(8,128)(2,1)S(1)} %get-tuple-element.58), channel_id=1, source_target_pairs={{0,18},{1,19},{2,16},{3,17},{4,22},{5,23},{6,20},{7,21},{8,26},{9,... | collective-permute-start | bytes 196616 | tf_op jit(solution)/shard_map/ppermute | solution.py:64
  47.5 4.3 %collective-permute-start.22 = (bf16[128,256]{1,0:T(8,128)(2,1)S(1)}, bf16[128,256]{1,0:T(8,128)(2,1)S(1)}, u32[]{:S(2)}, u32[]{:S(2)}) collective-permute-start(bf16[128,256]{1,0:T(8,128)(2,1)S(1)} %get-tuple-element.58), channel_id=1, source_target_pairs={{0,2},{1,3},{2,0},{3,1},{4,6},{5,7},{6,4},{7,5},{8,10},{9,11},{10,... | collective-permute-start | bytes 196616 | tf_op jit(solution)/shard_map/ppermute | solution.py:64
  48.0 4.8 %collective-permute-start.23 = (bf16[128,256]{1,0:T(8,128)(2,1)S(1)}, bf16[128,256]{1,0:T(8,128)(2,1)S(1)}, u32[]{:S(2)}, u32[]{:S(2)}) collective-permute-start(bf16[128,256]{1,0:T(8,128)(2,1)S(1)} %get-tuple-element.59), channel_id=1, source_target_pairs={{0,16},{1,17},{2,18},{3,19},{4,20},{5,21},{6,22},{7,23},{8,24},{9,... | collective-permute-start | bytes 196616 | tf_op jit(solution)/shard_map/ppermute | solution.py:64
  49.5 3.3 %collective-permute-start.19 = (bf16[128,256]{1,0:T(8,128)(2,1)S(1)}, bf16[128,256]{1,0:T(8,128)(2,1)S(1)}, u32[]{:S(2)}, u32[]{:S(2)}) collective-permute-start(bf16[128,256]{1,0:T(8,128)(2,1)S(1)} %collective-permute-done.15), channel_id=1, source_target_pairs={{0,8},{1,9},{2,10},{3,11},{4,12},{5,13},{6,14},{7,15},{8,0},{9,1},... | collective-permute-start | bytes 196616 | tf_op jit(solution)/shard_map/ppermute | solution.py:58
  49.5 3.3 %collective-permute-start.25 = (bf16[128,256]{1,0:T(8,128)(2,1)S(1)}, bf16[128,256]{1,0:T(8,128)(2,1)S(1)}, u32[]{:S(2)}, u32[]{:S(2)}) collective-permute-start(bf16[128,256]{1,0:T(8,128)(2,1)S(1)} %get-tuple-element.59), channel_id=1, source_target_pairs={{0,8},{1,9},{2,10},{3,11},{4,12},{5,13},{6,14},{7,15},{8,0},{9,1},... | collective-permute-start | bytes 196616 | tf_op jit(solution)/shard_map/ppermute | solution.py:58
  (5 other events, 6.5 us)
